TPU v7x, 512 devices: a whole 4x8x8 slice. The times are simulated.
512 devices in a mesh: gz: 64 (over z, x, y_lo), gy: 8 (over y_hi, core).
Axes of the slice: x: 4, y: 8 (y_hi: 4, y_lo: 2; y = y_hi * 2 + y_lo), z: 8, core: 2. Of those that a mesh axis runs over, the one named last changes fastest.
Arguments:
- observed: float32 [512, 128, 1024], P('gz', 'gy'), may hold values from 0.2 to 5
- estimate: float32 [512, 128, 1024], P('gz', 'gy'), may hold values from 0.5 to 2
- psf_y: float32 [31], replicated, may hold values from 0.05 to 1
- psf_x: float32 [31], replicated, may hold values from 0.05 to 1
- psf_z: float32 [63], replicated, may hold values from 0.05 to 1
Outputs:
- restored: float32 [512, 128, 1024], P('gz', 'gy')
All inputs are finite; a program needn't handle non-finite values.
Results may differ from a plain program's by a relative error of at most 0.0001.
Values sent between devices are 32-bit elements; how exact they have to be, the bound alone decides.
No kernel may reach another device: no remote copies, remote signals or barrier semaphores. Data moves between devices by JAX's collectives and lax.ppermute only.
A program may use at most 64 MiB of HBM per device.

v0:
```python
import jax
import jax.numpy as jnp
from jax import lax
from jax.sharding import PartitionSpec as P

ITERS = 2


def extended(array, sides, width):
    for axis, dim in sides:
        peers, length = (lax.axis_size(axis), array.shape[dim])
        up = [(i, (i + 1) % peers) for i in range(peers - 1)]
        down = [(j, i) for i, j in up]
        last = lax.slice_in_dim(array, length - width, length, axis=dim)
        leading = lax.slice_in_dim(array, 0, width, axis=dim)
        before = lax.ppermute(last, axis, up)
        after = lax.ppermute(leading, axis, down)
        array = jnp.concatenate([before, array, after], axis=dim)
    return array


def banded(weights, n_in, n_out, shift_by):
    length = weights.shape[0]
    span = n_in + n_out - 1
    lead = n_out - 1 + shift_by
    zero_value = jnp.zeros((), weights.dtype)
    diagonals = lax.pad(weights, zero_value, [(lead, span - lead - length, 0)])
    tiled = jnp.tile(diagonals, n_out + 1)[: n_out * (span + 1)]
    hankel = tiled.reshape(n_out, span + 1)[:, :n_in]
    return hankel[::-1].T


def blur_rows(volume, matrix_x):
    reach = (matrix_x.shape[0] - matrix_x.shape[1]) // 2
    block = matrix_x.shape[1]
    width = volume.shape[2]
    count = width // block
    padded = jnp.pad(volume, ((0, 0), (0, 0), (reach, reach)))
    windows = jnp.stack(
        [padded[:, :, b * block : b * block + block + 2 * reach] for b in range(count)], axis=2
    )
    blurred = jnp.einsum("zybq,qi->zybi", windows, matrix_x, precision=lax.Precision.HIGHEST)
    return blurred.reshape(volume.shape)


def in_plane(volume, matrix_y, matrix_x):
    reach = (matrix_y.shape[0] - matrix_y.shape[1]) // 2
    padded = extended(volume, (("gy", 1),), reach)
    blurred = jnp.einsum("zqx,qi->zix", padded, matrix_y, precision=lax.Precision.HIGHEST)
    return blur_rows(blurred, matrix_x)


def to_columns(volume):
    planes = volume.shape[0]
    return lax.all_to_all(volume.reshape(planes, -1), "gz", split_axis=1, concat_axis=0, tiled=True)


def to_slabs(columns, slab_shape):
    returned = lax.all_to_all(columns, "gz", split_axis=0, concat_axis=1, tiled=True)
    return returned.reshape(slab_shape)


def axial(columns, matrix_z):
    return jnp.dot(matrix_z.T, columns, precision=lax.Precision.HIGHEST)


def per_device(observed, estimate, psf_y, psf_x, psf_z):
    wy = psf_y / jnp.sum(psf_y)
    wx = psf_x / jnp.sum(psf_x)
    wz = psf_z / jnp.sum(psf_z)
    slab_shape = estimate.shape
    planes, strip, width = slab_shape
    depth = planes * lax.axis_size("gz")
    reach_y = wy.shape[0] // 2
    reach_x = wx.shape[0] // 2
    reach_z = wz.shape[0] // 2
    block = 128
    fwd_y = banded(wy, strip + 2 * reach_y, strip, 0)
    adj_y = banded(wy[::-1], strip + 2 * reach_y, strip, 0)
    fwd_x = banded(wx, block + 2 * reach_x, block, 0)
    adj_x = banded(wx[::-1], block + 2 * reach_x, block, 0)
    fwd_z = banded(wz, depth, depth, -reach_z)
    adj_z = banded(wz[::-1], depth, depth, -reach_z)
    for sweep in range(ITERS):
        blurred = to_slabs(axial(to_columns(in_plane(estimate, fwd_y, fwd_x)), fwd_z), slab_shape)
        ratio = observed / blurred
        returned = to_slabs(axial(to_columns(ratio), adj_z), slab_shape)
        estimate = estimate * in_plane(returned, adj_y, adj_x)
    return estimate


def solution(mesh):
    return jax.shard_map(
        per_device,
        mesh=mesh,
        in_specs=(P("gz", "gy", None), P("gz", "gy", None), P(), P(), P()),
        out_specs=P("gz", "gy", None),
        check_vma=False,
    )
```

profile of v0, /device:TPU:1, one launch (start us, length us, event | category | flops | bytes accessed | tf_op | source)
XLA Modules:
  0.0 301.8 jit_solution(14147265202483703443)
XLA Ops:
  1.4 8.8 %collective-permute-start.1 = (f32[8,15,1024]{2,1,0:T(8,128)S(1)}, f32[8,15,1024]{2,1,0:T(8,128)S(1)}, u32[]{:S(2)}, u32[]{:S(2)}) collective-permute-start(f32[8,15,1024]{2,1,0:T(8,128)S(1)} %get-tuple-element.12), channel_id=1, source_target_pairs={{1,0},{2,1},{3,2},{4,3},{5,4},{6,5},{7,6},{9,8},{10,9},{11,10},{12... | collective-permute-start | bytes 1474568 | tf_op jit(solution)/shard_map/ppermute | solution.py:17
  10.2 1.9 collective-permute-start
  16.0 3.5 %collective-permute-done.1 = f32[8,15,1024]{2,1,0:T(8,128)S(1)} collective-permute-done((f32[8,15,1024]{2,1,0:T(8,128)S(1)}, f32[8,15,1024]{2,1,0:T(8,128)S(1)}, u32[]{:S(2)}, u32[]{:S(2)}) %collective-permute-start.1) | collective-permute-done | bytes 491552 | tf_op jit(solution)/shard_map/ppermute | solution.py:17
  21.3 1.5 fusion.50
  24.1 15.6 %all-to-all-start = ((f32[8,64,256]{2,0,1:T(8,128)}), f32[8,64,256]{2,0,1:T(8,128)S(1)}, u32[]{:S(2)}, u32[]{:S(2)}) async-start(f32[8,64,256]{2,0,1:T(8,128)} %copy.32), calls=%async_computation | async-start | bytes 1048576 | tf_op jit(solution)/shard_map/all_to_all | solution.py:55
  41.5 2.7 tile.29
  44.2 1.6 slice-done
  49.0 3.5 %all-to-all-done = f32[8,64,256]{2,0,1:T(8,128)S(1)} async-done(((f32[8,64,256]{2,0,1:T(8,128)}), f32[8,64,256]{2,0,1:T(8,128)S(1)}, u32[]{:S(2)}, u32[]{:S(2)}) %all-to-all-start) | async-done | bytes 524320 | tf_op jit(solution)/shard_map/all_to_all | solution.py:55
  53.5 19.7 %all_to_all.128 = f32[64,8,256]{2,1,0:T(8,128)S(1)} all-to-all(f32[64,8,256]{2,1,0:T(8,128)S(1)} %fusion.38), channel_id=1, replica_groups=mesh['gz'=64,'gy'=8] {'gz'}, dimensions={0} | all-to-all | bytes 1048576 | tf_op jit(solution)/shard_map/all_to_all | solution.py:59
  74.9 5.7 %all-to-all-start.2 = ((f32[8,64,256]{2,0,1:T(8,128)}), f32[8,64,256]{2,0,1:T(8,128)}, u32[]{:S(2)}, u32[]{:S(2)}) async-start(f32[8,64,256]{2,0,1:T(8,128)} %copy.34), calls=%async_computation.2 | async-start | bytes 1048576 | tf_op jit(solution)/shard_map/all_to_all | solution.py:55
  81.0 2.7 tile.27
  83.7 1.6 slice-done.1
  85.3 1.5 reshape.81
  88.5 4.4 %all-to-all-done.2 = f32[8,64,256]{2,0,1:T(8,128)} async-done(((f32[8,64,256]{2,0,1:T(8,128)}), f32[8,64,256]{2,0,1:T(8,128)}, u32[]{:S(2)}, u32[]{:S(2)}) %all-to-all-start.2) | async-done | bytes 524320 | tf_op jit(solution)/shard_map/all_to_all | solution.py:55
  92.9 2.0 fusion.42
  95.0 18.8 %all_to_all.129 = f32[64,8,256]{2,1,0:T(8,128)S(1)} all-to-all(f32[64,8,256]{2,1,0:T(8,128)S(1)} %fusion.42), channel_id=1, replica_groups=mesh['gz'=64,'gy'=8] {'gz'}, dimensions={0} | all-to-all | bytes 1048576 | tf_op jit(solution)/shard_map/all_to_all | solution.py:59
  115.1 1.9 collective-permute-start.3
  117.0 23.6 %collective-permute-start.2 = (f32[8,15,1024]{2,1,0:T(8,128)}, f32[8,15,1024]{2,1,0:T(8,128)}, u32[]{:S(2)}, u32[]{:S(2)}) collective-permute-start(f32[8,15,1024]{2,1,0:T(8,128)} %get-tuple-element.9), channel_id=1, source_target_pairs={{0,1},{1,2},{2,3},{3,4},{4,5},{5,6},{6,7},{8,9},{9,10},{10,11},{11... | collective-permute-start | bytes 1474568 | tf_op jit(solution)/shard_map/ppermute | solution.py:16
  141.6 9.8 %collective-permute-done.3 = f32[8,15,1024]{2,1,0:T(8,128)} collective-permute-done((f32[8,15,1024]{2,1,0:T(8,128)}, f32[8,15,1024]{2,1,0:T(8,128)}, u32[]{:S(2)}, u32[]{:S(2)}) %collective-permute-start.3) | collective-permute-done | bytes 491552 | tf_op jit(solution)/shard_map/ppermute | solution.py:17
  151.4 2.2 fusion.30
  154.5 1.5 fusion.48
  158.0 1.9 collective-permute-start.5
  160.0 4.5 %collective-permute-start.4 = (f32[8,15,1024]{2,1,0:T(8,128)S(1)}, f32[8,15,1024]{2,1,0:T(8,128)S(1)}, u32[]{:S(2)}, u32[]{:S(2)}) collective-permute-start(f32[8,15,1024]{2,1,0:T(8,128)S(1)} %get-tuple-element.7), channel_id=1, source_target_pairs={{0,1},{1,2},{2,3},{3,4},{4,5},{5,6},{6,7},{8,9},{9,10},{10,11},{11... | collective-permute-start | bytes 1474568 | tf_op jit(solution)/shard_map/ppermute | solution.py:16
  164.5 10.0 %collective-permute-done.5 = f32[8,15,1024]{2,1,0:T(8,128)S(1)} collective-permute-done((f32[8,15,1024]{2,1,0:T(8,128)S(1)}, f32[8,15,1024]{2,1,0:T(8,128)S(1)}, u32[]{:S(2)}, u32[]{:S(2)}) %collective-permute-start.5) | collective-permute-done | bytes 491552 | tf_op jit(solution)/shard_map/ppermute | solution.py:17
  176.3 1.5 fusion.46
  180.1 20.5 %all_to_all.130 = f32[8,64,256]{2,0,1:T(8,128)S(1)} all-to-all(f32[8,64,256]{2,0,1:T(8,128)S(1)} %copy.40), channel_id=1, replica_groups=mesh['gz'=64,'gy'=8] {'gz'}, dimensions={1} | all-to-all | bytes 1048576 | tf_op jit(solution)/shard_map/all_to_all | solution.py:55
  201.6 18.1 %all_to_all.131 = f32[64,8,256]{2,1,0:T(8,128)S(1)} all-to-all(f32[64,8,256]{2,1,0:T(8,128)S(1)} %fusion.36), channel_id=1, replica_groups=mesh['gz'=64,'gy'=8] {'gz'}, dimensions={0} | all-to-all | bytes 1048576 | tf_op jit(solution)/shard_map/all_to_all | solution.py:59
  220.6 17.7 %all_to_all.132 = f32[8,64,256]{2,0,1:T(8,128)S(1)} all-to-all(f32[8,64,256]{2,0,1:T(8,128)S(1)} %copy.42), channel_id=1, replica_groups=mesh['gz'=64,'gy'=8] {'gz'}, dimensions={1} | all-to-all | bytes 1048576 | tf_op jit(solution)/shard_map/all_to_all | solution.py:55
  239.3 17.5 %all_to_all.133 = f32[64,8,256]{2,1,0:T(8,128)S(1)} all-to-all(f32[64,8,256]{2,1,0:T(8,128)S(1)} %fusion.40), channel_id=1, replica_groups=mesh['gz'=64,'gy'=8] {'gz'}, dimensions={0} | all-to-all | bytes 1048576 | tf_op jit(solution)/shard_map/all_to_all | solution.py:59
  257.2 1.9 collective-permute-start.7
  259.1 27.9 %collective-permute-start.6 = (f32[8,15,1024]{2,1,0:T(8,128)S(1)}, f32[8,15,1024]{2,1,0:T(8,128)S(1)}, u32[]{:S(2)}, u32[]{:S(2)}) collective-permute-start(f32[8,15,1024]{2,1,0:T(8,128)S(1)} %get-tuple-element.5), channel_id=1, source_target_pairs={{0,1},{1,2},{2,3},{3,4},{4,5},{5,6},{6,7},{8,9},{9,10},{10,11},{11... | collective-permute-start | bytes 1474568 | tf_op jit(solution)/shard_map/ppermute | solution.py:16
  287.1 10.4 %collective-permute-done.7 = f32[8,15,1024]{2,1,0:T(8,128)S(1)} collective-permute-done((f32[8,15,1024]{2,1,0:T(8,128)S(1)}, f32[8,15,1024]{2,1,0:T(8,128)S(1)}, u32[]{:S(2)}, u32[]{:S(2)}) %collective-permute-start.7) | collective-permute-done | bytes 491552 | tf_op jit(solution)/shard_map/ppermute | solution.py:17
  (129 shorter events, 34.5 us)
Async XLA Ops:
  0.0 19.4 %copy-start = (f32[8,16,1024]{2,1,0:T(8,128)S(1)}, f32[8,16,1024]{2,1,0:T(8,128)}, u32[]{:S(2)}) copy-start(f32[8,16,1024]{2,1,0:T(8,128)} %param.6) | copy-start | bytes 1572868
  0.0 12.1 %copy-start.4 = (f32[31]{0:T(128)S(1)}, f32[31]{0:T(128)}, u32[]{:S(2)}) copy-start(f32[31]{0:T(128)} %param.7) | copy-start | bytes 376
  0.0 12.8 %copy-start.5 = (f32[31]{0:T(128)S(1)}, f32[31]{0:T(128)}, u32[]{:S(2)}) copy-start(f32[31]{0:T(128)} %param.8) | copy-start | bytes 376
  1.4 18.1 %collective-permute-start.1 = (f32[8,15,1024]{2,1,0:T(8,128)S(1)}, f32[8,15,1024]{2,1,0:T(8,128)S(1)}, u32[]{:S(2)}, u32[]{:S(2)}) collective-permute-start(f32[8,15,1024]{2,1,0:T(8,128)S(1)} %get-tuple-element.12), channel_id=1, source_target_pairs={{1,0},{2,1},{3,2},{4,3},{5,4},{6,5},{7,6},{9,8},{10,9},{11,10},{12... | collective-permute-start | bytes 1474568 | tf_op jit(solution)/shard_map/ppermute | solution.py:17
  10.2 9.3 %collective-permute-start = (f32[8,15,1024]{2,1,0:T(8,128)S(1)}, f32[8,15,1024]{2,1,0:T(8,128)S(1)}, u32[]{:S(2)}, u32[]{:S(2)}) collective-permute-start(f32[8,15,1024]{2,1,0:T(8,128)S(1)} %get-tuple-element.11), channel_id=1, source_target_pairs={{0,1},{1,2},{2,3},{3,4},{4,5},{5,6},{6,7},{8,9},{9,10},{10,11},{11... | collective-permute-start | bytes 1474568 | tf_op jit(solution)/shard_map/ppermute | solution.py:16
  22.8 16.9 %copy-start.6 = (f32[63]{0:T(128)S(1)}, f32[63]{0:T(128)}, u32[]{:S(2)}) copy-start(f32[63]{0:T(128)} %param.9) | copy-start | bytes 760
  24.1 28.4 %all-to-all-start = ((f32[8,64,256]{2,0,1:T(8,128)}), f32[8,64,256]{2,0,1:T(8,128)S(1)}, u32[]{:S(2)}, u32[]{:S(2)}) async-start(f32[8,64,256]{2,0,1:T(8,128)} %copy.32), calls=%async_computation | async-start | bytes 1048576 | tf_op jit(solution)/shard_map/all_to_all | solution.py:55
  44.2 1.6 slice-start
  47.3 1.2 slice-start.2
  53.5 20.1 %copy-start.2 = (f32[8,16,1024]{2,1,0:T(8,128)S(1)}, f32[8,16,1024]{2,1,0:T(8,128)}, u32[]{:S(2)}) copy-start(f32[8,16,1024]{2,1,0:T(8,128)} %param.5) | copy-start | bytes 1572868
  74.9 18.0 %all-to-all-start.2 = ((f32[8,64,256]{2,0,1:T(8,128)}), f32[8,64,256]{2,0,1:T(8,128)}, u32[]{:S(2)}, u32[]{:S(2)}) async-start(f32[8,64,256]{2,0,1:T(8,128)} %copy.34), calls=%async_computation.2 | async-start | bytes 1048576 | tf_op jit(solution)/shard_map/all_to_all | solution.py:55
  83.7 1.6 slice-start.1
  86.8 1.2 slice-start.3
  115.1 36.4 %collective-permute-start.3 = (f32[8,15,1024]{2,1,0:T(8,128)}, f32[8,15,1024]{2,1,0:T(8,128)}, u32[]{:S(2)}, u32[]{:S(2)}) collective-permute-start(f32[8,15,1024]{2,1,0:T(8,128)} %get-tuple-element.10), channel_id=1, source_target_pairs={{1,0},{2,1},{3,2},{4,3},{5,4},{6,5},{7,6},{9,8},{10,9},{11,10},{12... | collective-permute-start | bytes 1474568 | tf_op jit(solution)/shard_map/ppermute | solution.py:17
  117.0 34.5 %collective-permute-start.2 = (f32[8,15,1024]{2,1,0:T(8,128)}, f32[8,15,1024]{2,1,0:T(8,128)}, u32[]{:S(2)}, u32[]{:S(2)}) collective-permute-start(f32[8,15,1024]{2,1,0:T(8,128)} %get-tuple-element.9), channel_id=1, source_target_pairs={{0,1},{1,2},{2,3},{3,4},{4,5},{5,6},{6,7},{8,9},{9,10},{10,11},{11... | collective-permute-start | bytes 1474568 | tf_op jit(solution)/shard_map/ppermute | solution.py:16
  154.4 2.5 copy-start.1
  158.0 16.4 %collective-permute-start.5 = (f32[8,15,1024]{2,1,0:T(8,128)S(1)}, f32[8,15,1024]{2,1,0:T(8,128)S(1)}, u32[]{:S(2)}, u32[]{:S(2)}) collective-permute-start(f32[8,15,1024]{2,1,0:T(8,128)S(1)} %get-tuple-element.8), channel_id=1, source_target_pairs={{1,0},{2,1},{3,2},{4,3},{5,4},{6,5},{7,6},{9,8},{10,9},{11,10},{12... | collective-permute-start | bytes 1474568 | tf_op jit(solution)/shard_map/ppermute | solution.py:17
  160.0 14.5 %collective-permute-start.4 = (f32[8,15,1024]{2,1,0:T(8,128)S(1)}, f32[8,15,1024]{2,1,0:T(8,128)S(1)}, u32[]{:S(2)}, u32[]{:S(2)}) collective-permute-start(f32[8,15,1024]{2,1,0:T(8,128)S(1)} %get-tuple-element.7), channel_id=1, source_target_pairs={{0,1},{1,2},{2,3},{3,4},{4,5},{5,6},{6,7},{8,9},{9,10},{10,11},{11... | collective-permute-start | bytes 1474568 | tf_op jit(solution)/shard_map/ppermute | solution.py:16
  201.6 18.4 %copy-start.3 = (f32[8,16,1024]{2,1,0:T(8,128)S(1)}, f32[8,16,1024]{2,1,0:T(8,128)}, u32[]{:S(2)}) copy-start(f32[8,16,1024]{2,1,0:T(8,128)} %param.5) | copy-start | bytes 1572868
  257.2 40.3 %collective-permute-start.7 = (f32[8,15,1024]{2,1,0:T(8,128)S(1)}, f32[8,15,1024]{2,1,0:T(8,128)S(1)}, u32[]{:S(2)}, u32[]{:S(2)}) collective-permute-start(f32[8,15,1024]{2,1,0:T(8,128)S(1)} %get-tuple-element.6), channel_id=1, source_target_pairs={{1,0},{2,1},{3,2},{4,3},{5,4},{6,5},{7,6},{9,8},{10,9},{11,10},{12... | collective-permute-start | bytes 1474568 | tf_op jit(solution)/shard_map/ppermute | solution.py:17
  259.1 38.3 %collective-permute-start.6 = (f32[8,15,1024]{2,1,0:T(8,128)S(1)}, f32[8,15,1024]{2,1,0:T(8,128)S(1)}, u32[]{:S(2)}, u32[]{:S(2)}) collective-permute-start(f32[8,15,1024]{2,1,0:T(8,128)S(1)} %get-tuple-element.5), channel_id=1, source_target_pairs={{0,1},{1,2},{2,3},{3,4},{4,5},{5,6},{6,7},{8,9},{9,10},{10,11},{11... | collective-permute-start | bytes 1474568 | tf_op jit(solution)/shard_map/ppermute | solution.py:16
where the time goes:
time: 304 us; the launch traced here: 302 us
  blocking collectives  112 us (37%)
  starting transfers between devices  93.9 us (31%)
  waiting for transfers between devices  41.5 us (14%)
  local copies, waits for them, and re-layouts  31 us (10%)
  matrix products  16.2 us (5%)
  other arithmetic  6.11 us (2%)
    all_to_all x4, blocking collectives, to_slabs(): lax.all_to_all(columns, 'gz', split_axis=0, concat_axis=1, tiled=True)  74 us
    ppermute x4, starting transfers between devices, extended(): before = lax.ppermute(last, axis, up)  58 us
    all_to_all x2, blocking collectives, to_columns(): lax.all_to_all(volume.reshape(planes, -1), 'gz', split_axis=1, concat_axi...  38.2 us
    ppermute x4, waiting for transfers between devices, extended(): after = lax.ppermute(leading, axis, down)  33.7 us
    all_to_all x2, starting transfers between devices, to_columns(): lax.all_to_all(volume.reshape(planes, -1), 'gz', split_axis=1, concat_axi...  21.4 us
    ppermute x4, starting transfers between devices, extended(): after = lax.ppermute(leading, axis, down)  14.5 us
    all_to_all x2, waiting for transfers between devices, to_columns(): lax.all_to_all(volume.reshape(planes, -1), 'gz', split_axis=1, concat_axi...  7.86 us
    another operation x12, local copies, waits for them, and re-layouts, banded(): tiled = jnp.tile(diagonals, n_out + 1)[:n_out * (span + 1)]  6.73 us
  transfers between devices with their start and end apart: 10, of which 6 were waited for; matrix products, arithmetic and copies ran while one was open for 5% of the time, Pallas kernels for 0%

commit v1 on v0

v1 whole, which is shorter than its diff:
```python
import jax
import jax.numpy as jnp
import numpy as np
from jax import lax
from jax.sharding import Mesh, PartitionSpec as P

ITERS = 2
HI = lax.Precision.HIGHEST
SLAB = ("x", "yl", "yh", "c")


def toeplitz(w, rows, cols, lead):
    taps = w.shape[0]
    period = cols + rows
    line = jnp.pad(w, (lead, period + 1 - lead - taps))
    flat = jnp.tile(line, rows)[: rows * period]
    return flat.reshape(rows, period)[:, :cols]


def x_index(b, c):
    x, yh, yl = b // 8, (b % 8) // 2, b % 2
    return ((x * 2 + yl) * 4 + yh) * 2 + c


SWAP = [(0, 1), (1, 0)]
NEXT = [(x_index(b, 0), x_index(b - 1, 1)) for b in range(1, 32)] + [
    (x_index(b, 1), x_index(b + 1, 0)) for b in range(31)
]
Z_FWD = [(((z + 1) % 8) * 2, z * 2) for z in range(8)] + [
    (((z - 1) % 8) * 2 + 1, z * 2 + 1) for z in range(8)
]
Z_ADJ = [(d, s) for s, d in Z_FWD]


def enter(volume):
    t = volume.reshape(128, 1024).T.reshape(4, 4, 2, 2, 16, 128)
    t = t.transpose(0, 2, 1, 3, 4, 5).reshape(64, 16, 128)
    t = lax.all_to_all(t, SLAB, 0, 0, tiled=True)
    t = t.reshape(8, 8, 16, 8, 16).transpose(2, 0, 3, 1, 4)
    return t.reshape(16, 64, 128)


def leave(block):
    t = block.reshape(16, 8, 8, 8, 16).transpose(1, 3, 0, 2, 4).reshape(64, 16, 128)
    t = lax.all_to_all(t, SLAB, 0, 0, tiled=True)
    t = t.reshape(4, 2, 4, 2, 16, 128).transpose(0, 2, 1, 3, 4, 5).reshape(1024, 128)
    return t.T.reshape(8, 16, 1024)


def per_device(observed, estimate, psf_y, psf_x, psf_z):
    core = lax.axis_index("c")
    slab = lax.axis_index("z")
    first = core == 0
    wy = psf_y / jnp.sum(psf_y)
    wx = psf_x / jnp.sum(psf_x)
    wz = psf_z / jnp.sum(psf_z)

    est = enter(estimate)
    obs = enter(observed)

    own_half = jnp.where(first, obs[:, :32], obs[:, 32:])
    keep = jnp.where(first, obs[:, 32:], obs[:, :32])
    got = lax.ppermute(own_half, ("z", "c"), Z_FWD)
    obs = jnp.concatenate([jnp.where(first, keep, got), jnp.where(first, got, keep)], axis=1)

    y_fwd = toeplitz(jnp.pad(wy, (0, 0)), 128, 158, 0)[:, 15:143].T
    y_adj = toeplitz(wy[::-1], 128, 158, 0)[:, 15:143].T

    row = lax.broadcasted_iota(jnp.int32, (64, 64), 0)
    col = lax.broadcasted_iota(jnp.int32, (64, 64), 1)
    zf = toeplitz(wz, 64, 128, 1)
    za = toeplitz(wz[::-1], 64, 128, 1)
    seam = jnp.where(first, slab == 7, slab == 0)
    f_lo = jnp.where(seam & (row >= 32), 0, zf[:, :64])
    f_hi = jnp.where(seam & (row < 32), 0, zf[:, 64:])
    a_lo = jnp.where((slab == 0) & (col < 32), 0, za[:, :64])
    a_hi = jnp.where((slab == 7) & (col >= 32), 0, za[:, 64:])
    f_own, f_got = jnp.where(first, f_lo, f_hi), jnp.where(first, f_hi, f_lo)
    a_own, a_got = jnp.where(first, a_hi, a_lo), jnp.where(first, a_lo, a_hi)

    def y_blur(v, m):
        return jnp.einsum("xzq,qy->xzy", v, m, precision=HI)

    def x_blur(v, w):
        swapped = lax.ppermute(v, "c", SWAP)
        passed = lax.ppermute(v, SLAB, NEXT)
        low = jnp.where(first, passed, swapped)
        high = jnp.where(first, swapped, passed)
        ext = jnp.concatenate([low, v, high], axis=0)
        total = w[0] * ext[1:17]
        for k in range(1, 31):
            total = total + w[k] * ext[k + 1 : k + 17]
        return total

    def z_blur(v, own, other, perm):
        got = lax.ppermute(v, ("z", "c"), perm)
        return jnp.einsum("xjy,ij->xiy", v, own, precision=HI) + jnp.einsum(
            "xjy,ij->xiy", got, other, precision=HI
        )

    for sweep in range(ITERS):
        blurred = z_blur(x_blur(y_blur(est, y_fwd), wx), f_own, f_got, Z_FWD)
        ratio = obs / blurred
        back = y_blur(x_blur(z_blur(ratio, a_own, a_got, Z_ADJ), wx[::-1]), y_adj)
        est = est * back
    return leave(est)


def solution(mesh):
    fine = Mesh(mesh.devices.reshape(8, 4, 2, 4, 2), ("z", "x", "yl", "yh", "c"))
    spec = P(("z", "x", "yl"), ("yh", "c"), None)
    return jax.shard_map(
        per_device,
        mesh=fine,
        in_specs=(spec, spec, P(), P(), P()),
        out_specs=spec,
        check_vma=False,
    )
```

time: 304 us -> 299 us (0.984)
  blocking collectives: 112 us -> 30.7 us
  other arithmetic: 6.11 us -> 49.3 us
  matrix products: 16.2 us -> 49.2 us
  starting transfers between devices: 93.9 us -> 62.7 us
  waiting for transfers between devices: 41.5 us -> 57.8 us
  local copies, waits for them, and re-layouts: 31 us -> 46.5 us
    all_to_all x6 -> x1, blocking collectives: 112 us -> 30.7 us  [leave(): t = lax.all_to_all(t, SLAB, 0, 0, tiled=True)]
    add x0 -> x2, other arithmetic: none -> 43.3 us  [x_blur(): total = total + w[k] * ext[k + 1:k + 17]]
    dot_general x12, matrix products: 16.2 us -> 49.2 us  [the longest x4 44.2 us: y_blur(): return jnp.einsum('xzq,qy->xzy', v, m, precision=HI)]
    ppermute x8 -> x13, starting transfers between devices: 72.5 us -> 45.1 us  [the longest x4 21.5 us: x_blur(): passed = lax.ppermute(v, SLAB, NEXT)]
    transpose x0 -> x8, local copies, waits for them, and re-layouts: none -> 18.5 us  [the longest x2 13.3 us: enter(): t = t.reshape(8, 8, 16, 8, 16).transpose(2, 0, 3, 1, 4)]
    reshape x12 -> x11, local copies, waits for them, and re-layouts: 5.14 us -> 22.9 us  [the longest x3 10.7 us: leave(): block.reshape(16, 8, 8, 8, 16).transpose(1, 3, 0, 2, 4).reshape(64, 16, 128)]
    ppermute x8 -> x13, waiting for transfers between devices: 33.7 us -> 44.3 us  [the longest x4 31.6 us: z_blur(): got = lax.ppermute(v, ('z', 'c'), perm)]
    all_to_all x12 -> x0, local copies, waits for them, and re-layouts: 5.93 us -> none  [the longest x8 5.24 us: to_columns(): lax.all_to_all(volume.reshape(planes, -1), 'gz', split_axis=1, concat_axi...]
  transfers between devices with their start and end apart: 10 -> 15, of which waited for: 6 -> 8; matrix products, arithmetic and copies ran while one was open for 5% -> 21% of each run, Pallas kernels for 0% -> 0%
where the time goes in v1:
time: 299 us; the launch traced here: 297 us
  starting transfers between devices  62.7 us (21%)
  waiting for transfers between devices  57.8 us (19%)
  other arithmetic  49.3 us (16%)
  matrix products  49.2 us (16%)
  local copies, waits for them, and re-layouts  46.5 us (16%)
  blocking collectives  30.7 us (10%)
    dot_general x4, matrix products, y_blur(): return jnp.einsum('xzq,qy->xzy', v, m, precision=HI)  44.2 us
    add x2, other arithmetic, x_blur(): total = total + w[k] * ext[k + 1:k + 17]  43.3 us
    ppermute x4, waiting for transfers between devices, z_blur(): got = lax.ppermute(v, ('z', 'c'), perm)  31.6 us
    all_to_all x1, blocking collectives, leave(): t = lax.all_to_all(t, SLAB, 0, 0, tiled=True)  30.7 us
    ppermute x4, starting transfers between devices, x_blur(): passed = lax.ppermute(v, SLAB, NEXT)  21.5 us
    all_to_all x2, starting transfers between devices, enter(): t = lax.all_to_all(t, SLAB, 0, 0, tiled=True)  17.5 us
    all_to_all x2, waiting for transfers between devices, enter(): t = lax.all_to_all(t, SLAB, 0, 0, tiled=True)  13.5 us
    transpose x2, local copies, waits for them, and re-layouts, enter(): t = t.reshape(8, 8, 16, 8, 16).transpose(2, 0, 3, 1, 4)  13.3 us
  transfers between devices with their start and end apart: 15, of which 8 were waited for; matrix products, arithmetic and copies ran while one was open for 21% of the time, Pallas kernels for 0%

profile of v1, /device:TPU:1, one launch (start us, length us, event | category | flops | bytes accessed | tf_op | source)
XLA Modules:
  0.0 296.7 jit_solution(4267866911851651171)
XLA Ops:
  2.1 11.6 %all-to-all-start = ((f32[64,16,128]{2,1,0:T(8,128)}), f32[64,16,128]{2,1,0:T(8,128)S(1)}, u32[]{:S(2)}, u32[]{:S(2)}) async-start(f32[64,16,128]{2,1,0:T(8,128)} %bitcast.4), calls=%async_computation | async-start | bytes 1048576 | tf_op jit(solution)/shard_map/all_to_all | solution.py:38
  18.0 13.5 %all-to-all-done = f32[64,16,128]{2,1,0:T(8,128)S(1)} async-done(((f32[64,16,128]{2,1,0:T(8,128)}), f32[64,16,128]{2,1,0:T(8,128)S(1)}, u32[]{:S(2)}, u32[]{:S(2)}) %all-to-all-start) | async-done | bytes 524320 | tf_op jit(solution)/shard_map/all_to_all | solution.py:38
  31.5 5.9 %all-to-all-start.1 = ((f32[64,16,128]{2,1,0:T(8,128)}), f32[64,16,128]{2,1,0:T(8,128)S(1)}, u32[]{:S(2)}, u32[]{:S(2)}) async-start(f32[64,16,128]{2,1,0:T(8,128)} %bitcast.12), calls=%async_computation.1 | async-start | bytes 1048576 | tf_op jit(solution)/shard_map/all_to_all | solution.py:38
  41.5 2.6 reshape.64
  44.1 6.6 %copy.17 = f32[16,8,8,8,16]{4,3,2,1,0:T(8,128)} copy(f32[16,8,8,8,16]{4,2,0,3,1:T(8,128)} %bitcast.148) | data formatting | bytes 1048576 | tf_op jit(solution)/shard_map/transpose | solution.py:39
  50.7 3.2 %reshape.65 = f32[16,64,128]{2,1,0:T(8,128)S(1)} reshape(f32[16,8,8,8,16]{4,3,2,1,0:T(8,128)} %copy.17) | data formatting | bytes 1048576 | tf_op jit(solution)/shard_map/reshape | solution.py:40
  54.6 3.5 %collective-permute-start.1 = (f32[16,64,128]{2,1,0:T(8,128)S(1)}, f32[16,64,128]{2,1,0:T(8,128)S(1)}, u32[]{:S(2)}, u32[]{:S(2)}) collective-permute-start(f32[16,64,128]{2,1,0:T(8,128)S(1)} %convolution_bitcast_fusion), channel_id=1, source_target_pairs={{8,1},{2,9},{10,3},{4,11},{12,5},{6,13},{14,7},{16,15},{24,17},{18... | collective-permute-start | bytes 1572872 | tf_op jit(solution)/shard_map/ppermute | solution.py:86
  61.4 2.6 reshape.70
  64.0 6.6 %copy.20 = f32[16,8,8,8,16]{4,3,2,1,0:T(8,128)} copy(f32[16,8,8,8,16]{4,2,0,3,1:T(8,128)} %bitcast.149) | data formatting | bytes 1048576 | tf_op jit(solution)/shard_map/transpose | solution.py:39
  70.6 3.2 %reshape.71 = f32[16,64,128]{2,1,0:T(8,128)S(1)} reshape(f32[16,8,8,8,16]{4,3,2,1,0:T(8,128)} %copy.20) | data formatting | bytes 1048576 | tf_op jit(solution)/shard_map/reshape | solution.py:40
  73.9 4.2 %collective-permute-start = (f32[16,32,128]{2,1,0:T(8,128)S(1)}, f32[16,32,128]{2,1,0:T(8,128)}, u32[]{:S(2)}, u32[]{:S(2)}) collective-permute-start(f32[16,32,128]{2,1,0:T(8,128)S(1)} %slice_select_fusion), channel_id=1, source_target_pairs={{64,0},{128,64},{192,128},{256,192},{320,256},{384,320},{448,384},... | collective-permute-start | bytes 786440 | tf_op jit(solution)/shard_map/ppermute | solution.py:63
  78.2 21.6 %fusion.323 = f32[16,64,128]{2,1,0:T(8,128)S(1)} fusion(f32[16,64,128]{2,1,0:T(8,128)S(1)} %convolution_bitcast_fusion, f32[16,64,128]{2,1,0:T(8,128)S(1)} %get-tuple-element.12, f32[16,64,128]{2,1,0:T(8,128)S(1)} %get-tuple-element.11, f32[]{:T(128)} %bitcast.47, f32[]{:T(128)} %bitcast.46, f32[]{:T(128)} %bitcast.45, f32[]{:T(128)} %bitcast.44, ...), kind=kLoop, calls=%fused_computation.499 | loop fusion | flops 11927552 | bytes 2097276 | tf_op jit(solution)/shard_map/add | solution.py:92
  99.8 4.0 %collective-permute-start.3 = (f32[16,64,128]{2,1,0:T(8,128)S(1)}, f32[16,64,128]{2,1,0:T(8,128)S(1)}, u32[]{:S(2)}, u32[]{:S(2)}) collective-permute-start(f32[16,64,128]{2,1,0:T(8,128)S(1)} %fusion.323), channel_id=1, source_target_pairs={{64,0},{128,64},{192,128},{256,192},{320,256},{384,320},{448,384},... | collective-permute-start | bytes 1572872 | tf_op jit(solution)/shard_map/ppermute | solution.py:96
  105.9 9.1 %collective-permute-done.3 = f32[16,64,128]{2,1,0:T(8,128)S(1)} collective-permute-done((f32[16,64,128]{2,1,0:T(8,128)S(1)}, f32[16,64,128]{2,1,0:T(8,128)S(1)}, u32[]{:S(2)}, u32[]{:S(2)}) %collective-permute-start.3) | collective-permute-done | bytes 524320 | tf_op jit(solution)/shard_map/ppermute | solution.py:96
  115.6 3.7 %collective-permute-start.4 = (f32[16,64,128]{2,1,0:T(8,128)S(1)}, f32[16,64,128]{2,1,0:T(8,128)S(1)}, u32[]{:S(2)}, u32[]{:S(2)}) collective-permute-start(f32[16,64,128]{2,1,0:T(8,128)S(1)} %fusion.5), channel_id=1, source_target_pairs={{0,64},{64,128},{128,192},{192,256},{256,320},{320,384},{384,448},... | collective-permute-start | bytes 1572872 | tf_op jit(solution)/shard_map/ppermute | solution.py:96
  119.7 6.2 %collective-permute-done.4 = f32[16,64,128]{2,1,0:T(8,128)S(1)} collective-permute-done((f32[16,64,128]{2,1,0:T(8,128)S(1)}, f32[16,64,128]{2,1,0:T(8,128)S(1)}, u32[]{:S(2)}, u32[]{:S(2)}) %collective-permute-start.4) | collective-permute-done | bytes 524320 | tf_op jit(solution)/shard_map/ppermute | solution.py:96
  127.1 8.4 %collective-permute-start.5 = (f32[16,64,128]{2,1,0:T(8,128)S(1)}, f32[16,64,128]{2,1,0:T(8,128)S(1)}, u32[]{:S(2)}, u32[]{:S(2)}) collective-permute-start(f32[16,64,128]{2,1,0:T(8,128)S(1)} %fusion.3), channel_id=1, source_target_pairs={{8,1},{2,9},{10,3},{4,11},{12,5},{6,13},{14,7},{16,15},{24,17},{18... | collective-permute-start | bytes 1572872 | tf_op jit(solution)/shard_map/ppermute | solution.py:86
  139.5 2.9 collective-permute-done.5
  142.5 21.1 %convolution_multiply_fusion.1 = f32[16,64,128]{2,1,0:T(8,128)S(1)} fusion(f32[16,64,128]{2,1,0:T(8,128)S(1)} %reshape.65, f32[16,64,128]{2,1,0:T(8,128)S(1)} %fusion.3, f32[16,64,128]{2,1,0:T(8,128)S(1)} %get-tuple-element.10, f32[16,64,128]{2,1,0:T(8,128)S(1)} %get-tuple-element.9, f32[]{:T(128)} %bitcast.81, f32[]{:T(128)} %bitcast.80, f32[]{:T(128)} %bitcast.79, ...), kind=kOutput, calls=%fused_computation.232 | convolution fusion | flops 213385216 | bytes 2687100 | tf_op jit(solution)/shard_map/xzq,qy->xzy/dot_general | solution.py:82
  164.2 3.6 %collective-permute-start.7 = (f32[16,64,128]{2,1,0:T(8,128)S(1)}, f32[16,64,128]{2,1,0:T(8,128)S(1)}, u32[]{:S(2)}, u32[]{:S(2)}) collective-permute-start(f32[16,64,128]{2,1,0:T(8,128)S(1)} %fusion.486), channel_id=1, source_target_pairs={{8,1},{2,9},{10,3},{4,11},{12,5},{6,13},{14,7},{16,15},{24,17},{18... | collective-permute-start | bytes 1572872 | tf_op jit(solution)/shard_map/ppermute | solution.py:86
  169.8 4.9 %collective-permute-done.7 = f32[16,64,128]{2,1,0:T(8,128)S(1)} collective-permute-done((f32[16,64,128]{2,1,0:T(8,128)S(1)}, f32[16,64,128]{2,1,0:T(8,128)S(1)}, u32[]{:S(2)}, u32[]{:S(2)}) %collective-permute-start.7) | collective-permute-done | bytes 524320 | tf_op jit(solution)/shard_map/ppermute | solution.py:86
  174.8 21.7 %fusion.123 = f32[16,64,128]{2,1,0:T(8,128)S(1)} fusion(f32[16,64,128]{2,1,0:T(8,128)S(1)} %fusion.486, f32[16,64,128]{2,1,0:T(8,128)S(1)} %get-tuple-element.8, f32[16,64,128]{2,1,0:T(8,128)S(1)} %get-tuple-element.7, f32[]{:T(128)} %bitcast.47, f32[]{:T(128)} %bitcast.46, f32[]{:T(128)} %bitcast.45, f32[]{:T(128)} %bitcast.44, f32[]{:T(128)} %bitcast.43, ...), kind=kLoop, calls=%fused_computation.327 | loop fusion | flops 11927552 | bytes 2097276 | tf_op jit(solution)/shard_map/add | solution.py:92
  199.1 8.6 %collective-permute-done.9 = f32[16,64,128]{2,1,0:T(8,128)S(1)} collective-permute-done((f32[16,64,128]{2,1,0:T(8,128)S(1)}, f32[16,64,128]{2,1,0:T(8,128)S(1)}, u32[]{:S(2)}, u32[]{:S(2)}) %collective-permute-start.9) | collective-permute-done | bytes 524320 | tf_op jit(solution)/shard_map/ppermute | solution.py:96
  208.3 2.1 collective-permute-start.10
  210.5 7.8 %collective-permute-done.10 = f32[16,64,128]{2,1,0:T(8,128)S(1)} collective-permute-done((f32[16,64,128]{2,1,0:T(8,128)S(1)}, f32[16,64,128]{2,1,0:T(8,128)S(1)}, u32[]{:S(2)}, u32[]{:S(2)}) %collective-permute-start.10) | collective-permute-done | bytes 524320 | tf_op jit(solution)/shard_map/ppermute | solution.py:96
  219.5 5.9 %collective-permute-start.11 = (f32[16,64,128]{2,1,0:T(8,128)S(1)}, f32[16,64,128]{2,1,0:T(8,128)S(1)}, u32[]{:S(2)}, u32[]{:S(2)}) collective-permute-start(f32[16,64,128]{2,1,0:T(8,128)S(1)} %fusion), channel_id=1, source_target_pairs={{8,1},{2,9},{10,3},{4,11},{12,5},{6,13},{14,7},{16,15},{24,17},{18... | collective-permute-start | bytes 1572872 | tf_op jit(solution)/shard_map/ppermute | solution.py:86
  227.4 4.9 %collective-permute-done.11 = f32[16,64,128]{2,1,0:T(8,128)S(1)} collective-permute-done((f32[16,64,128]{2,1,0:T(8,128)S(1)}, f32[16,64,128]{2,1,0:T(8,128)S(1)}, u32[]{:S(2)}, u32[]{:S(2)}) %collective-permute-start.11) | collective-permute-done | bytes 524320 | tf_op jit(solution)/shard_map/ppermute | solution.py:86
  232.4 21.8 %convolution_multiply_fusion = f32[16,64,128]{2,1,0:T(8,128)S(1)} fusion(f32[16,64,128]{2,1,0:T(8,128)S(1)} %convolution_multiply_fusion.1, f32[16,64,128]{2,1,0:T(8,128)S(1)} %fusion, f32[16,64,128]{2,1,0:T(8,128)S(1)} %get-tuple-element.6, f32[16,64,128]{2,1,0:T(8,128)S(1)} %get-tuple-element.5, f32[]{:T(128)} %bitcast.81, f32[]{:T(128)} %bitcast.80, ...), kind=kOutput, calls=%fused_computation.226 | convolution fusion | flops 213385216 | bytes 2702848 | tf_op jit(solution)/shard_map/xzq,qy->xzy/dot_general | solution.py:82
  254.2 2.6 reshape.75
  256.8 4.9 %copy.25 = f32[16,8,8,8,16]{4,2,0,3,1:T(8,128)} copy(f32[16,8,8,8,16]{4,3,2,1,0:T(8,128)} %reshape.75) | data formatting | bytes 1048576 | tf_op jit(solution)/shard_map/reshape | solution.py:44
  261.7 3.2 %reshape.76 = f32[64,16,128]{2,1,0:T(8,128)S(1)} reshape(f32[8,8,16,8,16]{4,3,2,1,0:T(8,128)} %bitcast.150) | data formatting | bytes 1048576 | tf_op jit(solution)/shard_map/reshape | solution.py:44
  265.0 30.7 %all_to_all.15 = f32[64,16,128]{2,1,0:T(8,128)S(1)} all-to-all(f32[64,16,128]{2,1,0:T(8,128)S(1)} %reshape.76), channel_id=1, replica_groups=mesh['z'=8,'x'=4,'yl'=2,'yh'=4,'c'=2] {'x','yl','yh','c'}, dimensions={0} | all-to-all | bytes 1048576 | tf_op jit(solution)/shard_map/all_to_all | solution.py:45
  (76 shorter events, 32.9 us)
Async XLA Ops:
  0.0 37.4 %copy-start.1 = (f32[31]{0:T(128)S(1)}, f32[31]{0:T(128)}, u32[]{:S(2)}) copy-start(f32[31]{0:T(128)} %param.7) | copy-start | bytes 376
  0.0 38.1 %copy-start.2 = (f32[31]{0:T(128)S(1)}, f32[31]{0:T(128)}, u32[]{:S(2)}) copy-start(f32[31]{0:T(128)} %param.8) | copy-start | bytes 376
  0.0 38.8 %copy-start.3 = (f32[63]{0:T(128)S(1)}, f32[63]{0:T(128)}, u32[]{:S(2)}) copy-start(f32[63]{0:T(128)} %param.9) | copy-start | bytes 760
  2.1 29.3 %all-to-all-start = ((f32[64,16,128]{2,1,0:T(8,128)}), f32[64,16,128]{2,1,0:T(8,128)S(1)}, u32[]{:S(2)}, u32[]{:S(2)}) async-start(f32[64,16,128]{2,1,0:T(8,128)} %bitcast.4), calls=%async_computation | async-start | bytes 1048576 | tf_op jit(solution)/shard_map/all_to_all | solution.py:38
  31.5 30.0 %all-to-all-start.1 = ((f32[64,16,128]{2,1,0:T(8,128)}), f32[64,16,128]{2,1,0:T(8,128)S(1)}, u32[]{:S(2)}, u32[]{:S(2)}) async-start(f32[64,16,128]{2,1,0:T(8,128)} %bitcast.12), calls=%async_computation.1 | async-start | bytes 1048576 | tf_op jit(solution)/shard_map/all_to_all | solution.py:38
  54.6 23.5 %collective-permute-start.1 = (f32[16,64,128]{2,1,0:T(8,128)S(1)}, f32[16,64,128]{2,1,0:T(8,128)S(1)}, u32[]{:S(2)}, u32[]{:S(2)}) collective-permute-start(f32[16,64,128]{2,1,0:T(8,128)S(1)} %convolution_bitcast_fusion), channel_id=1, source_target_pairs={{8,1},{2,9},{10,3},{4,11},{12,5},{6,13},{14,7},{16,15},{24,17},{18... | collective-permute-start | bytes 1572872 | tf_op jit(solution)/shard_map/ppermute | solution.py:86
  58.1 19.9 %collective-permute-start.2 = (f32[16,64,128]{2,1,0:T(8,128)S(1)}, f32[16,64,128]{2,1,0:T(8,128)S(1)}, u32[]{:S(2)}, u32[]{:S(2)}) collective-permute-start(f32[16,64,128]{2,1,0:T(8,128)S(1)} %convolution_bitcast_fusion), channel_id=1, source_target_pairs={{0,1},{1,0},{2,3},{3,2},{4,5},{5,4},{6,7},{7,6},{8,9},{9,8},{10,11... | collective-permute-start | bytes 1572872 | tf_op jit(solution)/shard_map/ppermute | solution.py:85
  73.9 30.4 %collective-permute-start = (f32[16,32,128]{2,1,0:T(8,128)S(1)}, f32[16,32,128]{2,1,0:T(8,128)}, u32[]{:S(2)}, u32[]{:S(2)}) collective-permute-start(f32[16,32,128]{2,1,0:T(8,128)S(1)} %slice_select_fusion), channel_id=1, source_target_pairs={{64,0},{128,64},{192,128},{256,192},{320,256},{384,320},{448,384},... | collective-permute-start | bytes 786440 | tf_op jit(solution)/shard_map/ppermute | solution.py:63
  99.8 15.2 %collective-permute-start.3 = (f32[16,64,128]{2,1,0:T(8,128)S(1)}, f32[16,64,128]{2,1,0:T(8,128)S(1)}, u32[]{:S(2)}, u32[]{:S(2)}) collective-permute-start(f32[16,64,128]{2,1,0:T(8,128)S(1)} %fusion.323), channel_id=1, source_target_pairs={{64,0},{128,64},{192,128},{256,192},{320,256},{384,320},{448,384},... | collective-permute-start | bytes 1572872 | tf_op jit(solution)/shard_map/ppermute | solution.py:96
  115.6 10.2 %collective-permute-start.4 = (f32[16,64,128]{2,1,0:T(8,128)S(1)}, f32[16,64,128]{2,1,0:T(8,128)S(1)}, u32[]{:S(2)}, u32[]{:S(2)}) collective-permute-start(f32[16,64,128]{2,1,0:T(8,128)S(1)} %fusion.5), channel_id=1, source_target_pairs={{0,64},{64,128},{128,192},{192,256},{256,320},{320,384},{384,448},... | collective-permute-start | bytes 1572872 | tf_op jit(solution)/shard_map/ppermute | solution.py:96
  127.1 15.3 %collective-permute-start.5 = (f32[16,64,128]{2,1,0:T(8,128)S(1)}, f32[16,64,128]{2,1,0:T(8,128)S(1)}, u32[]{:S(2)}, u32[]{:S(2)}) collective-permute-start(f32[16,64,128]{2,1,0:T(8,128)S(1)} %fusion.3), channel_id=1, source_target_pairs={{8,1},{2,9},{10,3},{4,11},{12,5},{6,13},{14,7},{16,15},{24,17},{18... | collective-permute-start | bytes 1572872 | tf_op jit(solution)/shard_map/ppermute | solution.py:86
  135.5 6.9 %collective-permute-start.6 = (f32[16,64,128]{2,1,0:T(8,128)S(1)}, f32[16,64,128]{2,1,0:T(8,128)S(1)}, u32[]{:S(2)}, u32[]{:S(2)}) collective-permute-start(f32[16,64,128]{2,1,0:T(8,128)S(1)} %fusion.3), channel_id=1, source_target_pairs={{0,1},{1,0},{2,3},{3,2},{4,5},{5,4},{6,7},{7,6},{8,9},{9,8},{10,11... | collective-permute-start | bytes 1572872 | tf_op jit(solution)/shard_map/ppermute | solution.py:85
  138.1 25.5 %copy-start = (f32[128,286]{1,0:T(8,128)}, f32[128,286]{1,0:T(8,128)S(1)}, u32[]{:S(2)}) copy-start(f32[128,286]{1,0:T(8,128)S(1)} %reshape.74) | copy-start | bytes 439300
  164.2 10.5 %collective-permute-start.7 = (f32[16,64,128]{2,1,0:T(8,128)S(1)}, f32[16,64,128]{2,1,0:T(8,128)S(1)}, u32[]{:S(2)}, u32[]{:S(2)}) collective-permute-start(f32[16,64,128]{2,1,0:T(8,128)S(1)} %fusion.486), channel_id=1, source_target_pairs={{8,1},{2,9},{10,3},{4,11},{12,5},{6,13},{14,7},{16,15},{24,17},{18... | collective-permute-start | bytes 1572872 | tf_op jit(solution)/shard_map/ppermute | solution.py:86
  167.9 6.9 %collective-permute-start.8 = (f32[16,64,128]{2,1,0:T(8,128)S(1)}, f32[16,64,128]{2,1,0:T(8,128)S(1)}, u32[]{:S(2)}, u32[]{:S(2)}) collective-permute-start(f32[16,64,128]{2,1,0:T(8,128)S(1)} %fusion.486), channel_id=1, source_target_pairs={{0,1},{1,0},{2,3},{3,2},{4,5},{5,4},{6,7},{7,6},{8,9},{9,8},{10,11... | collective-permute-start | bytes 1572872 | tf_op jit(solution)/shard_map/ppermute | solution.py:85
  196.5 11.1 %collective-permute-start.9 = (f32[16,64,128]{2,1,0:T(8,128)S(1)}, f32[16,64,128]{2,1,0:T(8,128)S(1)}, u32[]{:S(2)}, u32[]{:S(2)}) collective-permute-start(f32[16,64,128]{2,1,0:T(8,128)S(1)} %fusion.123), channel_id=1, source_target_pairs={{64,0},{128,64},{192,128},{256,192},{320,256},{384,320},{448,384},... | collective-permute-start | bytes 1572872 | tf_op jit(solution)/shard_map/ppermute | solution.py:96
  208.3 9.9 %collective-permute-start.10 = (f32[16,64,128]{2,1,0:T(8,128)S(1)}, f32[16,64,128]{2,1,0:T(8,128)S(1)}, u32[]{:S(2)}, u32[]{:S(2)}) collective-permute-start(f32[16,64,128]{2,1,0:T(8,128)S(1)} %fusion.2), channel_id=1, source_target_pairs={{0,64},{64,128},{128,192},{192,256},{256,320},{320,384},{384,448},... | collective-permute-start | bytes 1572872 | tf_op jit(solution)/shard_map/ppermute | solution.py:96
  219.5 12.8 %collective-permute-start.11 = (f32[16,64,128]{2,1,0:T(8,128)S(1)}, f32[16,64,128]{2,1,0:T(8,128)S(1)}, u32[]{:S(2)}, u32[]{:S(2)}) collective-permute-start(f32[16,64,128]{2,1,0:T(8,128)S(1)} %fusion), channel_id=1, source_target_pairs={{8,1},{2,9},{10,3},{4,11},{12,5},{6,13},{14,7},{16,15},{24,17},{18... | collective-permute-start | bytes 1572872 | tf_op jit(solution)/shard_map/ppermute | solution.py:86
  225.4 6.9 %collective-permute-start.12 = (f32[16,64,128]{2,1,0:T(8,128)S(1)}, f32[16,64,128]{2,1,0:T(8,128)S(1)}, u32[]{:S(2)}, u32[]{:S(2)}) collective-permute-start(f32[16,64,128]{2,1,0:T(8,128)S(1)} %fusion), channel_id=1, source_target_pairs={{0,1},{1,0},{2,3},{3,2},{4,5},{5,4},{6,7},{7,6},{8,9},{9,8},{10,11... | collective-permute-start | bytes 1572872 | tf_op jit(solution)/shard_map/ppermute | solution.py:85

commit v2 on v1

v2 whole, which is shorter than its diff:
```python
import functools

import jax
import jax.numpy as jnp
from jax import lax
from jax.experimental import pallas as pl
from jax.experimental.pallas import tpu as pltpu
from jax.sharding import Mesh, PartitionSpec as P

ITERS = 2
HI = lax.Precision.HIGHEST
SLAB = ("x", "yl", "yh", "c")
BLOCK = jax.ShapeDtypeStruct((16, 64, 128), jnp.float32)
VMEM = pl.BlockSpec(memory_space=pltpu.VMEM)
SMEM = pl.BlockSpec(memory_space=pltpu.SMEM)


def x_index(b, c):
    x, yh, yl = b // 8, (b % 8) // 2, b % 2
    return ((x * 2 + yl) * 4 + yh) * 2 + c


SWAP = [(0, 1), (1, 0)]
NEXT = [(x_index(b, 0), x_index(b - 1, 1)) for b in range(1, 32)] + [
    (x_index(b, 1), x_index(b + 1, 0)) for b in range(31)
]
Z_FWD = [(((z + 1) % 8) * 2, z * 2) for z in range(8)] + [
    (((z - 1) % 8) * 2 + 1, z * 2 + 1) for z in range(8)
]
Z_ADJ = [(d, s) for s, d in Z_FWD]


def cost(us):
    return pl.CostEstimate(flops=int(us * 1e6), bytes_accessed=int(us * 3e6), transcendentals=0)


def swap_groups(tile):
    row = lax.broadcasted_iota(jnp.int32, (8, 128), 0)
    group = lax.broadcasted_iota(jnp.int32, (8, 128), 1) // 16
    for b in (1, 2, 4):
        up = pltpu.roll(pltpu.roll(tile, 8 - b, 0), 16 * b, 1)
        down = up if b == 4 else pltpu.roll(pltpu.roll(tile, b, 0), 128 - 16 * b, 1)
        take_up = ((row & b) == 0) & ((group & b) != 0)
        take_down = ((row & b) != 0) & ((group & b) == 0)
        tile = jnp.where(take_up, up, jnp.where(take_down, down, tile))
    return tile


def unpack_kernel(in_ref, out_ref):
    for zc in range(8):
        for x in range(16):
            tile = in_ref[pl.ds(zc * 128 + x, 8, stride=16), :]
            out_ref[x, zc * 8 : zc * 8 + 8, :] = swap_groups(tile)


def pack_kernel(in_ref, out_ref):
    for zc in range(8):
        for x in range(16):
            tile = in_ref[x, zc * 8 : zc * 8 + 8, :]
            out_ref[pl.ds(zc * 128 + x, 8, stride=16), :] = swap_groups(tile)


def unpack(rows):
    return pl.pallas_call(
        unpack_kernel, out_shape=BLOCK, in_specs=[VMEM], out_specs=VMEM, cost_estimate=cost(1), name="unpack"
    )(rows)


def pack(block):
    return pl.pallas_call(
        pack_kernel,
        out_shape=jax.ShapeDtypeStruct((1024, 128), jnp.float32),
        in_specs=[VMEM],
        out_specs=VMEM,
        cost_estimate=cost(1),
        name="pack",
    )(block)


def enter(volume):
    t = volume.reshape(128, 1024).T.reshape(4, 4, 2, 2, 16, 128)
    t = t.transpose(0, 2, 1, 3, 4, 5).reshape(64, 16, 128)
    t = lax.all_to_all(t, SLAB, 0, 0, tiled=True)
    return unpack(t.reshape(1024, 128))


def leave(block):
    t = pack(block).reshape(64, 16, 128)
    t = lax.all_to_all(t, SLAB, 0, 0, tiled=True)
    t = t.reshape(4, 2, 4, 2, 16, 128).transpose(0, 2, 1, 3, 4, 5).reshape(1024, 128)
    return t.T.reshape(8, 16, 1024)


def tap_vectors(psf_ref, flip):
    total = psf_ref[0]
    for k in range(1, 31):
        total = total + psf_ref[k]
    scale = 1.0 / jnp.full((8, 128), total, jnp.float32)
    return [psf_ref[30 - k if flip else k] * scale for k in range(31)]


def x_own_kernel(flip, psf_ref, own_ref, out_ref):
    w = tap_vectors(psf_ref, flip)

    def body(t, _):
        z = pl.ds(pl.multiple_of(t * 8, 8), 8)
        acc = [None] * 16
        for j in range(16):
            v = own_ref[j, z, :]
            for i in range(16):
                p = w[j - i + 15] * v
                acc[i] = p if acc[i] is None else acc[i] + p
        for i in range(16):
            out_ref[i, z, :] = acc[i]
        return 0

    lax.fori_loop(0, 8, body, 0)


def x_rest_kernel(flip, psf_ref, core_ref, part_ref, passed_ref, swapped_ref, out_ref):
    w = tap_vectors(psf_ref, flip)

    def run(low_ref, high_ref):
        def body(t, _):
            z = pl.ds(pl.multiple_of(t * 8, 8), 8)
            acc = [part_ref[i, z, :] for i in range(16)]
            for j in range(16):
                low, high = low_ref[j, z, :], high_ref[j, z, :]
                for i in range(16):
                    if i < j:
                        acc[i] = acc[i] + w[j - i - 1] * low
                    if i > j:
                        acc[i] = acc[i] + w[j - i + 31] * high
            for i in range(16):
                out_ref[i, z, :] = acc[i]
            return 0

        lax.fori_loop(0, 8, body, 0)

    @pl.when(core_ref[0] == 0)
    def _():
        run(passed_ref, swapped_ref)

    @pl.when(core_ref[0] != 0)
    def _():
        run(swapped_ref, passed_ref)


def x_blur(v, psf, core, flip):
    swapped = lax.ppermute(v, "c", SWAP)
    passed = lax.ppermute(v, SLAB, NEXT)
    part = pl.pallas_call(
        functools.partial(x_own_kernel, flip),
        out_shape=BLOCK,
        in_specs=[SMEM, VMEM],
        out_specs=VMEM,
        cost_estimate=cost(1),
        name="x_own",
    )(psf, v)
    return pl.pallas_call(
        functools.partial(x_rest_kernel, flip),
        out_shape=BLOCK,
        in_specs=[SMEM, SMEM, VMEM, VMEM, VMEM],
        out_specs=VMEM,
        cost_estimate=cost(1),
        name="x_rest",
    )(psf, core, part, passed, swapped)


def prep_kernel(place_ref, lines_ref, yf_ref, ya_ref, fo_ref, fg_ref, ao_ref, ag_ref):
    slab, first = place_ref[0], place_ref[1] == 0

    def band(at, rows):
        line = lines_ref[at : at + 1, :]
        line = line / jnp.sum(line, axis=1, keepdims=True)
        return pltpu.roll(jnp.broadcast_to(line, (rows, 256)), 0, 1, stride=1, stride_axis=0)

    yf_ref[...] = band(0, 128)[:, :128]
    ya_ref[...] = band(1, 128)[:, :128]
    row = lax.broadcasted_iota(jnp.int32, (64, 128), 0)
    col = lax.broadcasted_iota(jnp.int32, (64, 128), 1)
    fwd, adj = band(2, 64)[:, :128], band(3, 64)[:, :128]
    seam = (first & (slab == 7)) | (jnp.logical_not(first) & (slab == 0))
    seam = jnp.where(seam, 1, 0)
    fwd = jnp.where((seam == 1) & ((row >= 32) == (col < 64)), 0.0, fwd)
    bottom, top = jnp.where(slab == 0, 1, 0), jnp.where(slab == 7, 1, 0)
    adj = jnp.where((bottom == 1) & (col < 32), 0.0, adj)
    adj = jnp.where((top == 1) & (col >= 96), 0.0, adj)
    fl, fh, al, ah = fwd[:, :64], fwd[:, 64:], adj[:, :64], adj[:, 64:]
    pick = jnp.where(first, 1, 0) == 1
    fo_ref[...] = jnp.where(pick, fl, fh)
    fg_ref[...] = jnp.where(pick, fh, fl)
    ao_ref[...] = jnp.where(pick, ah, al)
    ag_ref[...] = jnp.where(pick, al, ah)


def prepare(psf_y, psf_z, slab, core):
    def line(taps, start):
        return jnp.roll(jnp.pad(taps, (0, 256 - taps.shape[0])), start)

    lines = jnp.stack(
        [line(psf_y[::-1], -15), line(psf_y, -15), line(psf_z, 1), line(psf_z[::-1], 1)]
    )
    lines = jnp.concatenate([lines, lines], axis=0)
    square = jax.ShapeDtypeStruct((128, 128), jnp.float32)
    small = jax.ShapeDtypeStruct((64, 64), jnp.float32)
    return pl.pallas_call(
        prep_kernel,
        out_shape=[square, square, small, small, small, small],
        in_specs=[SMEM, VMEM],
        out_specs=[VMEM] * 6,
        cost_estimate=cost(2),
        name="prepare",
    )(jnp.stack([slab, core]), lines)


def y_blur(v, m):
    return jnp.einsum("xzq,qy->xzy", v, m, precision=HI)


def z_blur(v, own, other, perm):
    got = lax.ppermute(v, ("z", "c"), perm)
    near = jnp.einsum("xjy,ij->xiy", v, own, precision=HI)
    return near + jnp.einsum("xjy,ij->xiy", got, other, precision=HI)


def per_device(observed, estimate, psf_y, psf_x, psf_z):
    core = lax.axis_index("c")
    slab = lax.axis_index("z")
    first = core == 0
    core_at = core.reshape(1)
    y_fwd, y_adj, f_own, f_got, a_own, a_got = prepare(psf_y, psf_z, slab, core)

    est = enter(estimate)
    obs = enter(observed)

    send = jnp.where(first, obs[:, :32], obs[:, 32:])
    keep = jnp.where(first, obs[:, 32:], obs[:, :32])
    got = lax.ppermute(send, ("z", "c"), Z_FWD)
    obs = jnp.concatenate([jnp.where(first, keep, got), jnp.where(first, got, keep)], axis=1)

    for sweep in range(ITERS):
        blurred = x_blur(y_blur(est, y_fwd), psf_x, core_at, False)
        ratio = obs / z_blur(blurred, f_own, f_got, Z_FWD)
        back = x_blur(z_blur(ratio, a_own, a_got, Z_ADJ), psf_x, core_at, True)
        est = est * y_blur(back, y_adj)
    return leave(est)


def solution(mesh):
    fine = Mesh(mesh.devices.reshape(8, 4, 2, 4, 2), ("z", "x", "yl", "yh", "c"))
    spec = P(("z", "x", "yl"), ("yh", "c"), None)
    return jax.shard_map(
        per_device,
        mesh=fine,
        in_specs=(spec, spec, P(), P(), P()),
        out_specs=spec,
        check_vma=False,
    )
```

time: 299 us -> 244 us (0.82)
  Pallas kernels: 0 us -> 65.4 us
  other arithmetic: 49.3 us -> 0.9 us
  matrix products: 49.2 us -> 10.9 us
  local copies, waits for them, and re-layouts: 46.5 us -> 14.7 us
    pallas_call x0 -> x12, Pallas kernels: none -> 65.4 us  [the longest x2 28.1 us: unpack(): pl.pallas_call(unpack_kernel, out_shape=BLOCK, in_specs=[VMEM], out_specs...]
    add x2 -> x0, other arithmetic: 43.3 us -> none  [x_blur(): total = total + w[k] * ext[k + 1:k + 17]]
    dot_general x4, matrix products: 44.2 us -> 6.16 us  [y_blur(): return jnp.einsum('xzq,qy->xzy', v, m, precision=HI)]
    reshape x11 -> x0, local copies, waits for them, and re-layouts: 22.9 us -> none  [the longest x3 10.7 us: leave(): block.reshape(16, 8, 8, 8, 16).transpose(1, 3, 0, 2, 4).reshape(64, 16, 128)]
    transpose x2 -> x0, local copies, waits for them, and re-layouts: 13.3 us -> none  [enter(): t = t.reshape(8, 8, 16, 8, 16).transpose(2, 0, 3, 1, 4)]
    ppermute x1, waiting for transfers between devices: 0.01 us -> 12.2 us  [per_device(): got = lax.ppermute(send, ('z', 'c'), Z_FWD)]
    unnamed x8 -> x54, local copies, waits for them, and re-layouts: 0.02 us -> 9.26 us
    ppermute x4, waiting for transfers between devices: 31.6 us -> 23.2 us  [z_blur(): got = lax.ppermute(v, ('z', 'c'), perm)]
  transfers between devices with their start and end apart: 15 -> 15, of which waited for: 8 -> 8; matrix products, arithmetic and copies ran while one was open for 21% -> 2% of each run, Pallas kernels for 0% -> 16%
where the time goes in v2:
time: 244 us; the launch traced here: 243 us
  Pallas kernels  65.4 us (27%)
  starting transfers between devices  61.3 us (25%)
  waiting for transfers between devices  58.1 us (24%)
  blocking collectives  30.9 us (13%)
  local copies, waits for them, and re-layouts  14.7 us (6%)
  matrix products  10.9 us (4%)
    all_to_all x1, blocking collectives, leave(): t = lax.all_to_all(t, SLAB, 0, 0, tiled=True)  30.9 us
    pallas_call x2, Pallas kernels, unpack(): pl.pallas_call(unpack_kernel, out_shape=BLOCK, in_specs=[VMEM], out_specs...  28.1 us
    ppermute x4, waiting for transfers between devices, z_blur(): got = lax.ppermute(v, ('z', 'c'), perm)  23.2 us
    ppermute x4, starting transfers between devices, x_blur(): passed = lax.ppermute(v, SLAB, NEXT)  19.5 us
    all_to_all x2, starting transfers between devices, enter(): t = lax.all_to_all(t, SLAB, 0, 0, tiled=True)  17.7 us
    all_to_all x2, waiting for transfers between devices, enter(): t = lax.all_to_all(t, SLAB, 0, 0, tiled=True)  15.5 us
    pallas_call x1, Pallas kernels, pack(): pl.pallas_call(pack_kernel, out_shape=jax.ShapeDtypeStruct((1024, 128), j...  14.2 us
    ppermute x4, starting transfers between devices, z_blur(): got = lax.ppermute(v, ('z', 'c'), perm)  12.4 us
  transfers between devices with their start and end apart: 15, of which 8 were waited for; matrix products, arithmetic and copies ran while one was open for 2% of the time, Pallas kernels for 16%

profile of v2, /device:TPU:1, one launch (start us, length us, event | category | flops | bytes accessed | tf_op | source)
XLA Modules:
  0.0 242.5 jit_solution(17282989621062725687)
XLA Ops:
  2.1 11.8 %all-to-all-start = ((f32[64,16,128]{2,1,0:T(8,128)}), f32[64,16,128]{2,1,0:T(8,128)S(1)}, u32[]{:S(2)}, u32[]{:S(2)}) async-start(f32[64,16,128]{2,1,0:T(8,128)} %bitcast.4), calls=%async_computation | async-start | bytes 1048576 | tf_op jit(solution)/shard_map/all_to_all | solution.py:83
  16.0 15.5 %all-to-all-done = f32[64,16,128]{2,1,0:T(8,128)S(1)} async-done(((f32[64,16,128]{2,1,0:T(8,128)}), f32[64,16,128]{2,1,0:T(8,128)S(1)}, u32[]{:S(2)}, u32[]{:S(2)}) %all-to-all-start) | async-done | bytes 524320 | tf_op jit(solution)/shard_map/all_to_all | solution.py:83
  32.3 5.9 %all-to-all-start.1 = ((f32[64,16,128]{2,1,0:T(8,128)}), f32[64,16,128]{2,1,0:T(8,128)S(1)}, u32[]{:S(2)}, u32[]{:S(2)}) async-start(f32[64,16,128]{2,1,0:T(8,128)} %bitcast.17), calls=%async_computation.1 | async-start | bytes 1048576 | tf_op jit(solution)/shard_map/all_to_all | solution.py:83
  41.5 14.1 %unpack.2 = f32[16,64,128]{2,1,0:T(8,128)} custom-call(f32[1024,128]{1,0:T(8,128)} %bitcast.86), custom_call_target="tpu_custom_call" | custom-call | flops 1000000 | bytes 3000000 | tf_op jit(solution)/shard_map/unpack/pallas_call | solution.py:64
  57.2 3.5 %collective-permute-start.1 = (f32[16,64,128]{2,1,0:T(8,128)S(1)}, f32[16,64,128]{2,1,0:T(8,128)S(1)}, u32[]{:S(2)}, u32[]{:S(2)}) collective-permute-start(f32[16,64,128]{2,1,0:T(8,128)S(1)} %convolution_bitcast_fusion.own_ref), channel_id=1, source_target_pairs={{8,1},{2,9},{10,3},{4,11},{12,5},{6,13},{14,7},{16,15},{24,17},{18... | collective-permute-start | bytes 1572872 | tf_op jit(solution)/shard_map/ppermute | solution.py:151
  62.7 2.5 %x_own.4.part_ref = f32[16,64,128]{2,1,0:T(8,128)} custom-call(f32[31]{0:T(128)} %psf_ref.15, f32[16,64,128]{2,1,0:T(8,128)} %copy-done.6), custom_call_target="tpu_custom_call" | custom-call | flops 1000000 | bytes 3000000 | tf_op jit(solution)/shard_map/x_own/pallas_call | solution.py:152
  66.0 14.0 %unpack.3 = f32[16,64,128]{2,1,0:T(8,128)} custom-call(f32[1024,128]{1,0:T(8,128)} %bitcast.87), custom_call_target="tpu_custom_call" | custom-call | flops 1000000 | bytes 3000000 | tf_op jit(solution)/shard_map/unpack/pallas_call | solution.py:64
  81.6 2.9 %x_rest.4 = f32[16,64,128]{2,1,0:T(8,128)} custom-call(f32[31]{0:T(128)} %psf_ref.15, s32[1]{0:T(128)} %bitcast.6.core_ref, f32[16,64,128]{2,1,0:T(8,128)} %x_own.4.part_ref, f32[16,64,128]{2,1,0:T(8,128)} %copy-done.10, f32[16,64,128]{2,1,0:T(8,128)} %copy-done.11), custom_call_target="tpu_custom_call" | custom-call | flops 1000000 | bytes 3000000 | tf_op jit(solution)/shard_map/x_rest/pallas_call | solution.py:160
  84.5 4.0 %collective-permute-start.3 = (f32[16,64,128]{2,1,0:T(8,128)}, f32[16,64,128]{2,1,0:T(8,128)S(1)}, u32[]{:S(2)}, u32[]{:S(2)}) collective-permute-start(f32[16,64,128]{2,1,0:T(8,128)} %x_rest.4), channel_id=1, source_target_pairs={{64,0},{128,64},{192,128},{256,192},{320,256},{384,320},{448,384},... | collective-permute-start | bytes 1572872 | tf_op jit(solution)/shard_map/ppermute | solution.py:222
  88.6 4.0 %collective-permute-start = (f32[16,32,128]{2,1,0:T(8,128)S(1)}, f32[16,32,128]{2,1,0:T(8,128)S(1)}, u32[]{:S(2)}, u32[]{:S(2)}) collective-permute-start(f32[16,32,128]{2,1,0:T(8,128)S(1)} %slice_select_fusion), channel_id=1, source_target_pairs={{64,0},{128,64},{192,128},{256,192},{320,256},{384,320},{448,384},... | collective-permute-start | bytes 786440 | tf_op jit(solution)/shard_map/ppermute | solution.py:239
  92.6 12.2 %collective-permute-done = f32[16,32,128]{2,1,0:T(8,128)S(1)} collective-permute-done((f32[16,32,128]{2,1,0:T(8,128)S(1)}, f32[16,32,128]{2,1,0:T(8,128)S(1)}, u32[]{:S(2)}, u32[]{:S(2)}) %collective-permute-start) | collective-permute-done | bytes 262176 | tf_op jit(solution)/shard_map/ppermute | solution.py:239
  106.5 3.7 %collective-permute-start.4 = (f32[16,64,128]{2,1,0:T(8,128)S(1)}, f32[16,64,128]{2,1,0:T(8,128)S(1)}, u32[]{:S(2)}, u32[]{:S(2)}) collective-permute-start(f32[16,64,128]{2,1,0:T(8,128)S(1)} %fusion.5), channel_id=1, source_target_pairs={{0,64},{64,128},{128,192},{192,256},{256,320},{320,384},{384,448},... | collective-permute-start | bytes 1572872 | tf_op jit(solution)/shard_map/ppermute | solution.py:222
  110.2 6.5 %collective-permute-done.4 = f32[16,64,128]{2,1,0:T(8,128)S(1)} collective-permute-done((f32[16,64,128]{2,1,0:T(8,128)S(1)}, f32[16,64,128]{2,1,0:T(8,128)S(1)}, u32[]{:S(2)}, u32[]{:S(2)}) %collective-permute-start.4) | collective-permute-done | bytes 524320 | tf_op jit(solution)/shard_map/ppermute | solution.py:222
  118.1 6.4 %collective-permute-start.5 = (f32[16,64,128]{2,1,0:T(8,128)S(1)}, f32[16,64,128]{2,1,0:T(8,128)S(1)}, u32[]{:S(2)}, u32[]{:S(2)}) collective-permute-start(f32[16,64,128]{2,1,0:T(8,128)S(1)} %fusion.3.own_ref), channel_id=1, source_target_pairs={{8,1},{2,9},{10,3},{4,11},{12,5},{6,13},{14,7},{16,15},{24,17},{18... | collective-permute-start | bytes 1572872 | tf_op jit(solution)/shard_map/ppermute | solution.py:151
  126.5 2.5 %x_own.5.part_ref = f32[16,64,128]{2,1,0:T(8,128)} custom-call(f32[31]{0:T(128)} %psf_ref.15, f32[16,64,128]{2,1,0:T(8,128)} %copy-done.3), custom_call_target="tpu_custom_call" | custom-call | flops 1000000 | bytes 3000000 | tf_op jit(solution)/shard_map/x_own/pallas_call | solution.py:152
  129.0 2.4 collective-permute-done.5.passed_ref
  133.0 2.9 %x_rest.5 = f32[16,64,128]{2,1,0:T(8,128)} custom-call(f32[31]{0:T(128)} %psf_ref.15, s32[1]{0:T(128)} %bitcast.6.core_ref, f32[16,64,128]{2,1,0:T(8,128)} %x_own.5.part_ref, f32[16,64,128]{2,1,0:T(8,128)} %copy-done.14, f32[16,64,128]{2,1,0:T(8,128)} %copy-done.17), custom_call_target="tpu_custom_call" | custom-call | flops 1000000 | bytes 3000000 | tf_op jit(solution)/shard_map/x_rest/pallas_call | solution.py:160
  138.0 3.7 %collective-permute-start.7 = (f32[16,64,128]{2,1,0:T(8,128)S(1)}, f32[16,64,128]{2,1,0:T(8,128)S(1)}, u32[]{:S(2)}, u32[]{:S(2)}) collective-permute-start(f32[16,64,128]{2,1,0:T(8,128)S(1)} %fusion.8.own_ref), channel_id=1, source_target_pairs={{8,1},{2,9},{10,3},{4,11},{12,5},{6,13},{14,7},{16,15},{24,17},{18... | collective-permute-start | bytes 1572872 | tf_op jit(solution)/shard_map/ppermute | solution.py:151
  143.6 2.5 %x_own.6.part_ref = f32[16,64,128]{2,1,0:T(8,128)} custom-call(f32[31]{0:T(128)} %psf_ref.15, f32[16,64,128]{2,1,0:T(8,128)} %copy-done.7), custom_call_target="tpu_custom_call" | custom-call | flops 1000000 | bytes 3000000 | tf_op jit(solution)/shard_map/x_own/pallas_call | solution.py:152
  146.2 2.4 collective-permute-done.7.passed_ref
  150.2 2.8 %x_rest.6 = f32[16,64,128]{2,1,0:T(8,128)} custom-call(f32[31]{0:T(128)} %psf_ref.15, s32[1]{0:T(128)} %bitcast.6.core_ref, f32[16,64,128]{2,1,0:T(8,128)} %x_own.6.part_ref, f32[16,64,128]{2,1,0:T(8,128)} %copy-done.15, f32[16,64,128]{2,1,0:T(8,128)} %copy-done.18), custom_call_target="tpu_custom_call" | custom-call | flops 1000000 | bytes 3000000 | tf_op jit(solution)/shard_map/x_rest/pallas_call | solution.py:160
  153.0 2.2 collective-permute-start.9
  155.2 9.2 %collective-permute-done.9 = f32[16,64,128]{2,1,0:T(8,128)S(1)} collective-permute-done((f32[16,64,128]{2,1,0:T(8,128)}, f32[16,64,128]{2,1,0:T(8,128)S(1)}, u32[]{:S(2)}, u32[]{:S(2)}) %collective-permute-start.9) | collective-permute-done | bytes 524320 | tf_op jit(solution)/shard_map/ppermute | solution.py:222
  165.7 2.5 %collective-permute-start.10 = (f32[16,64,128]{2,1,0:T(8,128)S(1)}, f32[16,64,128]{2,1,0:T(8,128)S(1)}, u32[]{:S(2)}, u32[]{:S(2)}) collective-permute-start(f32[16,64,128]{2,1,0:T(8,128)S(1)} %fusion.2), channel_id=1, source_target_pairs={{0,64},{64,128},{128,192},{192,256},{256,320},{320,384},{384,448},... | collective-permute-start | bytes 1572872 | tf_op jit(solution)/shard_map/ppermute | solution.py:222
  168.2 7.4 %collective-permute-done.10 = f32[16,64,128]{2,1,0:T(8,128)S(1)} collective-permute-done((f32[16,64,128]{2,1,0:T(8,128)S(1)}, f32[16,64,128]{2,1,0:T(8,128)S(1)}, u32[]{:S(2)}, u32[]{:S(2)}) %collective-permute-start.10) | collective-permute-done | bytes 524320 | tf_op jit(solution)/shard_map/ppermute | solution.py:222
  176.8 5.9 %collective-permute-start.11 = (f32[16,64,128]{2,1,0:T(8,128)S(1)}, f32[16,64,128]{2,1,0:T(8,128)S(1)}, u32[]{:S(2)}, u32[]{:S(2)}) collective-permute-start(f32[16,64,128]{2,1,0:T(8,128)S(1)} %fusion.own_ref), channel_id=1, source_target_pairs={{8,1},{2,9},{10,3},{4,11},{12,5},{6,13},{14,7},{16,15},{24,17},{18... | collective-permute-start | bytes 1572872 | tf_op jit(solution)/shard_map/ppermute | solution.py:151
  184.7 2.5 %x_own.7.part_ref = f32[16,64,128]{2,1,0:T(8,128)} custom-call(f32[31]{0:T(128)} %psf_ref.15, f32[16,64,128]{2,1,0:T(8,128)} %copy-done.2), custom_call_target="tpu_custom_call" | custom-call | flops 1000000 | bytes 3000000 | tf_op jit(solution)/shard_map/x_own/pallas_call | solution.py:152
  187.2 2.4 collective-permute-done.11.passed_ref
  191.2 2.8 %x_rest.7 = f32[16,64,128]{2,1,0:T(8,128)} custom-call(f32[31]{0:T(128)} %psf_ref.15, s32[1]{0:T(128)} %bitcast.6.core_ref, f32[16,64,128]{2,1,0:T(8,128)} %x_own.7.part_ref, f32[16,64,128]{2,1,0:T(8,128)} %copy-done.13, f32[16,64,128]{2,1,0:T(8,128)} %copy-done.16), custom_call_target="tpu_custom_call" | custom-call | flops 1000000 | bytes 3000000 | tf_op jit(solution)/shard_map/x_rest/pallas_call | solution.py:160
  194.0 2.4 convolution_multiply_fusion.in_ref
  196.4 14.2 %pack.1 = f32[1024,128]{1,0:T(8,128)} custom-call(f32[16,64,128]{2,1,0:T(8,128)} %convolution_multiply_fusion.in_ref), custom_call_target="tpu_custom_call" | custom-call | flops 1000000 | bytes 3000000 | tf_op jit(solution)/shard_map/pack/pallas_call | solution.py:70
  210.6 30.9 %all_to_all.15 = f32[64,16,128]{2,1,0:T(8,128)S(1)} all-to-all(f32[64,16,128]{2,1,0:T(8,128)} %bitcast.88), channel_id=1, replica_groups=mesh['z'=8,'x'=4,'yl'=2,'yh'=4,'c'=2] {'x','yl','yh','c'}, dimensions={0} | all-to-all | bytes 1048576 | tf_op jit(solution)/shard_map/all_to_all | solution.py:89
  (99 shorter events, 33.5 us)
Async XLA Ops:
  2.1 11.8 %copy-start.24 = (f32[31]{0:T(128)S(1)}, f32[31]{0:T(128)}, u32[]{:S(2)}) copy-start(f32[31]{0:T(128)} %param.7) | copy-start | bytes 376
  2.1 12.7 %copy-start.8 = (f32[8,16,1024]{2,1,0:T(8,128)S(1)}, f32[8,16,1024]{2,1,0:T(8,128)}, u32[]{:S(2)}) copy-start(f32[8,16,1024]{2,1,0:T(8,128)} %param.5) | copy-start | bytes 1572868
  2.1 29.5 %all-to-all-start = ((f32[64,16,128]{2,1,0:T(8,128)}), f32[64,16,128]{2,1,0:T(8,128)S(1)}, u32[]{:S(2)}, u32[]{:S(2)}) async-start(f32[64,16,128]{2,1,0:T(8,128)} %bitcast.4), calls=%async_computation | async-start | bytes 1048576 | tf_op jit(solution)/shard_map/all_to_all | solution.py:83
  32.3 32.9 %all-to-all-start.1 = ((f32[64,16,128]{2,1,0:T(8,128)}), f32[64,16,128]{2,1,0:T(8,128)S(1)}, u32[]{:S(2)}, u32[]{:S(2)}) async-start(f32[64,16,128]{2,1,0:T(8,128)} %bitcast.17), calls=%async_computation.1 | async-start | bytes 1048576 | tf_op jit(solution)/shard_map/all_to_all | solution.py:83
  41.5 14.1 %copy-start.20 = (f32[128,128]{1,0:T(8,128)S(1)}, f32[128,128]{1,0:T(8,128)}, u32[]{:S(2)}) copy-start(f32[128,128]{1,0:T(8,128)} %get-tuple-element.13) | copy-start | bytes 196612
  57.2 5.5 %copy-start.6 = (f32[16,64,128]{2,1,0:T(8,128)}, f32[16,64,128]{2,1,0:T(8,128)S(1)}, u32[]{:S(2)}) copy-start(f32[16,64,128]{2,1,0:T(8,128)S(1)} %convolution_bitcast_fusion.own_ref) | copy-start | bytes 1572868
  57.2 22.8 %collective-permute-start.1 = (f32[16,64,128]{2,1,0:T(8,128)S(1)}, f32[16,64,128]{2,1,0:T(8,128)S(1)}, u32[]{:S(2)}, u32[]{:S(2)}) collective-permute-start(f32[16,64,128]{2,1,0:T(8,128)S(1)} %convolution_bitcast_fusion.own_ref), channel_id=1, source_target_pairs={{8,1},{2,9},{10,3},{4,11},{12,5},{6,13},{14,7},{16,15},{24,17},{18... | collective-permute-start | bytes 1572872 | tf_op jit(solution)/shard_map/ppermute | solution.py:151
  60.8 19.3 %collective-permute-start.2 = (f32[16,64,128]{2,1,0:T(8,128)S(1)}, f32[16,64,128]{2,1,0:T(8,128)S(1)}, u32[]{:S(2)}, u32[]{:S(2)}) collective-permute-start(f32[16,64,128]{2,1,0:T(8,128)S(1)} %convolution_bitcast_fusion.own_ref), channel_id=1, source_target_pairs={{0,1},{1,0},{2,3},{3,2},{4,5},{5,4},{6,7},{7,6},{8,9},{9,8},{10,11... | collective-permute-start | bytes 1572872 | tf_op jit(solution)/shard_map/ppermute | solution.py:150
  80.0 8.5 %copy-start.1 = (f32[16,64,128]{2,1,0:T(8,128)S(1)}, f32[16,64,128]{2,1,0:T(8,128)}, u32[]{:S(2)}) copy-start(f32[16,64,128]{2,1,0:T(8,128)} %unpack.3) | copy-start | bytes 1572868
  84.5 20.3 %collective-permute-start.3 = (f32[16,64,128]{2,1,0:T(8,128)}, f32[16,64,128]{2,1,0:T(8,128)S(1)}, u32[]{:S(2)}, u32[]{:S(2)}) collective-permute-start(f32[16,64,128]{2,1,0:T(8,128)} %x_rest.4), channel_id=1, source_target_pairs={{64,0},{128,64},{192,128},{256,192},{320,256},{384,320},{448,384},... | collective-permute-start | bytes 1572872 | tf_op jit(solution)/shard_map/ppermute | solution.py:222
  88.6 16.3 %copy-start.23 = (f32[64,64]{1,0:T(8,128)S(1)}, f32[64,64]{1,0:T(8,128)}, u32[]{:S(2)}) copy-start(f32[64,64]{1,0:T(8,128)} %get-tuple-element.14) | copy-start | bytes 49156
  88.6 16.2 %collective-permute-start = (f32[16,32,128]{2,1,0:T(8,128)S(1)}, f32[16,32,128]{2,1,0:T(8,128)S(1)}, u32[]{:S(2)}, u32[]{:S(2)}) collective-permute-start(f32[16,32,128]{2,1,0:T(8,128)S(1)} %slice_select_fusion), channel_id=1, source_target_pairs={{64,0},{128,64},{192,128},{256,192},{320,256},{384,320},{448,384},... | collective-permute-start | bytes 786440 | tf_op jit(solution)/shard_map/ppermute | solution.py:239
  104.8 1.0 copy-start.9
  104.8 1.0 copy-start.25
  105.9 10.9 %copy-start.22 = (f32[64,64]{1,0:T(8,128)S(1)}, f32[64,64]{1,0:T(8,128)}, u32[]{:S(2)}) copy-start(f32[64,64]{1,0:T(8,128)} %get-tuple-element.15) | copy-start | bytes 49156
  106.5 10.2 %collective-permute-start.4 = (f32[16,64,128]{2,1,0:T(8,128)S(1)}, f32[16,64,128]{2,1,0:T(8,128)S(1)}, u32[]{:S(2)}, u32[]{:S(2)}) collective-permute-start(f32[16,64,128]{2,1,0:T(8,128)S(1)} %fusion.5), channel_id=1, source_target_pairs={{0,64},{64,128},{128,192},{192,256},{256,320},{320,384},{384,448},... | collective-permute-start | bytes 1572872 | tf_op jit(solution)/shard_map/ppermute | solution.py:222
  118.1 8.4 %copy-start.3 = (f32[16,64,128]{2,1,0:T(8,128)}, f32[16,64,128]{2,1,0:T(8,128)S(1)}, u32[]{:S(2)}) copy-start(f32[16,64,128]{2,1,0:T(8,128)S(1)} %fusion.3.own_ref) | copy-start | bytes 1572868
  118.1 13.3 %collective-permute-start.5 = (f32[16,64,128]{2,1,0:T(8,128)S(1)}, f32[16,64,128]{2,1,0:T(8,128)S(1)}, u32[]{:S(2)}, u32[]{:S(2)}) collective-permute-start(f32[16,64,128]{2,1,0:T(8,128)S(1)} %fusion.3.own_ref), channel_id=1, source_target_pairs={{8,1},{2,9},{10,3},{4,11},{12,5},{6,13},{14,7},{16,15},{24,17},{18... | collective-permute-start | bytes 1572872 | tf_op jit(solution)/shard_map/ppermute | solution.py:151
  124.5 6.9 %collective-permute-start.6 = (f32[16,64,128]{2,1,0:T(8,128)S(1)}, f32[16,64,128]{2,1,0:T(8,128)S(1)}, u32[]{:S(2)}, u32[]{:S(2)}) collective-permute-start(f32[16,64,128]{2,1,0:T(8,128)S(1)} %fusion.3.own_ref), channel_id=1, source_target_pairs={{0,1},{1,0},{2,3},{3,2},{4,5},{5,4},{6,7},{7,6},{8,9},{9,8},{10,11... | collective-permute-start | bytes 1572872 | tf_op jit(solution)/shard_map/ppermute | solution.py:150
  129.0 6.8 %copy-start = (f32[16,64,128]{2,1,0:T(8,128)S(1)}, f32[16,64,128]{2,1,0:T(8,128)}, u32[]{:S(2)}) copy-start(f32[16,64,128]{2,1,0:T(8,128)} %unpack.2) | copy-start | bytes 1572868
  129.0 6.8 %copy-start.19 = (f32[128,128]{1,0:T(8,128)S(1)}, f32[128,128]{1,0:T(8,128)}, u32[]{:S(2)}) copy-start(f32[128,128]{1,0:T(8,128)} %get-tuple-element.16) | copy-start | bytes 196612
  138.0 5.6 %copy-start.7 = (f32[16,64,128]{2,1,0:T(8,128)}, f32[16,64,128]{2,1,0:T(8,128)S(1)}, u32[]{:S(2)}) copy-start(f32[16,64,128]{2,1,0:T(8,128)S(1)} %fusion.8.own_ref) | copy-start | bytes 1572868
  138.0 10.5 %collective-permute-start.7 = (f32[16,64,128]{2,1,0:T(8,128)S(1)}, f32[16,64,128]{2,1,0:T(8,128)S(1)}, u32[]{:S(2)}, u32[]{:S(2)}) collective-permute-start(f32[16,64,128]{2,1,0:T(8,128)S(1)} %fusion.8.own_ref), channel_id=1, source_target_pairs={{8,1},{2,9},{10,3},{4,11},{12,5},{6,13},{14,7},{16,15},{24,17},{18... | collective-permute-start | bytes 1572872 | tf_op jit(solution)/shard_map/ppermute | solution.py:151
  141.7 6.9 %collective-permute-start.8 = (f32[16,64,128]{2,1,0:T(8,128)S(1)}, f32[16,64,128]{2,1,0:T(8,128)S(1)}, u32[]{:S(2)}, u32[]{:S(2)}) collective-permute-start(f32[16,64,128]{2,1,0:T(8,128)S(1)} %fusion.8.own_ref), channel_id=1, source_target_pairs={{0,1},{1,0},{2,3},{3,2},{4,5},{5,4},{6,7},{7,6},{8,9},{9,8},{10,11... | collective-permute-start | bytes 1572872 | tf_op jit(solution)/shard_map/ppermute | solution.py:150
  149.3 0.8 copy-start.18
  153.0 12.0 %copy-start.12 = (f32[16,64,128]{2,1,0:T(8,128)S(1)}, f32[16,64,128]{2,1,0:T(8,128)}, u32[]{:S(2)}) copy-start(f32[16,64,128]{2,1,0:T(8,128)} %x_rest.6) | copy-start | bytes 1572868
  153.0 11.5 %collective-permute-start.9 = (f32[16,64,128]{2,1,0:T(8,128)}, f32[16,64,128]{2,1,0:T(8,128)S(1)}, u32[]{:S(2)}, u32[]{:S(2)}) collective-permute-start(f32[16,64,128]{2,1,0:T(8,128)} %x_rest.6), channel_id=1, source_target_pairs={{64,0},{128,64},{192,128},{256,192},{320,256},{384,320},{448,384},... | collective-permute-start | bytes 1572872 | tf_op jit(solution)/shard_map/ppermute | solution.py:222
  165.7 9.9 %collective-permute-start.10 = (f32[16,64,128]{2,1,0:T(8,128)S(1)}, f32[16,64,128]{2,1,0:T(8,128)S(1)}, u32[]{:S(2)}, u32[]{:S(2)}) collective-permute-start(f32[16,64,128]{2,1,0:T(8,128)S(1)} %fusion.2), channel_id=1, source_target_pairs={{0,64},{64,128},{128,192},{192,256},{256,320},{320,384},{384,448},... | collective-permute-start | bytes 1572872 | tf_op jit(solution)/shard_map/ppermute | solution.py:222
  176.8 7.9 %copy-start.2 = (f32[16,64,128]{2,1,0:T(8,128)}, f32[16,64,128]{2,1,0:T(8,128)S(1)}, u32[]{:S(2)}) copy-start(f32[16,64,128]{2,1,0:T(8,128)S(1)} %fusion.own_ref) | copy-start | bytes 1572868
  176.8 12.8 %collective-permute-start.11 = (f32[16,64,128]{2,1,0:T(8,128)S(1)}, f32[16,64,128]{2,1,0:T(8,128)S(1)}, u32[]{:S(2)}, u32[]{:S(2)}) collective-permute-start(f32[16,64,128]{2,1,0:T(8,128)S(1)} %fusion.own_ref), channel_id=1, source_target_pairs={{8,1},{2,9},{10,3},{4,11},{12,5},{6,13},{14,7},{16,15},{24,17},{18... | collective-permute-start | bytes 1572872 | tf_op jit(solution)/shard_map/ppermute | solution.py:151
  182.7 6.9 %collective-permute-start.12 = (f32[16,64,128]{2,1,0:T(8,128)S(1)}, f32[16,64,128]{2,1,0:T(8,128)S(1)}, u32[]{:S(2)}, u32[]{:S(2)}) collective-permute-start(f32[16,64,128]{2,1,0:T(8,128)S(1)} %fusion.own_ref), channel_id=1, source_target_pairs={{0,1},{1,0},{2,3},{3,2},{4,5},{5,4},{6,7},{7,6},{8,9},{9,8},{10,11... | collective-permute-start | bytes 1572872 | tf_op jit(solution)/shard_map/ppermute | solution.py:150
  190.4 0.8 copy-start.16
  (10 other events, 7.8 us)

commit v3 on v2

--- a/solution.py
+++ b/solution.py
@@ -10,7 +10,7 @@
 ITERS = 2
 HI = lax.Precision.HIGHEST
 SLAB = ("x", "yl", "yh", "c")
-BLOCK = jax.ShapeDtypeStruct((16, 64, 128), jnp.float32)
+BLOCK = (16, 64, 128)
 VMEM = pl.BlockSpec(memory_space=pltpu.VMEM)
 SMEM = pl.BlockSpec(memory_space=pltpu.SMEM)
 
@@ -34,47 +34,58 @@
     return pl.CostEstimate(flops=int(us * 1e6), bytes_accessed=int(us * 3e6), transcendentals=0)
 
 
-def swap_groups(tile):
-    row = lax.broadcasted_iota(jnp.int32, (8, 128), 0)
+def swap_groups(tiles):
     group = lax.broadcasted_iota(jnp.int32, (8, 128), 1) // 16
+    tiles = [tiles[0]] + [pltpu.roll(tiles[i], 16 * i, 1) for i in range(1, 8)]
     for b in (1, 2, 4):
-        up = pltpu.roll(pltpu.roll(tile, 8 - b, 0), 16 * b, 1)
-        down = up if b == 4 else pltpu.roll(pltpu.roll(tile, b, 0), 128 - 16 * b, 1)
-        take_up = ((row & b) == 0) & ((group & b) != 0)
-        take_down = ((row & b) != 0) & ((group & b) == 0)
-        tile = jnp.where(take_up, up, jnp.where(take_down, down, tile))
-    return tile
-
-
-def unpack_kernel(in_ref, out_ref):
+        taken = (group & b) != 0
+        tiles = [jnp.where(taken, tiles[(i + b) % 8], tiles[i]) for i in range(8)]
+    return [tiles[0]] + [pltpu.roll(tiles[8 - i], 128 - 16 * i, 1) for i in range(1, 8)]
+
+
+def unpack_kernel(in_ref, out_ref, rows_ref):
+    for zc in range(8):
+        for half in range(2):
+            at = zc * 128 + half * 8
+            tiles = swap_groups([in_ref[at + 16 * i : at + 16 * i + 8, :] for i in range(8)])
+            for i in range(8):
+                rows_ref[at + 16 * i : at + 16 * i + 8, :] = tiles[i]
     for zc in range(8):
         for x in range(16):
-            tile = in_ref[pl.ds(zc * 128 + x, 8, stride=16), :]
-            out_ref[x, zc * 8 : zc * 8 + 8, :] = swap_groups(tile)
-
-
-def pack_kernel(in_ref, out_ref):
+            out_ref[x, zc * 8 : zc * 8 + 8, :] = rows_ref[pl.ds(zc * 128 + x, 8, stride=16), :]
+
+
+def pack_kernel(in_ref, out_ref, rows_ref):
     for zc in range(8):
         for x in range(16):
-            tile = in_ref[x, zc * 8 : zc * 8 + 8, :]
-            out_ref[pl.ds(zc * 128 + x, 8, stride=16), :] = swap_groups(tile)
+            rows_ref[pl.ds(zc * 128 + x, 8, stride=16), :] = in_ref[x, zc * 8 : zc * 8 + 8, :]
+    for zc in range(8):
+        for half in range(2):
+            at = zc * 128 + half * 8
+            tiles = swap_groups([rows_ref[at + 16 * i : at + 16 * i + 8, :] for i in range(8)])
+            for i in range(8):
+                out_ref[at + 16 * i : at + 16 * i + 8, :] = tiles[i]
+
+
+def call(kernel, out, args, us, name, scratch=()):
+    pinned = [a if a.ndim == 1 else pltpu.with_memory_space_constraint(a, pltpu.VMEM) for a in args]
+    return pl.pallas_call(
+        kernel,
+        out_shape=jax.tree.map(lambda s: pltpu.VMEM(s, jnp.float32), out, is_leaf=lambda s: isinstance(s, tuple)),
+        in_specs=[SMEM if a.ndim == 1 else VMEM for a in args],
+        out_specs=jax.tree.map(lambda s: VMEM, out, is_leaf=lambda s: isinstance(s, tuple)),
+        scratch_shapes=[pltpu.VMEM(s, jnp.float32) for s in scratch],
+        cost_estimate=cost(us),
+        name=name,
+    )(*pinned)
 
 
 def unpack(rows):
-    return pl.pallas_call(
-        unpack_kernel, out_shape=BLOCK, in_specs=[VMEM], out_specs=VMEM, cost_estimate=cost(1), name="unpack"
-    )(rows)
+    return call(unpack_kernel, BLOCK, [rows], 1, "unpack", [(1024, 128)])
 
 
 def pack(block):
-    return pl.pallas_call(
-        pack_kernel,
-        out_shape=jax.ShapeDtypeStruct((1024, 128), jnp.float32),
-        in_specs=[VMEM],
-        out_specs=VMEM,
-        cost_estimate=cost(1),
-        name="pack",
-    )(block)
+    return call(pack_kernel, (1024, 128), [block], 1, "pack", [(1024, 128)])
 
 
 def enter(volume):
@@ -149,22 +160,10 @@
 def x_blur(v, psf, core, flip):
     swapped = lax.ppermute(v, "c", SWAP)
     passed = lax.ppermute(v, SLAB, NEXT)
-    part = pl.pallas_call(
-        functools.partial(x_own_kernel, flip),
-        out_shape=BLOCK,
-        in_specs=[SMEM, VMEM],
-        out_specs=VMEM,
-        cost_estimate=cost(1),
-        name="x_own",
-    )(psf, v)
-    return pl.pallas_call(
-        functools.partial(x_rest_kernel, flip),
-        out_shape=BLOCK,
-        in_specs=[SMEM, SMEM, VMEM, VMEM, VMEM],
-        out_specs=VMEM,
-        cost_estimate=cost(1),
-        name="x_rest",
-    )(psf, core, part, passed, swapped)
+    part = call(functools.partial(x_own_kernel, flip), BLOCK, [psf, v], 1.3, "x_own")
+    return call(
+        functools.partial(x_rest_kernel, flip), BLOCK, [psf, core, part, passed, swapped], 1.3, "x_rest"
+    )
 
 
 def prep_kernel(place_ref, lines_ref, yf_ref, ya_ref, fo_ref, fg_ref, ao_ref, ag_ref):
@@ -202,16 +201,8 @@
         [line(psf_y[::-1], -15), line(psf_y, -15), line(psf_z, 1), line(psf_z[::-1], 1)]
     )
     lines = jnp.concatenate([lines, lines], axis=0)
-    square = jax.ShapeDtypeStruct((128, 128), jnp.float32)
-    small = jax.ShapeDtypeStruct((64, 64), jnp.float32)
-    return pl.pallas_call(
-        prep_kernel,
-        out_shape=[square, square, small, small, small, small],
-        in_specs=[SMEM, VMEM],
-        out_specs=[VMEM] * 6,
-        cost_estimate=cost(2),
-        name="prepare",
-    )(jnp.stack([slab, core]), lines)
+    out = [(128, 128)] * 2 + [(64, 64)] * 4
+    return call(prep_kernel, out, [jnp.stack([slab, core]), lines], 2, "prepare")
 
 
 def y_blur(v, m):

time: 244 us -> 192 us (0.79)
  Pallas kernels: 65.4 us -> 14.7 us
  waiting for transfers between devices: 58.1 us -> 70.1 us
  local copies, waits for them, and re-layouts: 14.7 us -> 5.59 us
  matrix products: 10.9 us -> 6.88 us
    pallas_call x12, Pallas kernels: 65.4 us -> 14.7 us  [call(): pl.pallas_call(kernel, out_shape=jax.tree.map(lambda s: pltpu.VMEM(s, jnp...]
    all_to_all x2, waiting for transfers between devices: 15.5 us -> 24.3 us  [enter(): t = lax.all_to_all(t, SLAB, 0, 0, tiled=True)]
    unnamed x54 -> x14, local copies, waits for them, and re-layouts: 9.26 us -> 0.76 us
    dot_general x4, matrix products: 6.16 us -> 2.26 us  [y_blur(): return jnp.einsum('xzq,qy->xzy', v, m, precision=HI)]
    ppermute x4, waiting for transfers between devices: 7.15 us -> 10.5 us  [x_blur(): passed = lax.ppermute(v, SLAB, NEXT)]
  transfers between devices with their start and end apart: 15 -> 15, of which waited for: 8 -> 9; matrix products, arithmetic and copies ran while one was open for 2% -> 2% of each run, Pallas kernels for 16% -> 4%
where the time goes in v3:
time: 192 us; the launch traced here: 191 us
  waiting for transfers between devices  70.1 us (37%)
  starting transfers between devices  61.7 us (32%)
  blocking collectives  31.1 us (16%)
  Pallas kernels  14.7 us (8%)
  matrix products  6.88 us (4%)
  local copies, waits for them, and re-layouts  5.59 us (3%)
    all_to_all x1, blocking collectives, leave(): t = lax.all_to_all(t, SLAB, 0, 0, tiled=True)  31.1 us
    all_to_all x2, waiting for transfers between devices, enter(): t = lax.all_to_all(t, SLAB, 0, 0, tiled=True)  24.3 us
    ppermute x4, waiting for transfers between devices, z_blur(): got = lax.ppermute(v, ('z', 'c'), perm)  23.2 us
    ppermute x4, starting transfers between devices, x_blur(): passed = lax.ppermute(v, SLAB, NEXT)  20.1 us
    all_to_all x2, starting transfers between devices, enter(): t = lax.all_to_all(t, SLAB, 0, 0, tiled=True)  17.7 us
    pallas_call x12, Pallas kernels, call(): pl.pallas_call(kernel, out_shape=jax.tree.map(lambda s: pltpu.VMEM(s, jnp...  14.7 us
    ppermute x4, starting transfers between devices, z_blur(): got = lax.ppermute(v, ('z', 'c'), perm)  12.1 us
    ppermute x1, waiting for transfers between devices, per_device(): got = lax.ppermute(send, ('z', 'c'), Z_FWD)  12 us
  transfers between devices with their start and end apart: 15, of which 9 were waited for; matrix products, arithmetic and copies ran while one was open for 2% of the time, Pallas kernels for 4%

profile of v3, /device:TPU:1, one launch (start us, length us, event | category | flops | bytes accessed | tf_op | source)
XLA Modules:
  0.0 191.3 jit_solution(6006338750035860550)
XLA Ops:
  2.1 11.8 %all-to-all-start = ((f32[64,16,128]{2,1,0:T(8,128)}), f32[64,16,128]{2,1,0:T(8,128)S(1)}, u32[]{:S(2)}, u32[]{:S(2)}) async-start(f32[64,16,128]{2,1,0:T(8,128)} %bitcast.4), calls=%async_computation | async-start | bytes 1048576 | tf_op jit(solution)/shard_map/all_to_all | solution.py:94
  16.0 15.6 %all-to-all-done = f32[64,16,128]{2,1,0:T(8,128)S(1)} async-done(((f32[64,16,128]{2,1,0:T(8,128)}), f32[64,16,128]{2,1,0:T(8,128)S(1)}, u32[]{:S(2)}, u32[]{:S(2)}) %all-to-all-start) | async-done | bytes 524320 | tf_op jit(solution)/shard_map/all_to_all | solution.py:94
  31.5 5.9 %all-to-all-start.1 = ((f32[64,16,128]{2,1,0:T(8,128)}), f32[64,16,128]{2,1,0:T(8,128)S(1)}, u32[]{:S(2)}, u32[]{:S(2)}) async-start(f32[64,16,128]{2,1,0:T(8,128)} %bitcast.17), calls=%async_computation.1 | async-start | bytes 1048576 | tf_op jit(solution)/shard_map/all_to_all | solution.py:94
  40.9 3.5 %collective-permute-start.1 = (f32[16,64,128]{2,1,0:T(8,128)S(1)}, f32[16,64,128]{2,1,0:T(8,128)S(1)}, u32[]{:S(2)}, u32[]{:S(2)}) collective-permute-start(f32[16,64,128]{2,1,0:T(8,128)S(1)} %convolution_bitcast_fusion.own_ref), channel_id=1, source_target_pairs={{8,1},{2,9},{10,3},{4,11},{12,5},{6,13},{14,7},{16,15},{24,17},{18... | collective-permute-start | bytes 1572872 | tf_op jit(solution)/shard_map/ppermute | solution.py:162
  44.4 1.9 %collective-permute-start.2 = (f32[16,64,128]{2,1,0:T(8,128)S(1)}, f32[16,64,128]{2,1,0:T(8,128)}, u32[]{:S(2)}, u32[]{:S(2)}) collective-permute-start(f32[16,64,128]{2,1,0:T(8,128)S(1)} %convolution_bitcast_fusion.own_ref), channel_id=1, source_target_pairs={{0,1},{1,0},{2,3},{3,2},{4,5},{5,4},{6,7},{7,6},{8,9},{9,8},{10,11... | collective-permute-start | bytes 1572872 | tf_op jit(solution)/shard_map/ppermute | solution.py:161
  46.4 8.7 %all-to-all-done.1 = f32[64,16,128]{2,1,0:T(8,128)S(1)} async-done(((f32[64,16,128]{2,1,0:T(8,128)}), f32[64,16,128]{2,1,0:T(8,128)S(1)}, u32[]{:S(2)}, u32[]{:S(2)}) %all-to-all-start.1) | async-done | bytes 524320 | tf_op jit(solution)/shard_map/all_to_all | solution.py:94
  56.0 1.3 x_own.4.part_ref
  57.3 1.7 x_rest.4
  59.1 4.0 %collective-permute-start.3 = (f32[16,64,128]{2,1,0:T(8,128)S(1)}, f32[16,64,128]{2,1,0:T(8,128)S(1)}, u32[]{:S(2)}, u32[]{:S(2)}) collective-permute-start(f32[16,64,128]{2,1,0:T(8,128)S(1)} %x_rest.4), channel_id=1, source_target_pairs={{64,0},{128,64},{192,128},{256,192},{320,256},{384,320},{448,384},... | collective-permute-start | bytes 1572872 | tf_op jit(solution)/shard_map/ppermute | solution.py:213
  63.1 4.0 %collective-permute-start = (f32[16,32,128]{2,1,0:T(8,128)S(1)}, f32[16,32,128]{2,1,0:T(8,128)S(1)}, u32[]{:S(2)}, u32[]{:S(2)}) collective-permute-start(f32[16,32,128]{2,1,0:T(8,128)S(1)} %slice_select_fusion), channel_id=1, source_target_pairs={{64,0},{128,64},{192,128},{256,192},{320,256},{384,320},{448,384},... | collective-permute-start | bytes 786440 | tf_op jit(solution)/shard_map/ppermute | solution.py:230
  67.1 12.0 %collective-permute-done = f32[16,32,128]{2,1,0:T(8,128)S(1)} collective-permute-done((f32[16,32,128]{2,1,0:T(8,128)S(1)}, f32[16,32,128]{2,1,0:T(8,128)S(1)}, u32[]{:S(2)}, u32[]{:S(2)}) %collective-permute-start) | collective-permute-done | bytes 262176 | tf_op jit(solution)/shard_map/ppermute | solution.py:230
  80.6 3.7 %collective-permute-start.4 = (f32[16,64,128]{2,1,0:T(8,128)S(1)}, f32[16,64,128]{2,1,0:T(8,128)S(1)}, u32[]{:S(2)}, u32[]{:S(2)}) collective-permute-start(f32[16,64,128]{2,1,0:T(8,128)S(1)} %fusion.5), channel_id=1, source_target_pairs={{0,64},{64,128},{128,192},{192,256},{256,320},{320,384},{384,448},... | collective-permute-start | bytes 1572872 | tf_op jit(solution)/shard_map/ppermute | solution.py:213
  84.3 6.6 %collective-permute-done.4 = f32[16,64,128]{2,1,0:T(8,128)S(1)} collective-permute-done((f32[16,64,128]{2,1,0:T(8,128)S(1)}, f32[16,64,128]{2,1,0:T(8,128)S(1)}, u32[]{:S(2)}, u32[]{:S(2)}) %collective-permute-start.4) | collective-permute-done | bytes 524320 | tf_op jit(solution)/shard_map/ppermute | solution.py:213
  92.0 6.9 %collective-permute-start.5 = (f32[16,64,128]{2,1,0:T(8,128)S(1)}, f32[16,64,128]{2,1,0:T(8,128)S(1)}, u32[]{:S(2)}, u32[]{:S(2)}) collective-permute-start(f32[16,64,128]{2,1,0:T(8,128)S(1)} %fusion.3.own_ref), channel_id=1, source_target_pairs={{8,1},{2,9},{10,3},{4,11},{12,5},{6,13},{14,7},{16,15},{24,17},{18... | collective-permute-start | bytes 1572872 | tf_op jit(solution)/shard_map/ppermute | solution.py:162
  98.9 1.9 %collective-permute-start.6 = (f32[16,64,128]{2,1,0:T(8,128)S(1)}, f32[16,64,128]{2,1,0:T(8,128)S(1)}, u32[]{:S(2)}, u32[]{:S(2)}) collective-permute-start(f32[16,64,128]{2,1,0:T(8,128)S(1)} %fusion.3.own_ref), channel_id=1, source_target_pairs={{0,1},{1,0},{2,3},{3,2},{4,5},{5,4},{6,7},{7,6},{8,9},{9,8},{10,11... | collective-permute-start | bytes 1572872 | tf_op jit(solution)/shard_map/ppermute | solution.py:161
  100.8 1.3 x_own.5.part_ref
  102.2 3.6 %collective-permute-done.5.passed_ref = f32[16,64,128]{2,1,0:T(8,128)S(1)} collective-permute-done((f32[16,64,128]{2,1,0:T(8,128)S(1)}, f32[16,64,128]{2,1,0:T(8,128)S(1)}, u32[]{:S(2)}, u32[]{:S(2)}) %collective-permute-start.5) | collective-permute-done | bytes 524320 | tf_op jit(solution)/shard_map/ppermute | solution.py:162
  105.8 1.3 x_rest.5
  108.3 3.6 %collective-permute-start.7 = (f32[16,64,128]{2,1,0:T(8,128)S(1)}, f32[16,64,128]{2,1,0:T(8,128)S(1)}, u32[]{:S(2)}, u32[]{:S(2)}) collective-permute-start(f32[16,64,128]{2,1,0:T(8,128)S(1)} %fusion.8.own_ref), channel_id=1, source_target_pairs={{8,1},{2,9},{10,3},{4,11},{12,5},{6,13},{14,7},{16,15},{24,17},{18... | collective-permute-start | bytes 1572872 | tf_op jit(solution)/shard_map/ppermute | solution.py:162
  111.9 1.9 %collective-permute-start.8 = (f32[16,64,128]{2,1,0:T(8,128)S(1)}, f32[16,64,128]{2,1,0:T(8,128)S(1)}, u32[]{:S(2)}, u32[]{:S(2)}) collective-permute-start(f32[16,64,128]{2,1,0:T(8,128)S(1)} %fusion.8.own_ref), channel_id=1, source_target_pairs={{0,1},{1,0},{2,3},{3,2},{4,5},{5,4},{6,7},{7,6},{8,9},{9,8},{10,11... | collective-permute-start | bytes 1572872 | tf_op jit(solution)/shard_map/ppermute | solution.py:161
  113.8 1.3 x_own.6.part_ref
  115.2 3.6 %collective-permute-done.7.passed_ref = f32[16,64,128]{2,1,0:T(8,128)S(1)} collective-permute-done((f32[16,64,128]{2,1,0:T(8,128)S(1)}, f32[16,64,128]{2,1,0:T(8,128)S(1)}, u32[]{:S(2)}, u32[]{:S(2)}) %collective-permute-start.7) | collective-permute-done | bytes 524320 | tf_op jit(solution)/shard_map/ppermute | solution.py:162
  120.1 2.1 %collective-permute-start.9 = (f32[16,64,128]{2,1,0:T(8,128)S(1)}, f32[16,64,128]{2,1,0:T(8,128)S(1)}, u32[]{:S(2)}, u32[]{:S(2)}) collective-permute-start(f32[16,64,128]{2,1,0:T(8,128)S(1)} %x_rest.6), channel_id=1, source_target_pairs={{64,0},{128,64},{192,128},{256,192},{320,256},{384,320},{448,384},... | collective-permute-start | bytes 1572872 | tf_op jit(solution)/shard_map/ppermute | solution.py:213
  122.2 9.2 %collective-permute-done.9 = f32[16,64,128]{2,1,0:T(8,128)S(1)} collective-permute-done((f32[16,64,128]{2,1,0:T(8,128)S(1)}, f32[16,64,128]{2,1,0:T(8,128)S(1)}, u32[]{:S(2)}, u32[]{:S(2)}) %collective-permute-start.9) | collective-permute-done | bytes 524320 | tf_op jit(solution)/shard_map/ppermute | solution.py:213
  132.6 2.4 %collective-permute-start.10 = (f32[16,64,128]{2,1,0:T(8,128)S(1)}, f32[16,64,128]{2,1,0:T(8,128)S(1)}, u32[]{:S(2)}, u32[]{:S(2)}) collective-permute-start(f32[16,64,128]{2,1,0:T(8,128)S(1)} %fusion.2), channel_id=1, source_target_pairs={{0,64},{64,128},{128,192},{192,256},{256,320},{320,384},{384,448},... | collective-permute-start | bytes 1572872 | tf_op jit(solution)/shard_map/ppermute | solution.py:213
  135.1 7.5 %collective-permute-done.10 = f32[16,64,128]{2,1,0:T(8,128)S(1)} collective-permute-done((f32[16,64,128]{2,1,0:T(8,128)S(1)}, f32[16,64,128]{2,1,0:T(8,128)S(1)}, u32[]{:S(2)}, u32[]{:S(2)}) %collective-permute-start.10) | collective-permute-done | bytes 524320 | tf_op jit(solution)/shard_map/ppermute | solution.py:213
  143.7 6.0 %collective-permute-start.11 = (f32[16,64,128]{2,1,0:T(8,128)S(1)}, f32[16,64,128]{2,1,0:T(8,128)S(1)}, u32[]{:S(2)}, u32[]{:S(2)}) collective-permute-start(f32[16,64,128]{2,1,0:T(8,128)S(1)} %fusion.own_ref), channel_id=1, source_target_pairs={{8,1},{2,9},{10,3},{4,11},{12,5},{6,13},{14,7},{16,15},{24,17},{18... | collective-permute-start | bytes 1572872 | tf_op jit(solution)/shard_map/ppermute | solution.py:162
  149.7 2.1 %collective-permute-start.12 = (f32[16,64,128]{2,1,0:T(8,128)S(1)}, f32[16,64,128]{2,1,0:T(8,128)S(1)}, u32[]{:S(2)}, u32[]{:S(2)}) collective-permute-start(f32[16,64,128]{2,1,0:T(8,128)S(1)} %fusion.own_ref), channel_id=1, source_target_pairs={{0,1},{1,0},{2,3},{3,2},{4,5},{5,4},{6,7},{7,6},{8,9},{9,8},{10,11... | collective-permute-start | bytes 1572872 | tf_op jit(solution)/shard_map/ppermute | solution.py:161
  151.8 1.3 x_own.7.part_ref
  153.1 3.4 %collective-permute-done.11.passed_ref = f32[16,64,128]{2,1,0:T(8,128)S(1)} collective-permute-done((f32[16,64,128]{2,1,0:T(8,128)S(1)}, f32[16,64,128]{2,1,0:T(8,128)S(1)}, u32[]{:S(2)}, u32[]{:S(2)}) %collective-permute-start.11) | collective-permute-done | bytes 524320 | tf_op jit(solution)/shard_map/ppermute | solution.py:162
  156.5 1.3 x_rest.7
  159.3 31.1 %all_to_all.15 = f32[64,16,128]{2,1,0:T(8,128)S(1)} all-to-all(f32[64,16,128]{2,1,0:T(8,128)S(1)} %bitcast.88), channel_id=1, replica_groups=mesh['z'=8,'x'=4,'yl'=2,'yh'=4,'c'=2] {'x','yl','yh','c'}, dimensions={0} | all-to-all | bytes 1048576 | tf_op jit(solution)/shard_map/all_to_all | solution.py:100
  (59 shorter events, 18.3 us)
Async XLA Ops:
  2.1 11.8 %copy-start.5 = (f32[31]{0:T(128)S(1)}, f32[31]{0:T(128)}, u32[]{:S(2)}) copy-start(f32[31]{0:T(128)} %param.7) | copy-start | bytes 376
  2.1 12.7 %copy-start = (f32[8,16,1024]{2,1,0:T(8,128)S(1)}, f32[8,16,1024]{2,1,0:T(8,128)}, u32[]{:S(2)}) copy-start(f32[8,16,1024]{2,1,0:T(8,128)} %param.5) | copy-start | bytes 1572868
  2.1 29.5 %all-to-all-start = ((f32[64,16,128]{2,1,0:T(8,128)}), f32[64,16,128]{2,1,0:T(8,128)S(1)}, u32[]{:S(2)}, u32[]{:S(2)}) async-start(f32[64,16,128]{2,1,0:T(8,128)} %bitcast.4), calls=%async_computation | async-start | bytes 1048576 | tf_op jit(solution)/shard_map/all_to_all | solution.py:94
  14.0 0.7 copy-start.6
  31.5 23.6 %all-to-all-start.1 = ((f32[64,16,128]{2,1,0:T(8,128)}), f32[64,16,128]{2,1,0:T(8,128)S(1)}, u32[]{:S(2)}, u32[]{:S(2)}) async-start(f32[64,16,128]{2,1,0:T(8,128)} %bitcast.17), calls=%async_computation.1 | async-start | bytes 1048576 | tf_op jit(solution)/shard_map/all_to_all | solution.py:94
  40.9 16.4 %collective-permute-start.1 = (f32[16,64,128]{2,1,0:T(8,128)S(1)}, f32[16,64,128]{2,1,0:T(8,128)S(1)}, u32[]{:S(2)}, u32[]{:S(2)}) collective-permute-start(f32[16,64,128]{2,1,0:T(8,128)S(1)} %convolution_bitcast_fusion.own_ref), channel_id=1, source_target_pairs={{8,1},{2,9},{10,3},{4,11},{12,5},{6,13},{14,7},{16,15},{24,17},{18... | collective-permute-start | bytes 1572872 | tf_op jit(solution)/shard_map/ppermute | solution.py:162
  44.4 12.9 %collective-permute-start.2 = (f32[16,64,128]{2,1,0:T(8,128)S(1)}, f32[16,64,128]{2,1,0:T(8,128)}, u32[]{:S(2)}, u32[]{:S(2)}) collective-permute-start(f32[16,64,128]{2,1,0:T(8,128)S(1)} %convolution_bitcast_fusion.own_ref), channel_id=1, source_target_pairs={{0,1},{1,0},{2,3},{3,2},{4,5},{5,4},{6,7},{7,6},{8,9},{9,8},{10,11... | collective-permute-start | bytes 1572872 | tf_op jit(solution)/shard_map/ppermute | solution.py:161
  59.1 20.1 %collective-permute-start.3 = (f32[16,64,128]{2,1,0:T(8,128)S(1)}, f32[16,64,128]{2,1,0:T(8,128)S(1)}, u32[]{:S(2)}, u32[]{:S(2)}) collective-permute-start(f32[16,64,128]{2,1,0:T(8,128)S(1)} %x_rest.4), channel_id=1, source_target_pairs={{64,0},{128,64},{192,128},{256,192},{320,256},{384,320},{448,384},... | collective-permute-start | bytes 1572872 | tf_op jit(solution)/shard_map/ppermute | solution.py:213
  63.1 16.0 %collective-permute-start = (f32[16,32,128]{2,1,0:T(8,128)S(1)}, f32[16,32,128]{2,1,0:T(8,128)S(1)}, u32[]{:S(2)}, u32[]{:S(2)}) collective-permute-start(f32[16,32,128]{2,1,0:T(8,128)S(1)} %slice_select_fusion), channel_id=1, source_target_pairs={{64,0},{128,64},{192,128},{256,192},{320,256},{384,320},{448,384},... | collective-permute-start | bytes 786440 | tf_op jit(solution)/shard_map/ppermute | solution.py:230
  79.2 0.7 copy-start.1
  79.2 0.8 copy-start.3
  80.6 10.2 %collective-permute-start.4 = (f32[16,64,128]{2,1,0:T(8,128)S(1)}, f32[16,64,128]{2,1,0:T(8,128)S(1)}, u32[]{:S(2)}, u32[]{:S(2)}) collective-permute-start(f32[16,64,128]{2,1,0:T(8,128)S(1)} %fusion.5), channel_id=1, source_target_pairs={{0,64},{64,128},{128,192},{192,256},{256,320},{320,384},{384,448},... | collective-permute-start | bytes 1572872 | tf_op jit(solution)/shard_map/ppermute | solution.py:213
  92.0 13.8 %collective-permute-start.5 = (f32[16,64,128]{2,1,0:T(8,128)S(1)}, f32[16,64,128]{2,1,0:T(8,128)S(1)}, u32[]{:S(2)}, u32[]{:S(2)}) collective-permute-start(f32[16,64,128]{2,1,0:T(8,128)S(1)} %fusion.3.own_ref), channel_id=1, source_target_pairs={{8,1},{2,9},{10,3},{4,11},{12,5},{6,13},{14,7},{16,15},{24,17},{18... | collective-permute-start | bytes 1572872 | tf_op jit(solution)/shard_map/ppermute | solution.py:162
  98.9 6.9 %collective-permute-start.6 = (f32[16,64,128]{2,1,0:T(8,128)S(1)}, f32[16,64,128]{2,1,0:T(8,128)S(1)}, u32[]{:S(2)}, u32[]{:S(2)}) collective-permute-start(f32[16,64,128]{2,1,0:T(8,128)S(1)} %fusion.3.own_ref), channel_id=1, source_target_pairs={{0,1},{1,0},{2,3},{3,2},{4,5},{5,4},{6,7},{7,6},{8,9},{9,8},{10,11... | collective-permute-start | bytes 1572872 | tf_op jit(solution)/shard_map/ppermute | solution.py:161
  108.3 10.5 %collective-permute-start.7 = (f32[16,64,128]{2,1,0:T(8,128)S(1)}, f32[16,64,128]{2,1,0:T(8,128)S(1)}, u32[]{:S(2)}, u32[]{:S(2)}) collective-permute-start(f32[16,64,128]{2,1,0:T(8,128)S(1)} %fusion.8.own_ref), channel_id=1, source_target_pairs={{8,1},{2,9},{10,3},{4,11},{12,5},{6,13},{14,7},{16,15},{24,17},{18... | collective-permute-start | bytes 1572872 | tf_op jit(solution)/shard_map/ppermute | solution.py:162
  111.9 6.9 %collective-permute-start.8 = (f32[16,64,128]{2,1,0:T(8,128)S(1)}, f32[16,64,128]{2,1,0:T(8,128)S(1)}, u32[]{:S(2)}, u32[]{:S(2)}) collective-permute-start(f32[16,64,128]{2,1,0:T(8,128)S(1)} %fusion.8.own_ref), channel_id=1, source_target_pairs={{0,1},{1,0},{2,3},{3,2},{4,5},{5,4},{6,7},{7,6},{8,9},{9,8},{10,11... | collective-permute-start | bytes 1572872 | tf_op jit(solution)/shard_map/ppermute | solution.py:161
  120.1 11.9 %copy-start.2 = (f32[16,32,128]{2,1,0:T(8,128)S(1)}, f32[16,32,128]{2,1,0:T(8,128)}, u32[]{:S(2)}) copy-start(f32[16,32,128]{2,1,0:T(8,128)} %copy-done.1) | copy-start | bytes 786436
  120.1 11.9 %copy-start.4 = (f32[16,32,128]{2,1,0:T(8,128)S(1)}, f32[16,32,128]{2,1,0:T(8,128)}, u32[]{:S(2)}) copy-start(f32[16,32,128]{2,1,0:T(8,128)} %copy-done.3) | copy-start | bytes 786436
  120.1 11.3 %collective-permute-start.9 = (f32[16,64,128]{2,1,0:T(8,128)S(1)}, f32[16,64,128]{2,1,0:T(8,128)S(1)}, u32[]{:S(2)}, u32[]{:S(2)}) collective-permute-start(f32[16,64,128]{2,1,0:T(8,128)S(1)} %x_rest.6), channel_id=1, source_target_pairs={{64,0},{128,64},{192,128},{256,192},{320,256},{384,320},{448,384},... | collective-permute-start | bytes 1572872 | tf_op jit(solution)/shard_map/ppermute | solution.py:213
  132.6 9.9 %collective-permute-start.10 = (f32[16,64,128]{2,1,0:T(8,128)S(1)}, f32[16,64,128]{2,1,0:T(8,128)S(1)}, u32[]{:S(2)}, u32[]{:S(2)}) collective-permute-start(f32[16,64,128]{2,1,0:T(8,128)S(1)} %fusion.2), channel_id=1, source_target_pairs={{0,64},{64,128},{128,192},{192,256},{256,320},{320,384},{384,448},... | collective-permute-start | bytes 1572872 | tf_op jit(solution)/shard_map/ppermute | solution.py:213
  143.7 12.8 %collective-permute-start.11 = (f32[16,64,128]{2,1,0:T(8,128)S(1)}, f32[16,64,128]{2,1,0:T(8,128)S(1)}, u32[]{:S(2)}, u32[]{:S(2)}) collective-permute-start(f32[16,64,128]{2,1,0:T(8,128)S(1)} %fusion.own_ref), channel_id=1, source_target_pairs={{8,1},{2,9},{10,3},{4,11},{12,5},{6,13},{14,7},{16,15},{24,17},{18... | collective-permute-start | bytes 1572872 | tf_op jit(solution)/shard_map/ppermute | solution.py:162
  149.7 6.9 %collective-permute-start.12 = (f32[16,64,128]{2,1,0:T(8,128)S(1)}, f32[16,64,128]{2,1,0:T(8,128)S(1)}, u32[]{:S(2)}, u32[]{:S(2)}) collective-permute-start(f32[16,64,128]{2,1,0:T(8,128)S(1)} %fusion.own_ref), channel_id=1, source_target_pairs={{0,1},{1,0},{2,3},{3,2},{4,5},{5,4},{6,7},{7,6},{8,9},{9,8},{10,11... | collective-permute-start | bytes 1572872 | tf_op jit(solution)/shard_map/ppermute | solution.py:161

commit v4 on v1

v4 whole, which is shorter than its diff:
```python
import functools

import jax
import jax.numpy as jnp
from jax import lax
from jax.experimental import pallas as pl
from jax.experimental.pallas import tpu as pltpu
from jax.sharding import Mesh, PartitionSpec as P

HI = lax.Precision.HIGHEST
SLAB = ("x", "yl", "yh", "c")
BLOCK = (16, 64, 128)
ROWS = (1024, 128)
VMEM = pl.BlockSpec(memory_space=pltpu.VMEM)
SMEM = pl.BlockSpec(memory_space=pltpu.SMEM)


def x_index(b, c):
    x, yh, yl = b // 8, (b % 8) // 2, b % 2
    return ((x * 2 + yl) * 4 + yh) * 2 + c


SWAP = [(0, 1), (1, 0)]
NEXT = [(x_index(b, 0), x_index(b - 1, 1)) for b in range(1, 32)] + [
    (x_index(b, 1), x_index(b + 1, 0)) for b in range(31)
]
UP = [(z, z + 1) for z in range(7)]
DOWN = [(z + 1, z) for z in range(7)]


def is_shape(s):
    return isinstance(s, tuple)


def call(kernel, out, args, us, name, scratch=()):
    pinned = [a if a.ndim == 1 else pltpu.with_memory_space_constraint(a, pltpu.VMEM) for a in args]
    return pl.pallas_call(
        kernel,
        out_shape=jax.tree.map(lambda s: pltpu.VMEM(s, jnp.float32), out, is_leaf=is_shape),
        in_specs=[SMEM if a.ndim == 1 else VMEM for a in args],
        out_specs=jax.tree.map(lambda s: VMEM, out, is_leaf=is_shape),
        scratch_shapes=[pltpu.VMEM(s, jnp.float32) for s in scratch],
        cost_estimate=pl.CostEstimate(
            flops=int(us * 1e6), bytes_accessed=int(us * 3e6), transcendentals=0
        ),
        compiler_params=pltpu.CompilerParams(vmem_limit_bytes=16 * 2**20),
        name=name,
    )(*pinned)


def dot(a, b):
    return jnp.dot(a, b, precision=HI, preferred_element_type=jnp.float32)


def band(psf_ref, lead, flip, rows):
    taps = psf_ref.shape[0]
    lane = lax.broadcasted_iota(jnp.int32, (8, 256), 1)
    line = jnp.zeros((8, 256), jnp.float32)
    total = psf_ref[0]
    for k in range(taps):
        if k:
            total = total + psf_ref[k]
        line = jnp.where(lane == (k + lead) % 256, psf_ref[taps - 1 - k if flip else k], line)
    line = line / jnp.full((8, 256), total, jnp.float32)
    return pltpu.roll(jnp.broadcast_to(line[:1], (rows, 256)), 0, 1, stride=1, stride_axis=0)


def x_band(psf_ref, flip):
    m = band(psf_ref, -15, not flip, 128)
    return m[:, :128], m[:, 128:]


def prep_kernel(psf_y_ref, psf_z_ref, yf_ref, ya_ref, zo_ref, zl_ref, zh_ref, za_ref):
    yf_ref[...] = band(psf_y_ref, -15, True, 128)[:, :128]
    ya_ref[...] = band(psf_y_ref, -15, False, 128)[:, :128]
    fwd = band(psf_z_ref, 1, False, 128)
    zl_ref[...] = fwd[:64, :64]
    zo_ref[...] = fwd[:, 64:128]
    zh_ref[...] = fwd[64:, 128:192]
    za_ref[...] = band(psf_z_ref, 1, True, 64)[:, :128]


def prepare(psf_y, psf_z):
    out = [(128, 128), (128, 128), (128, 64), (64, 64), (64, 64), (64, 128)]
    return call(prep_kernel, out, [psf_y, psf_z], 1, "prepare")


def blur_lanes(tiles, near, far):
    lane = lax.broadcasted_iota(jnp.int32, tiles[0].shape, 1)
    zero = jnp.zeros_like(tiles[0])
    out = []
    for t in range(8):
        after = tiles[t + 1] if t < 7 else zero
        before = tiles[t - 1] if t > 0 else zero
        out.append(dot(tiles[t], near) + dot(jnp.where(lane < 64, after, before), far))
    return out


def rows_at(t, i, per=16, offset=0):
    block = 8 * t + i
    return x_index(block // 2, block % 2) * per + offset


def write_columns(out_ref, t, tile, per=16, offset=0):
    turned = tile.T
    for i in range(8):
        at = rows_at(t, i, per, offset)
        out_ref[at : at + 16, :] = turned[16 * i : 16 * i + 16, :]


def first_kernel(psf_x_ref, est_ref, obs_ref, out_ref):
    near, far = x_band(psf_x_ref, False)
    blurred = blur_lanes([est_ref[:, 128 * t : 128 * t + 128] for t in range(8)], near, far)
    for t in range(8):
        write_columns(out_ref, t, blurred[t], 32, 0)
        write_columns(out_ref, t, obs_ref[:, 128 * t : 128 * t + 128], 32, 16)


def turn_kernel(in_ref, out_ref):
    for t in range(8):
        write_columns(out_ref, t, in_ref[:, 128 * t : 128 * t + 128])


def last_kernel(psf_x_ref, back_ref, est_ref, out_ref):
    near, far = x_band(psf_x_ref, True)

    def tile(ref, t):
        spots = [rows_at(t, i) for i in range(8)]
        return jnp.concatenate([ref[at : at + 16, :] for at in spots], axis=0).T

    blurred = blur_lanes([tile(back_ref, t) for t in range(8)], near, far)
    for t in range(8):
        out_ref[:, 128 * t : 128 * t + 128] = blurred[t] * tile(est_ref, t)


def swap_groups(tiles):
    group = lax.broadcasted_iota(jnp.int32, (8, 128), 1) // 16
    tiles = [tiles[0]] + [pltpu.roll(tiles[i], 16 * i, 1) for i in range(1, 8)]
    for b in (1, 2, 4):
        taken = (group & b) != 0
        tiles = [jnp.where(taken, tiles[(i + b) % 8], tiles[i]) for i in range(8)]
    return [tiles[0]] + [pltpu.roll(tiles[8 - i], 128 - 16 * i, 1) for i in range(1, 8)]


def unpack_one(in_ref, out_ref, rows_ref, per, offset):
    for zc in range(8):
        for half in range(2):
            at = zc * 8 * per + half * 8 + offset
            tiles = swap_groups([in_ref[at + per * i : at + per * i + 8, :] for i in range(8)])
            at = zc * 128 + half * 8
            for i in range(8):
                rows_ref[at + 16 * i : at + 16 * i + 8, :] = tiles[i]
    for zc in range(8):
        for x in range(16):
            out_ref[x, zc * 8 : zc * 8 + 8, :] = rows_ref[pl.ds(zc * 128 + x, 8, stride=16), :]


def unpack_kernel(in_ref, out_ref, rows_ref):
    unpack_one(in_ref, out_ref, rows_ref, 16, 0)


def unpack_pair_kernel(in_ref, y_ref, a_ref, b_ref, rows_ref, more_ref):
    unpack_one(in_ref, a_ref, rows_ref, 32, 0)
    for x in range(16):
        a_ref[x] = dot(a_ref[x], y_ref[...])
    unpack_one(in_ref, b_ref, more_ref, 32, 16)


def pack_kernel(in_ref, out_ref, rows_ref):
    for zc in range(8):
        for x in range(16):
            rows_ref[pl.ds(zc * 128 + x, 8, stride=16), :] = in_ref[x, zc * 8 : zc * 8 + 8, :]
    for zc in range(8):
        for half in range(2):
            at = zc * 128 + half * 8
            tiles = swap_groups([rows_ref[at + 16 * i : at + 16 * i + 8, :] for i in range(8)])
            for i in range(8):
                out_ref[at + 16 * i : at + 16 * i + 8, :] = tiles[i]


def exchange(rows):
    per = rows.shape[0] // 64
    t = lax.all_to_all(rows.reshape(64, per, 128), SLAB, 0, 0, tiled=True)
    return t.reshape(rows.shape)


def tap_vectors(psf_ref, flip):
    total = psf_ref[0]
    for k in range(1, 31):
        total = total + psf_ref[k]
    scale = 1.0 / jnp.full((8, 128), total, jnp.float32)
    return [psf_ref[30 - k if flip else k] * scale for k in range(31)]


def add_block(w, ref, z, acc, shift):
    for j in range(16):
        v = ref[j, z, :]
        for i in range(16):
            k = j + shift - i + 15
            if 0 <= k <= 30:
                p = w[k] * v
                acc[i] = p if acc[i] is None else acc[i] + p
    return acc


def over_planes(body):
    def step(t, _):
        body(pl.ds(pl.multiple_of(t * 8, 8), 8))
        return 0

    lax.fori_loop(0, 8, step, 0)


def near_kernel(flip, psf_ref, core_ref, own_ref, swapped_ref, out_ref):
    w = tap_vectors(psf_ref, flip)

    def run(shift):
        def body(z):
            acc = add_block(w, own_ref, z, [None] * 16, 0)
            acc = add_block(w, swapped_ref, z, acc, shift)
            for i in range(16):
                out_ref[i, z, :] = acc[i]

        over_planes(body)

    pl.when(core_ref[0] == 0)(lambda: run(16))
    pl.when(core_ref[0] != 0)(lambda: run(-16))


def far_part(w, core_ref, part_ref, passed_ref, finish):
    def run(shift):
        def body(z):
            acc = [part_ref[i, z, :] for i in range(16)]
            finish(z, add_block(w, passed_ref, z, acc, shift))

        over_planes(body)

    pl.when(core_ref[0] == 0)(lambda: run(-16))
    pl.when(core_ref[0] != 0)(lambda: run(16))


def far_kernel(flip, psf_ref, core_ref, part_ref, passed_ref, out_ref):
    w = tap_vectors(psf_ref, flip)

    def finish(z, acc):
        for i in range(16):
            out_ref[i, z, :] = acc[i]

    far_part(w, core_ref, part_ref, passed_ref, finish)


def update_kernel(flip, psf_ref, core_ref, part_ref, passed_ref, est_ref, y_ref, new_ref, out_ref):
    w = tap_vectors(psf_ref, flip)

    def finish(z, acc):
        for i in range(16):
            new_ref[i, z, :] = est_ref[i, z, :] * acc[i]

    far_part(w, core_ref, part_ref, passed_ref, finish)
    for i in range(16):
        out_ref[i] = dot(new_ref[i], y_ref[...])


def x_halo(v, psf, core, flip):
    passed = lax.ppermute(v, SLAB, NEXT)
    swapped = lax.ppermute(v, "c", SWAP)
    near = call(functools.partial(near_kernel, flip), BLOCK, [psf, core, v, swapped], 2, "x_near")
    return near, passed


def own_kernel(v_ref, zo_ref, out_ref):
    for x in range(16):
        out_ref[x] = dot(zo_ref[...], v_ref[x])


def ratio_kernel(
    slab_ref, part_ref, below_ref, above_ref, obs_ref, obs_below_ref, obs_above_ref,
    zl_ref, zh_ref, za_ref, ya_ref, out_ref, ratio_ref
):
    has_below = jnp.full((32, 128), slab_ref[0], jnp.int32) > 0
    has_above = jnp.full((32, 128), slab_ref[0], jnp.int32) < 7
    for x in range(16):
        low = part_ref[x, :64, :] + dot(zl_ref[...], below_ref[x])
        high = part_ref[x, 64:, :] + dot(zh_ref[...], above_ref[x])
        ratio_ref[x, :32, :] = jnp.where(has_below, obs_below_ref[x] / low[:32], 0.0)
        ratio_ref[x, 32:64, :] = obs_ref[x, :32, :] / low[32:]
        ratio_ref[x, 64:96, :] = obs_ref[x, 32:, :] / high[:32]
        ratio_ref[x, 96:, :] = jnp.where(has_above, obs_above_ref[x] / high[32:], 0.0)
    for x in range(16):
        out_ref[x] = dot(dot(za_ref[...], ratio_ref[x]), ya_ref[...])


def per_device(observed, estimate, psf_y, psf_x, psf_z):
    core = lax.axis_index("c").reshape(1)
    slab = lax.axis_index("z").reshape(1)
    est0 = estimate.reshape(128, 1024)

    first = call(first_kernel, (2048, 128), [psf_x, est0, observed.reshape(128, 1024)], 4, "first")
    arrived = exchange(first)
    yf, ya, zo, zl, zh, za = prepare(psf_y, psf_z)
    turned = call(turn_kernel, ROWS, [est0], 1, "turn")

    def z_phase(v, obs, obs_below, obs_above, riding):
        below = lax.ppermute(v, "z", UP)
        above = lax.ppermute(v, "z", DOWN)
        if obs_below is None:
            obs_below = lax.ppermute(obs[:, 32:], "z", UP)
            obs_above = lax.ppermute(obs[:, :32], "z", DOWN)
        part = call(own_kernel, (16, 128, 128), [v, zo], 1, "z_own")
        riding, part = lax.optimization_barrier((riding, part))
        rode = exchange(riding)
        back = call(
            ratio_kernel,
            BLOCK,
            [slab, part, below, above, obs, obs_below, obs_above, zl, zh, za, ya],
            4,
            "ratio",
            [(16, 128, 128)],
        )
        return back, rode, obs_below, obs_above

    v, obs = call(unpack_pair_kernel, [BLOCK, BLOCK], [arrived, yf], 2, "unpack_pair", [ROWS, ROWS])
    back, rode, obs_below, obs_above = z_phase(v, obs, None, None, turned)
    est = call(unpack_kernel, BLOCK, [rode], 1, "unpack", [ROWS])

    near, passed = x_halo(back, psf_x, core, True)
    est, v = call(
        functools.partial(update_kernel, True),
        [BLOCK, BLOCK],
        [psf_x, core, near, passed, est, yf],
        2,
        "update",
    )
    est_rows = call(pack_kernel, ROWS, [est], 1, "pack_est", [ROWS])
    near, passed = x_halo(v, psf_x, core, False)
    v = call(functools.partial(far_kernel, False), BLOCK, [psf_x, core, near, passed], 1, "x_far")

    back, rode, _, _ = z_phase(v, obs, obs_below, obs_above, est_rows)
    back = exchange(call(pack_kernel, ROWS, [back], 1, "pack_back", [ROWS]))
    out = call(last_kernel, (128, 1024), [psf_x, back, rode], 4, "last")
    return out.reshape(8, 16, 1024)


def solution(mesh):
    fine = Mesh(mesh.devices.reshape(8, 4, 2, 4, 2), ("z", "x", "yl", "yh", "c"))
    spec = P(("z", "x", "yl"), ("yh", "c"), None)
    return jax.shard_map(
        per_device,
        mesh=fine,
        in_specs=(spec, spec, P(), P(), P()),
        out_specs=spec,
        check_vma=False,
    )
```

time: 299 us -> 176 us (0.59)
  other arithmetic: 49.3 us -> 0 us
  matrix products: 49.2 us -> 0 us
  local copies, waits for them, and re-layouts: 46.5 us -> 6.21 us
  Pallas kernels: 0 us -> 26.8 us
  waiting for transfers between devices: 57.8 us -> 50.1 us
    dot_general x12 -> x0, matrix products: 49.2 us -> none  [the longest x4 44.2 us: y_blur(): return jnp.einsum('xzq,qy->xzy', v, m, precision=HI)]
    add x2 -> x0, other arithmetic: 43.3 us -> none  [x_blur(): total = total + w[k] * ext[k + 1:k + 17]]
    pallas_call x0 -> x16, Pallas kernels: none -> 26.8 us  [call(): pl.pallas_call(kernel, out_shape=jax.tree.map(lambda s: pltpu.VMEM(s, jnp...]
    reshape x11 -> x0, local copies, waits for them, and re-layouts: 22.9 us -> none  [the longest x3 10.7 us: leave(): block.reshape(16, 8, 8, 8, 16).transpose(1, 3, 0, 2, 4).reshape(64, 16, 128)]
    ppermute x13 -> x10, waiting for transfers between devices: 44.3 us -> 22.7 us  [the longest x2 9.93 us: z_phase(): above = lax.ppermute(v, 'z', DOWN)]
    transpose x8 -> x0, local copies, waits for them, and re-layouts: 18.5 us -> none  [the longest x2 13.3 us: enter(): t = t.reshape(8, 8, 16, 8, 16).transpose(2, 0, 3, 1, 4)]
    ppermute x13 -> x10, starting transfers between devices: 45.1 us -> 30.3 us  [the longest x2 10.1 us: z_phase(): below = lax.ppermute(v, 'z', UP)]
    all_to_all x2 -> x3, waiting for transfers between devices: 13.5 us -> 27.4 us  [exchange(): t = lax.all_to_all(rows.reshape(64, per, 128), SLAB, 0, 0, tiled=True)]
  transfers between devices with their start and end apart: 15 -> 13, of which waited for: 8 -> 7; matrix products, arithmetic and copies ran while one was open for 21% -> 0% of each run, Pallas kernels for 0% -> 9%
where the time goes in v4:
time: 176 us; the launch traced here: 173 us
  starting transfers between devices  61.2 us (35%)
  waiting for transfers between devices  50.1 us (28%)
  blocking collectives  28.7 us (16%)
  Pallas kernels  26.8 us (15%)
  local copies, waits for them, and re-layouts  6.21 us (4%)
    all_to_all x3, starting transfers between devices, exchange(): t = lax.all_to_all(rows.reshape(64, per, 128), SLAB, 0, 0, tiled=True)  30.9 us
    all_to_all x1, blocking collectives, exchange(): t = lax.all_to_all(rows.reshape(64, per, 128), SLAB, 0, 0, tiled=True)  28.7 us
    all_to_all x3, waiting for transfers between devices, exchange(): t = lax.all_to_all(rows.reshape(64, per, 128), SLAB, 0, 0, tiled=True)  27.4 us
    pallas_call x16, Pallas kernels, call(): pl.pallas_call(kernel, out_shape=jax.tree.map(lambda s: pltpu.VMEM(s, jnp...  26.8 us
    ppermute x2, starting transfers between devices, z_phase(): below = lax.ppermute(v, 'z', UP)  10.1 us
    ppermute x2, waiting for transfers between devices, z_phase(): above = lax.ppermute(v, 'z', DOWN)  9.93 us
    ppermute x2, starting transfers between devices, x_halo(): passed = lax.ppermute(v, SLAB, NEXT)  6.88 us
    ppermute x2, waiting for transfers between devices, x_halo(): passed = lax.ppermute(v, SLAB, NEXT)  6.72 us
  transfers between devices with their start and end apart: 13, of which 7 were waited for; matrix products, arithmetic and copies ran while one was open for 0% of the time, Pallas kernels for 9%

profile of v4, /device:TPU:1, one launch (start us, length us, event | category | flops | bytes accessed | tf_op | source)
XLA Modules:
  0.0 173.2 jit_solution(2481192479411023449)
XLA Ops:
  0.7 1.0 copy-done
  1.7 1.0 copy-done.2
  2.7 2.8 %first.1 = f32[2048,128]{1,0:T(8,128)} custom-call(f32[31]{0:T(128)S(1)} %copy-done.5, f32[128,1024]{1,0:T(8,128)S(1)} %bitcast.15, f32[128,1024]{1,0:T(8,128)S(1)} %bitcast.21), custom_call_target="tpu_custom_call" | custom-call | flops 4000000 | bytes 12000000 | tf_op jit(solution)/shard_map/first/pallas_call | solution.py:37
  5.6 11.8 %all-to-all-start = ((f32[64,32,128]{2,1,0:T(8,128)}), f32[64,32,128]{2,1,0:T(8,128)S(1)}, u32[]{:S(2)}, u32[]{:S(2)}) async-start(f32[64,32,128]{2,1,0:T(8,128)} %bitcast.4), calls=%async_computation | async-start | bytes 2097152 | tf_op jit(solution)/shard_map/all_to_all | solution.py:183
  18.2 27.3 %all-to-all-done = f32[64,32,128]{2,1,0:T(8,128)S(1)} async-done(((f32[64,32,128]{2,1,0:T(8,128)}), f32[64,32,128]{2,1,0:T(8,128)S(1)}, u32[]{:S(2)}, u32[]{:S(2)}) %all-to-all-start) | async-done | bytes 1048608 | tf_op jit(solution)/shard_map/all_to_all | solution.py:183
  45.6 1.6 unpack_pair.1
  47.1 1.3 collective-permute-start.1
  48.4 5.4 %collective-permute-start = (f32[16,64,128]{2,1,0:T(8,128)S(1)}, f32[16,64,128]{2,1,0:T(8,128)}, u32[]{:S(2)}, u32[]{:S(2)}) collective-permute-start(f32[16,64,128]{2,1,0:T(8,128)S(1)} %get-tuple-element.20.v_ref), channel_id=1, source_target_pairs={{0,64},{64,128},{128,192},{192,256},{256,320},{320,384},{384,448},... | collective-permute-start | bytes 1572872 | tf_op jit(solution)/shard_map/ppermute | solution.py:304
  55.8 6.8 %all-to-all-start.1 = ((f32[64,16,128]{2,1,0:T(8,128)}), f32[64,16,128]{2,1,0:T(8,128)S(1)}, u32[]{:S(2)}, u32[]{:S(2)}) async-start(f32[64,16,128]{2,1,0:T(8,128)} %bitcast.6), calls=%async_computation.1 | async-start | bytes 1048576 | tf_op jit(solution)/shard_map/all_to_all | solution.py:183
  63.5 1.3 collective-permute-start.3
  64.8 4.0 %collective-permute-start.2 = (f32[16,32,128]{2,1,0:T(8,128)}, f32[16,32,128]{2,1,0:T(8,128)S(1)}, u32[]{:S(2)}, u32[]{:S(2)}) collective-permute-start(f32[16,32,128]{2,1,0:T(8,128)} %get-tuple-element.34), channel_id=1, source_target_pairs={{0,64},{64,128},{128,192},{192,256},{256,320},{320,384},{384,448},... | collective-permute-start | bytes 786440 | tf_op jit(solution)/shard_map/ppermute | solution.py:307
  68.8 4.2 %collective-permute-done.3.obs_above_ref = f32[16,32,128]{2,1,0:T(8,128)S(1)} collective-permute-done((f32[16,32,128]{2,1,0:T(8,128)}, f32[16,32,128]{2,1,0:T(8,128)S(1)}, u32[]{:S(2)}, u32[]{:S(2)}) %collective-permute-start.3) | collective-permute-done | bytes 262176 | tf_op jit(solution)/shard_map/ppermute | solution.py:308
  74.0 4.0 %ratio.2.own_ref = f32[16,64,128]{2,1,0:T(8,128)S(1)} custom-call(s32[1]{0:T(128)} %bitcast.slab_ref, f32[16,128,128]{2,1,0:T(8,128)S(1)} %z_own.2.part_ref, f32[16,64,128]{2,1,0:T(8,128)} %collective-permute-done.below_ref, f32[16,64,128]{2,1,0:T(8,128)} %collective-permute-done.1.above_ref, f32[16,64,128]{2,1,0:T(8,128)S(1)} %get-tuple-element.23.obs_ref, ...), custom_call_target="tpu_custom_call" | custom-call | flops 4000000 | bytes 12000000 | tf_op jit(solution)/shard_map/ratio/pallas_call | solution.py:37
  78.1 3.5 %collective-permute-start.4 = (f32[16,64,128]{2,1,0:T(8,128)S(1)}, f32[16,64,128]{2,1,0:T(8,128)S(1)}, u32[]{:S(2)}, u32[]{:S(2)}) collective-permute-start(f32[16,64,128]{2,1,0:T(8,128)S(1)} %ratio.2.own_ref), channel_id=1, source_target_pairs={{0,1},{1,0},{2,3},{3,2},{4,5},{5,4},{6,7},{7,6},{8,9},{9,8},{10,11... | collective-permute-start | bytes 1572872 | tf_op jit(solution)/shard_map/ppermute | solution.py:266
  81.6 3.2 %collective-permute-start.5 = (f32[16,64,128]{2,1,0:T(8,128)S(1)}, f32[16,64,128]{2,1,0:T(8,128)}, u32[]{:S(2)}, u32[]{:S(2)}) collective-permute-start(f32[16,64,128]{2,1,0:T(8,128)S(1)} %ratio.2.own_ref), channel_id=1, source_target_pairs={{8,1},{2,9},{10,3},{4,11},{12,5},{6,13},{14,7},{16,15},{24,17},{18... | collective-permute-start | bytes 1572872 | tf_op jit(solution)/shard_map/ppermute | solution.py:265
  86.5 1.0 copy-done.4
  87.5 1.6 x_near.2.part_ref
  89.1 3.1 %collective-permute-done.5.passed_ref = f32[16,64,128]{2,1,0:T(8,128)} collective-permute-done((f32[16,64,128]{2,1,0:T(8,128)S(1)}, f32[16,64,128]{2,1,0:T(8,128)}, u32[]{:S(2)}, u32[]{:S(2)}) %collective-permute-start.5) | collective-permute-done | bytes 524320 | tf_op jit(solution)/shard_map/ppermute | solution.py:265
  92.2 2.4 %update.1 = (f32[16,64,128]{2,1,0:T(8,128)S(1)}, f32[16,64,128]{2,1,0:T(8,128)S(1)}) custom-call(f32[31]{0:T(128)S(1)} %copy-done.5, s32[1]{0:T(128)} %bitcast.1.core_ref, f32[16,64,128]{2,1,0:T(8,128)S(1)} %x_near.2.part_ref, f32[16,64,128]{2,1,0:T(8,128)} %collective-permute-done.5.passed_ref, f32[16,64,128]{2,1,0:T(8,128)S(1)} %unpack.1.est_ref, ...), custom_call_target="tpu_custom_call" | custom-call | flops 2000000 | bytes 6000000 | tf_op jit(solution)/shard_map/update/pallas_call | solution.py:37
  94.6 1.9 %collective-permute-start.6 = (f32[16,64,128]{2,1,0:T(8,128)S(1)}, f32[16,64,128]{2,1,0:T(8,128)S(1)}, u32[]{:S(2)}, u32[]{:S(2)}) collective-permute-start(f32[16,64,128]{2,1,0:T(8,128)S(1)} %get-tuple-element.30.own_ref), channel_id=1, source_target_pairs={{0,1},{1,0},{2,3},{3,2},{4,5},{5,4},{6,7},{7,6},{8,9},{9,8},{10,11... | collective-permute-start | bytes 1572872 | tf_op jit(solution)/shard_map/ppermute | solution.py:266
  96.6 3.7 %collective-permute-start.7 = (f32[16,64,128]{2,1,0:T(8,128)S(1)}, f32[16,64,128]{2,1,0:T(8,128)S(1)}, u32[]{:S(2)}, u32[]{:S(2)}) collective-permute-start(f32[16,64,128]{2,1,0:T(8,128)S(1)} %get-tuple-element.30.own_ref), channel_id=1, source_target_pairs={{8,1},{2,9},{10,3},{4,11},{12,5},{6,13},{14,7},{16,15},{24,17},{18... | collective-permute-start | bytes 1572872 | tf_op jit(solution)/shard_map/ppermute | solution.py:265
  100.3 1.6 pack_est.1
  101.9 1.6 x_near.3.part_ref
  103.5 3.6 %collective-permute-done.7.passed_ref = f32[16,64,128]{2,1,0:T(8,128)S(1)} collective-permute-done((f32[16,64,128]{2,1,0:T(8,128)S(1)}, f32[16,64,128]{2,1,0:T(8,128)S(1)}, u32[]{:S(2)}, u32[]{:S(2)}) %collective-permute-start.7) | collective-permute-done | bytes 524320 | tf_op jit(solution)/shard_map/ppermute | solution.py:265
  107.1 1.1 x_far.1.v_ref
  109.2 12.3 %all-to-all-start.3 = ((f32[64,16,128]{2,1,0:T(8,128)}), f32[64,16,128]{2,1,0:T(8,128)S(1)}, u32[]{:S(2)}, u32[]{:S(2)}) async-start(f32[64,16,128]{2,1,0:T(8,128)} %bitcast.10), calls=%async_computation.3 | async-start | bytes 1048576 | tf_op jit(solution)/shard_map/all_to_all | solution.py:183
  121.5 1.3 collective-permute-start.9
  122.8 4.7 %collective-permute-start.8 = (f32[16,64,128]{2,1,0:T(8,128)S(1)}, f32[16,64,128]{2,1,0:T(8,128)S(1)}, u32[]{:S(2)}, u32[]{:S(2)}) collective-permute-start(f32[16,64,128]{2,1,0:T(8,128)S(1)} %x_far.1.v_ref), channel_id=1, source_target_pairs={{0,64},{64,128},{128,192},{192,256},{256,320},{320,384},{384,448},... | collective-permute-start | bytes 1572872 | tf_op jit(solution)/shard_map/ppermute | solution.py:304
  127.5 9.9 %collective-permute-done.9.above_ref = f32[16,64,128]{2,1,0:T(8,128)S(1)} collective-permute-done((f32[16,64,128]{2,1,0:T(8,128)S(1)}, f32[16,64,128]{2,1,0:T(8,128)S(1)}, u32[]{:S(2)}, u32[]{:S(2)}) %collective-permute-start.9) | collective-permute-done | bytes 524320 | tf_op jit(solution)/shard_map/ppermute | solution.py:305
  138.3 2.9 %ratio.3.in_ref = f32[16,64,128]{2,1,0:T(8,128)S(1)} custom-call(s32[1]{0:T(128)} %bitcast.slab_ref, f32[16,128,128]{2,1,0:T(8,128)S(1)} %z_own.3.part_ref, f32[16,64,128]{2,1,0:T(8,128)S(1)} %collective-permute-done.8.below_ref, f32[16,64,128]{2,1,0:T(8,128)S(1)} %collective-permute-done.9.above_ref, f32[16,64,128]{2,1,0:T(8,128)S(1)} %get-tuple-element.23.obs_ref, ...), custom_call_target="tpu_custom_call" | custom-call | flops 4000000 | bytes 12000000 | tf_op jit(solution)/shard_map/ratio/pallas_call | solution.py:37
  142.0 28.7 %all_to_all.20 = f32[64,16,128]{2,1,0:T(8,128)S(1)} all-to-all(f32[64,16,128]{2,1,0:T(8,128)S(1)} %bitcast.19), channel_id=1, replica_groups=mesh['z'=8,'x'=4,'yl'=2,'yh'=4,'c'=2] {'x','yl','yh','c'}, dimensions={0} | all-to-all | bytes 1048576 | tf_op jit(solution)/shard_map/all_to_all | solution.py:183
  170.7 1.7 last.1
  (29 shorter events, 10.4 us)
Async XLA Ops:
  0.0 0.7 copy-start.5
  0.7 1.0 copy-start
  1.7 1.0 copy-start.2
  5.6 11.8 %copy-start.6 = (f32[31]{0:T(128)S(1)}, f32[31]{0:T(128)}, u32[]{:S(2)}) copy-start(f32[31]{0:T(128)} %psf_y_ref.1) | copy-start | bytes 376
  5.6 11.8 %copy-start.7 = (f32[63]{0:T(128)S(1)}, f32[63]{0:T(128)}, u32[]{:S(2)}) copy-start(f32[63]{0:T(128)} %psf_z_ref.1) | copy-start | bytes 760
  5.6 40.0 %all-to-all-start = ((f32[64,32,128]{2,1,0:T(8,128)}), f32[64,32,128]{2,1,0:T(8,128)S(1)}, u32[]{:S(2)}, u32[]{:S(2)}) async-start(f32[64,32,128]{2,1,0:T(8,128)} %bitcast.4), calls=%async_computation | async-start | bytes 2097152 | tf_op jit(solution)/shard_map/all_to_all | solution.py:183
  45.5 8.3 %copy-start.1 = (f32[8,16,1024]{2,1,0:T(8,128)S(1)}, f32[8,16,1024]{2,1,0:T(8,128)}, u32[]{:S(2)}) copy-start(f32[8,16,1024]{2,1,0:T(8,128)} %param.6) | copy-start | bytes 1572868
  47.1 26.9 %collective-permute-start.1 = (f32[16,64,128]{2,1,0:T(8,128)S(1)}, f32[16,64,128]{2,1,0:T(8,128)}, u32[]{:S(2)}, u32[]{:S(2)}) collective-permute-start(f32[16,64,128]{2,1,0:T(8,128)S(1)} %get-tuple-element.20.v_ref), channel_id=1, source_target_pairs={{64,0},{128,64},{192,128},{256,192},{320,256},{384,320},{448,384},... | collective-permute-start | bytes 1572872 | tf_op jit(solution)/shard_map/ppermute | solution.py:305
  48.4 25.6 %collective-permute-start = (f32[16,64,128]{2,1,0:T(8,128)S(1)}, f32[16,64,128]{2,1,0:T(8,128)}, u32[]{:S(2)}, u32[]{:S(2)}) collective-permute-start(f32[16,64,128]{2,1,0:T(8,128)S(1)} %get-tuple-element.20.v_ref), channel_id=1, source_target_pairs={{0,64},{64,128},{128,192},{192,256},{256,320},{320,384},{384,448},... | collective-permute-start | bytes 1572872 | tf_op jit(solution)/shard_map/ppermute | solution.py:304
  55.8 29.0 %all-to-all-start.1 = ((f32[64,16,128]{2,1,0:T(8,128)}), f32[64,16,128]{2,1,0:T(8,128)S(1)}, u32[]{:S(2)}, u32[]{:S(2)}) async-start(f32[64,16,128]{2,1,0:T(8,128)} %bitcast.6), calls=%async_computation.1 | async-start | bytes 1048576 | tf_op jit(solution)/shard_map/all_to_all | solution.py:183
  63.5 9.5 %collective-permute-start.3 = (f32[16,32,128]{2,1,0:T(8,128)}, f32[16,32,128]{2,1,0:T(8,128)S(1)}, u32[]{:S(2)}, u32[]{:S(2)}) collective-permute-start(f32[16,32,128]{2,1,0:T(8,128)} %get-tuple-element.33), channel_id=1, source_target_pairs={{64,0},{128,64},{192,128},{256,192},{320,256},{384,320},{448,384},... | collective-permute-start | bytes 786440 | tf_op jit(solution)/shard_map/ppermute | solution.py:308
  64.8 9.2 %collective-permute-start.2 = (f32[16,32,128]{2,1,0:T(8,128)}, f32[16,32,128]{2,1,0:T(8,128)S(1)}, u32[]{:S(2)}, u32[]{:S(2)}) collective-permute-start(f32[16,32,128]{2,1,0:T(8,128)} %get-tuple-element.34), channel_id=1, source_target_pairs={{0,64},{64,128},{128,192},{192,256},{256,320},{320,384},{384,448},... | collective-permute-start | bytes 786440 | tf_op jit(solution)/shard_map/ppermute | solution.py:307
  78.1 7.6 %collective-permute-start.4 = (f32[16,64,128]{2,1,0:T(8,128)S(1)}, f32[16,64,128]{2,1,0:T(8,128)S(1)}, u32[]{:S(2)}, u32[]{:S(2)}) collective-permute-start(f32[16,64,128]{2,1,0:T(8,128)S(1)} %ratio.2.own_ref), channel_id=1, source_target_pairs={{0,1},{1,0},{2,3},{3,2},{4,5},{5,4},{6,7},{7,6},{8,9},{9,8},{10,11... | collective-permute-start | bytes 1572872 | tf_op jit(solution)/shard_map/ppermute | solution.py:266
  81.6 10.6 %collective-permute-start.5 = (f32[16,64,128]{2,1,0:T(8,128)S(1)}, f32[16,64,128]{2,1,0:T(8,128)}, u32[]{:S(2)}, u32[]{:S(2)}) collective-permute-start(f32[16,64,128]{2,1,0:T(8,128)S(1)} %ratio.2.own_ref), channel_id=1, source_target_pairs={{8,1},{2,9},{10,3},{4,11},{12,5},{6,13},{14,7},{16,15},{24,17},{18... | collective-permute-start | bytes 1572872 | tf_op jit(solution)/shard_map/ppermute | solution.py:265
  85.7 0.8 copy-start.3
  86.5 1.0 copy-start.4
  94.6 7.3 %collective-permute-start.6 = (f32[16,64,128]{2,1,0:T(8,128)S(1)}, f32[16,64,128]{2,1,0:T(8,128)S(1)}, u32[]{:S(2)}, u32[]{:S(2)}) collective-permute-start(f32[16,64,128]{2,1,0:T(8,128)S(1)} %get-tuple-element.30.own_ref), channel_id=1, source_target_pairs={{0,1},{1,0},{2,3},{3,2},{4,5},{5,4},{6,7},{7,6},{8,9},{9,8},{10,11... | collective-permute-start | bytes 1572872 | tf_op jit(solution)/shard_map/ppermute | solution.py:266
  96.6 10.5 %collective-permute-start.7 = (f32[16,64,128]{2,1,0:T(8,128)S(1)}, f32[16,64,128]{2,1,0:T(8,128)S(1)}, u32[]{:S(2)}, u32[]{:S(2)}) collective-permute-start(f32[16,64,128]{2,1,0:T(8,128)S(1)} %get-tuple-element.30.own_ref), channel_id=1, source_target_pairs={{8,1},{2,9},{10,3},{4,11},{12,5},{6,13},{14,7},{16,15},{24,17},{18... | collective-permute-start | bytes 1572872 | tf_op jit(solution)/shard_map/ppermute | solution.py:265
  109.2 32.8 %all-to-all-start.3 = ((f32[64,16,128]{2,1,0:T(8,128)}), f32[64,16,128]{2,1,0:T(8,128)S(1)}, u32[]{:S(2)}, u32[]{:S(2)}) async-start(f32[64,16,128]{2,1,0:T(8,128)} %bitcast.10), calls=%async_computation.3 | async-start | bytes 1048576 | tf_op jit(solution)/shard_map/all_to_all | solution.py:183
  121.5 15.9 %collective-permute-start.9 = (f32[16,64,128]{2,1,0:T(8,128)S(1)}, f32[16,64,128]{2,1,0:T(8,128)S(1)}, u32[]{:S(2)}, u32[]{:S(2)}) collective-permute-start(f32[16,64,128]{2,1,0:T(8,128)S(1)} %x_far.1.v_ref), channel_id=1, source_target_pairs={{64,0},{128,64},{192,128},{256,192},{320,256},{384,320},{448,384},... | collective-permute-start | bytes 1572872 | tf_op jit(solution)/shard_map/ppermute | solution.py:305
  122.8 15.5 %collective-permute-start.8 = (f32[16,64,128]{2,1,0:T(8,128)S(1)}, f32[16,64,128]{2,1,0:T(8,128)S(1)}, u32[]{:S(2)}, u32[]{:S(2)}) collective-permute-start(f32[16,64,128]{2,1,0:T(8,128)S(1)} %x_far.1.v_ref), channel_id=1, source_target_pairs={{0,64},{64,128},{128,192},{192,256},{256,320},{320,384},{384,448},... | collective-permute-start | bytes 1572872 | tf_op jit(solution)/shard_map/ppermute | solution.py:304

commit v5 on v4

v5 whole, which is shorter than its diff:
```python
import functools

import jax
import jax.numpy as jnp
from jax import lax
from jax.experimental import pallas as pl
from jax.experimental.pallas import tpu as pltpu
from jax.sharding import Mesh, PartitionSpec as P

LIMIT = 6 * 2**20
SLAB = ("x", "yl", "yh", "c")
BLOCK = (16, 64, 128)
ROWS = (1024, 128)
VMEM = pl.BlockSpec(memory_space=pltpu.VMEM)
SMEM = pl.BlockSpec(memory_space=pltpu.SMEM)
HBM = pl.BlockSpec(memory_space=pltpu.HBM)


def x_index(b, c):
    x, yh, yl = b // 8, (b % 8) // 2, b % 2
    return ((x * 2 + yl) * 4 + yh) * 2 + c


SWAP = [(0, 1), (1, 0)]
NEXT = [(x_index(b, 0), x_index(b - 1, 1)) for b in range(1, 32)] + [
    (x_index(b, 1), x_index(b + 1, 0)) for b in range(31)
]
UP = [(z, z + 1) for z in range(7)]
DOWN = [(z + 1, z) for z in range(7)]


def is_shape(s):
    return isinstance(s, tuple)


def call(kernel, out, args, us, name, scratch=(), free=(), free_out=False):
    pinned = [
        a if a.ndim == 1 or i in free else pltpu.with_memory_space_constraint(a, pltpu.VMEM)
        for i, a in enumerate(args)
    ]
    kind = jax.ShapeDtypeStruct if free_out else pltpu.VMEM
    return pl.pallas_call(
        kernel,
        out_shape=jax.tree.map(lambda s: kind(s, jnp.float32), out, is_leaf=is_shape),
        in_specs=[SMEM if a.ndim == 1 else VMEM for a in args],
        out_specs=jax.tree.map(lambda s: VMEM, out, is_leaf=is_shape),
        scratch_shapes=[pltpu.VMEM(s, jnp.float32) for s in scratch],
        cost_estimate=pl.CostEstimate(
            flops=int(us * 1e9), bytes_accessed=int(us * 3e6), transcendentals=0
        ),
        compiler_params=pltpu.CompilerParams(vmem_limit_bytes=LIMIT),
        name=name,
    )(*pinned)


def split(m):
    high = m.astype(jnp.bfloat16)
    return high, (m - high.astype(jnp.float32)).astype(jnp.bfloat16)


def dot(a, b):
    (ah, al), (bh, bl) = a, b

    def one(p, q):
        return jnp.dot(p, q, preferred_element_type=jnp.float32)

    return one(ah, bh) + (one(al, bh) + one(ah, bl))


def band(psf_ref, lead, flip, rows):
    taps = psf_ref.shape[0]
    lane = lax.broadcasted_iota(jnp.int32, (8, 256), 1)
    line = jnp.zeros((8, 256), jnp.float32)
    total = psf_ref[0]
    for k in range(taps):
        if k:
            total = total + psf_ref[k]
        line = jnp.where(lane == (k + lead) % 256, psf_ref[taps - 1 - k if flip else k], line)
    line = line / jnp.full((8, 256), total, jnp.float32)
    return pltpu.roll(jnp.broadcast_to(line[:1], (rows, 256)), 0, 1, stride=1, stride_axis=0)


def x_band(psf_ref, flip):
    m = band(psf_ref, -15, not flip, 128)
    return m[:, :128], m[:, 128:]


def prep_kernel(psf_y_ref, psf_z_ref, yf_ref, ya_ref, zo_ref, zl_ref, zh_ref, za_ref):
    yf_ref[...] = band(psf_y_ref, -15, True, 128)[:, :128]
    ya_ref[...] = band(psf_y_ref, -15, False, 128)[:, :128]
    fwd = band(psf_z_ref, 1, False, 128)
    zl_ref[...] = fwd[:64, :64]
    zo_ref[...] = fwd[:, 64:128]
    zh_ref[...] = fwd[64:, 128:192]
    za_ref[...] = band(psf_z_ref, 1, True, 64)[:, :128]


def prepare(psf_y, psf_z):
    out = [(128, 128), (128, 128), (128, 64), (64, 64), (64, 64), (64, 128)]
    return call(prep_kernel, out, [psf_y, psf_z], 1, "prepare")


def blur_lanes(tiles, near, far):
    lane = lax.broadcasted_iota(jnp.int32, tiles[0].shape, 1)
    zero = jnp.zeros_like(tiles[0])
    near, far = split(near), split(far)
    out = []
    for t in range(8):
        after = tiles[t + 1] if t < 7 else zero
        before = tiles[t - 1] if t > 0 else zero
        out.append(dot(split(tiles[t]), near) + dot(split(jnp.where(lane < 64, after, before)), far))
    return out


def rows_at(t, i, per=16, offset=0):
    block = 8 * t + i
    return x_index(block // 2, block % 2) * per + offset


def write_columns(out_ref, t, tile, per=16, offset=0):
    turned = tile.T
    for i in range(8):
        at = rows_at(t, i, per, offset)
        out_ref[at : at + 16, :] = turned[16 * i : 16 * i + 16, :]


def first_kernel(psf_x_ref, est_hbm, obs_hbm, out_ref, est_ref, obs_ref, sems):
    copies = [
        pltpu.make_async_copy(
            src.at[pl.ds(16 * i, 16), :], dst.at[pl.ds(16 * i, 16), :], sems.at[8 * n + i]
        )
        for n, (src, dst) in enumerate(((est_hbm, est_ref), (obs_hbm, obs_ref)))
        for i in range(8)
    ]
    for copy in copies:
        copy.start()
    near, far = x_band(psf_x_ref, False)
    for copy in copies[:8]:
        copy.wait()
    blurred = blur_lanes([est_ref[:, 128 * t : 128 * t + 128] for t in range(8)], near, far)
    for t in range(8):
        write_columns(out_ref, t, blurred[t], 32, 0)
    for copy in copies[8:]:
        copy.wait()
    for t in range(8):
        write_columns(out_ref, t, obs_ref[:, 128 * t : 128 * t + 128], 32, 16)


def turn_kernel(in_ref, out_ref):
    for t in range(8):
        write_columns(out_ref, t, in_ref[:, 128 * t : 128 * t + 128])


def last_kernel(psf_x_ref, back_ref, est_ref, out_ref):
    near, far = x_band(psf_x_ref, True)

    def tile(ref, t):
        spots = [rows_at(t, i) for i in range(8)]
        return jnp.concatenate([ref[at : at + 16, :] for at in spots], axis=0).T

    blurred = blur_lanes([tile(back_ref, t) for t in range(8)], near, far)
    for t in range(8):
        out_ref[:, 128 * t : 128 * t + 128] = blurred[t] * tile(est_ref, t)


def swap_groups(tiles):
    group = lax.broadcasted_iota(jnp.int32, (8, 128), 1) // 16
    tiles = [tiles[0]] + [pltpu.roll(tiles[i], 16 * i, 1) for i in range(1, 8)]
    for b in (1, 2, 4):
        taken = (group & b) != 0
        tiles = [jnp.where(taken, tiles[(i + b) % 8], tiles[i]) for i in range(8)]
    return [tiles[0]] + [pltpu.roll(tiles[8 - i], 128 - 16 * i, 1) for i in range(1, 8)]


def unpack_one(in_ref, out_ref, rows_ref, per, offset):
    for zc in range(8):
        for half in range(2):
            at = zc * 8 * per + half * 8 + offset
            tiles = swap_groups([in_ref[at + per * i : at + per * i + 8, :] for i in range(8)])
            at = zc * 128 + half * 8
            for i in range(8):
                rows_ref[at + 16 * i : at + 16 * i + 8, :] = tiles[i]
    for zc in range(8):
        for x in range(16):
            out_ref[x, zc * 8 : zc * 8 + 8, :] = rows_ref[pl.ds(zc * 128 + x, 8, stride=16), :]


def unpack_kernel(in_ref, out_ref, rows_ref):
    unpack_one(in_ref, out_ref, rows_ref, 16, 0)


def arrive_kernel(in_ref, y_ref, up_ref, down_ref, rows_ref, more_ref, obs_ref):
    unpack_one(in_ref, up_ref, rows_ref, 32, 0)
    unpack_one(in_ref, obs_ref, more_ref, 32, 16)
    y = split(y_ref[...])
    for x in range(16):
        v = dot(split(up_ref[x, :64, :]), y)
        up_ref[x, :64, :] = v
        down_ref[x, :64, :] = v
        up_ref[x, 64:, :] = obs_ref[x, 32:, :]
        down_ref[x, 64:, :] = obs_ref[x, :32, :]


def pack_one(in_ref, out_ref, rows_ref, per, offset):
    for zc in range(8):
        for x in range(16):
            rows_ref[pl.ds(zc * 128 + x, 8, stride=16), :] = in_ref[x, zc * 8 : zc * 8 + 8, :]
    for zc in range(8):
        for half in range(2):
            at = zc * 128 + half * 8
            tiles = swap_groups([rows_ref[at + 16 * i : at + 16 * i + 8, :] for i in range(8)])
            at = zc * 8 * per + half * 8 + offset
            for i in range(8):
                out_ref[at + per * i : at + per * i + 8, :] = tiles[i]


def pack_kernel(in_ref, out_ref, rows_ref):
    pack_one(in_ref, out_ref, rows_ref, 16, 0)


def exchange(rows):
    per = rows.shape[0] // 64
    t = lax.all_to_all(rows.reshape(64, per, 128), SLAB, 0, 0, tiled=True)
    return t.reshape(rows.shape)


def tap_vectors(psf_ref, flip):
    total = psf_ref[0]
    for k in range(1, 31):
        total = total + psf_ref[k]
    scale = 1.0 / jnp.full((8, 128), total, jnp.float32)
    return [psf_ref[30 - k if flip else k] * scale for k in range(31)]


def add_block(w, ref, z, acc, shift):
    for j in range(16):
        v = ref[j, z, :]
        for i in range(16):
            k = j + shift - i + 15
            if 0 <= k <= 30:
                p = w[k] * v
                acc[i] = p if acc[i] is None else acc[i] + p
    return acc


def over_planes(body):
    def step(t, _):
        body(pl.ds(pl.multiple_of(t * 8, 8), 8))
        return 0

    lax.fori_loop(0, 8, step, 0)


def own_x_kernel(flip, psf_ref, own_ref, out_ref):
    w = tap_vectors(psf_ref, flip)

    def body(z):
        acc = add_block(w, own_ref, z, [None] * 16, 0)
        for i in range(16):
            out_ref[i, z, :] = acc[i]

    over_planes(body)


def add_side(w, core_ref, part_ref, side_ref, shift, finish):
    def run(shift):
        def body(z):
            acc = [part_ref[i, z, :] for i in range(16)]
            finish(z, add_block(w, side_ref, z, acc, shift))

        over_planes(body)

    pl.when(core_ref[0] == 0)(lambda: run(shift))
    pl.when(core_ref[0] != 0)(lambda: run(-shift))


def side_kernel(flip, shift, psf_ref, core_ref, part_ref, side_ref, out_ref):
    def finish(z, acc):
        for i in range(16):
            out_ref[i, z, :] = acc[i]

    add_side(tap_vectors(psf_ref, flip), core_ref, part_ref, side_ref, shift, finish)


def update_kernel(flip, psf_ref, core_ref, part_ref, side_ref, est_ref, y_ref, new_ref, out_ref):
    def finish(z, acc):
        for i in range(16):
            new_ref[i, z, :] = est_ref[i, z, :] * acc[i]

    add_side(tap_vectors(psf_ref, flip), core_ref, part_ref, side_ref, 16, finish)
    y = split(y_ref[...])
    for i in range(16):
        out_ref[i] = dot(split(new_ref[i]), y)


def x_halo(v, psf, core, flip, ride=None):
    passed = lax.ppermute(v, SLAB, NEXT)
    swapped = lax.ppermute(v, "c", SWAP)
    part = call(functools.partial(own_x_kernel, flip), BLOCK, [psf, v], 1.3, "x_own")
    if ride is not None:
        ride, part = lax.optimization_barrier((ride, part))
        ride = exchange(ride)
    kernel = functools.partial(side_kernel, flip, -16)
    part = call(kernel, BLOCK, [psf, core, part, passed], 1, "x_passed")
    return part, swapped, ride


def ratio_kernel(
    slab_ref, v_ref, below_ref, above_ref, obs_ref, zo_ref, zl_ref, zh_ref, za_ref, ya_ref,
    out_ref, ratio_ref
):
    has_below = jnp.full((32, 128), slab_ref[0], jnp.int32) > 0
    has_above = jnp.full((32, 128), slab_ref[0], jnp.int32) < 7
    own, low_band, high_band = split(zo_ref[...]), split(zl_ref[...]), split(zh_ref[...])
    adjoint, y = split(za_ref[...]), split(ya_ref[...])
    for x in range(16):
        part = dot(own, split(v_ref[x, :64, :]))
        low = part[:64] + dot(low_band, split(below_ref[x, :64, :]))
        high = part[64:] + dot(high_band, split(above_ref[x, :64, :]))
        ratio_ref[x, :32, :] = jnp.where(has_below, obs_ref[x, :32, :] / low[:32], 0.0)
        ratio_ref[x, 32:64, :] = obs_ref[x, 32:64, :] / low[32:]
        ratio_ref[x, 64:96, :] = obs_ref[x, 64:96, :] / high[:32]
        ratio_ref[x, 96:, :] = jnp.where(has_above, obs_ref[x, 96:, :] / high[32:], 0.0)
    for x in range(16):
        out_ref[x] = dot(split(dot(adjoint, split(ratio_ref[x]))), y)


def first_ratio_kernel(
    slab_ref, up_ref, down_ref, below_ref, above_ref, zo_ref, zl_ref, zh_ref, za_ref, ya_ref,
    out_ref, obs_ref, ratio_ref
):
    parts = (below_ref, down_ref, up_ref, above_ref)
    for i in range(4):
        obs_ref[:, 32 * i : 32 * i + 32, :] = parts[i][:, 64:, :]
    ratio_kernel(
        slab_ref, up_ref, below_ref, above_ref, obs_ref, zo_ref, zl_ref, zh_ref, za_ref, ya_ref,
        out_ref, ratio_ref
    )


def per_device(observed, estimate, psf_y, psf_x, psf_z):
    core = lax.axis_index("c").reshape(1)
    slab = lax.axis_index("z").reshape(1)
    est0 = estimate.reshape(128, 1024)

    first = pl.pallas_call(
        first_kernel,
        out_shape=pltpu.VMEM((2048, 128), jnp.float32),
        in_specs=[SMEM, HBM, HBM],
        out_specs=VMEM,
        scratch_shapes=[
            pltpu.VMEM((128, 1024), jnp.float32),
            pltpu.VMEM((128, 1024), jnp.float32),
            pltpu.SemaphoreType.DMA((16,)),
        ],
        compiler_params=pltpu.CompilerParams(vmem_limit_bytes=LIMIT),
        name="first",
    )(
        psf_x,
        pltpu.with_memory_space_constraint(est0, pltpu.HBM),
        pltpu.with_memory_space_constraint(observed.reshape(128, 1024), pltpu.HBM),
    )
    arrived = exchange(first)
    yf, ya, zo, zl, zh, za = prepare(psf_y, psf_z)
    turned = call(turn_kernel, ROWS, [est0], 1, "turn", free=(0,))

    mats = [zo, zl, zh, za, ya]
    out = [(16, 96, 128), (16, 96, 128)]
    up, down = call(arrive_kernel, out, [arrived, yf], 2, "arrive", [ROWS, ROWS, BLOCK])
    below = lax.ppermute(up, "z", UP)
    above = lax.ppermute(down, "z", DOWN)
    turned, up = lax.optimization_barrier((turned, up))
    rode = exchange(turned)
    back, obs = call(
        first_ratio_kernel,
        [BLOCK, (16, 128, 128)],
        [slab, up, down, below, above, *mats],
        100,
        "first_ratio",
        [(16, 128, 128)],
    )
    est = call(unpack_kernel, BLOCK, [rode], 1, "unpack", [ROWS])
    part, swapped, _ = x_halo(back, psf_x, core, True)
    est, v = call(
        functools.partial(update_kernel, True),
        [BLOCK, BLOCK],
        [psf_x, core, part, swapped, est, yf],
        2,
        "update",
    )
    est_rows = call(pack_kernel, ROWS, [est], 1, "pack_est", [ROWS])
    part, swapped, est_rows = x_halo(v, psf_x, core, False, est_rows)
    kernel = functools.partial(side_kernel, False, 16)
    v = call(kernel, BLOCK, [psf_x, core, part, swapped], 1, "x_swapped")

    below = lax.ppermute(v, "z", UP)
    above = lax.ppermute(v, "z", DOWN)
    back = call(
        ratio_kernel, BLOCK, [slab, v, below, above, obs, *mats], 4, "ratio", [(16, 128, 128)]
    )
    rows = exchange(call(pack_kernel, ROWS, [back], 1, "pack_back", [ROWS]))
    out = call(last_kernel, (128, 1024), [psf_x, rows, est_rows], 4, "last", free_out=True)
    return out.reshape(8, 16, 1024)


def solution(mesh):
    fine = Mesh(mesh.devices.reshape(8, 4, 2, 4, 2), ("z", "x", "yl", "yh", "c"))
    spec = P(("z", "x", "yl"), ("yh", "c"), None)
    return jax.shard_map(
        per_device,
        mesh=fine,
        in_specs=(spec, spec, P(), P(), P()),
        out_specs=spec,
        check_vma=False,
    )
```

time: 176 us -> 160 us (0.909)
  starting transfers between devices: 61.2 us -> 51.1 us
  local copies, waits for them, and re-layouts: 6.21 us -> 1.69 us
  Pallas kernels: 26.8 us -> 24.4 us
    ppermute x6 -> x4, starting transfers between devices: 18 us -> 11.9 us  [the longest x1 4.89 us: per_device(): below = lax.ppermute(up, 'z', UP)]
    ppermute x6 -> x4, waiting for transfers between devices: 16 us -> 21.3 us  [the longest x1 9.91 us: per_device(): above = lax.ppermute(v, 'z', DOWN)]
    all_to_all x3, starting transfers between devices: 30.9 us -> 25.9 us  [exchange(): t = lax.all_to_all(rows.reshape(64, per, 128), SLAB, 0, 0, tiled=True)]
    ppermute x2, waiting for transfers between devices: 6.72 us -> 2.81 us  [x_halo(): passed = lax.ppermute(v, SLAB, NEXT)]
    unnamed x17 -> x12, local copies, waits for them, and re-layouts: 5.37 us -> 1.69 us
    ppermute x2, starting transfers between devices: 6.88 us -> 9.42 us  [x_halo(): passed = lax.ppermute(v, SLAB, NEXT)]
    pallas_call x16, Pallas kernels: 26.8 us -> 24.4 us  [the longest x15 20.7 us: call(): pl.pallas_call(kernel, out_shape=jax.tree.map(lambda s: kind(s, jnp.float...]
  transfers between devices with their start and end apart: 13 -> 11, of which waited for: 7 -> 6; matrix products, arithmetic and copies ran while one was open for 0% -> 0% of each run, Pallas kernels for 9% -> 10%
where the time goes in v5:
time: 160 us; the launch traced here: 158 us
  waiting for transfers between devices  51.4 us (32%)
  starting transfers between devices  51.1 us (32%)
  blocking collectives  28.7 us (18%)
  Pallas kernels  24.4 us (15%)
  local copies, waits for them, and re-layouts  1.69 us (1%)
    all_to_all x1, blocking collectives, exchange(): t = lax.all_to_all(rows.reshape(64, per, 128), SLAB, 0, 0, tiled=True)  28.7 us
    all_to_all x3, waiting for transfers between devices, exchange(): t = lax.all_to_all(rows.reshape(64, per, 128), SLAB, 0, 0, tiled=True)  27.4 us
    all_to_all x3, starting transfers between devices, exchange(): t = lax.all_to_all(rows.reshape(64, per, 128), SLAB, 0, 0, tiled=True)  25.9 us
    pallas_call x15, Pallas kernels, call(): pl.pallas_call(kernel, out_shape=jax.tree.map(lambda s: kind(s, jnp.float...  20.7 us
    ppermute x1, waiting for transfers between devices, per_device(): above = lax.ppermute(v, 'z', DOWN)  9.91 us
    ppermute x2, starting transfers between devices, x_halo(): passed = lax.ppermute(v, SLAB, NEXT)  9.42 us
    ppermute x1, waiting for transfers between devices, per_device(): below = lax.ppermute(up, 'z', UP)  5.69 us
    ppermute x1, starting transfers between devices, per_device(): below = lax.ppermute(up, 'z', UP)  4.89 us
  transfers between devices with their start and end apart: 11, of which 6 were waited for; matrix products, arithmetic and copies ran while one was open for 0% of the time, Pallas kernels for 10%

profile of v5, /device:TPU:1, one launch (start us, length us, event | category | flops | bytes accessed | tf_op | source)
XLA Modules:
  0.0 157.6 jit_solution(17714567446827513527)
XLA Ops:
  0.7 3.6 %first.1 = f32[2048,128]{1,0:T(8,128)} custom-call(f32[31]{0:T(128)S(1)} %copy-done.1, f32[128,1024]{1,0:T(8,128)} %bitcast.14, f32[128,1024]{1,0:T(8,128)} %bitcast.20), custom_call_target="tpu_custom_call" | custom-call | tf_op jit(solution)/shard_map/first/pallas_call | solution.py:346
  4.3 11.6 %all-to-all-start = ((f32[64,32,128]{2,1,0:T(8,128)}), f32[64,32,128]{2,1,0:T(8,128)S(1)}, u32[]{:S(2)}, u32[]{:S(2)}) async-start(f32[64,32,128]{2,1,0:T(8,128)} %bitcast.4), calls=%async_computation | async-start | bytes 2097152 | tf_op jit(solution)/shard_map/all_to_all | solution.py:223
  16.8 27.3 %all-to-all-done = f32[64,32,128]{2,1,0:T(8,128)S(1)} async-done(((f32[64,32,128]{2,1,0:T(8,128)}), f32[64,32,128]{2,1,0:T(8,128)S(1)}, u32[]{:S(2)}, u32[]{:S(2)}) %all-to-all-start) | async-done | bytes 1048608 | tf_op jit(solution)/shard_map/all_to_all | solution.py:223
  44.2 1.6 arrive.1
  45.8 4.9 %collective-permute-start = (f32[16,96,128]{2,1,0:T(8,128)S(1)}, f32[16,96,128]{2,1,0:T(8,128)}, u32[]{:S(2)}, u32[]{:S(2)}) collective-permute-start(f32[16,96,128]{2,1,0:T(8,128)S(1)} %get-tuple-element.23.up_ref), channel_id=1, source_target_pairs={{0,64},{64,128},{128,192},{192,256},{256,320},{320,384},{384,448},... | collective-permute-start | bytes 2359304 | tf_op jit(solution)/shard_map/ppermute | solution.py:370
  50.6 1.3 collective-permute-start.1
  51.9 1.0 turn.1
  52.9 6.8 %all-to-all-start.1 = ((f32[64,16,128]{2,1,0:T(8,128)}), f32[64,16,128]{2,1,0:T(8,128)S(1)}, u32[]{:S(2)}, u32[]{:S(2)}) async-start(f32[64,16,128]{2,1,0:T(8,128)} %bitcast.6), calls=%async_computation.1 | async-start | bytes 1048576 | tf_op jit(solution)/shard_map/all_to_all | solution.py:223
  59.8 5.7 %collective-permute-done.below_ref = f32[16,96,128]{2,1,0:T(8,128)} collective-permute-done((f32[16,96,128]{2,1,0:T(8,128)S(1)}, f32[16,96,128]{2,1,0:T(8,128)}, u32[]{:S(2)}, u32[]{:S(2)}) %collective-permute-start) | collective-permute-done | bytes 786464 | tf_op jit(solution)/shard_map/ppermute | solution.py:370
  65.5 4.8 %collective-permute-done.1.above_ref = f32[16,96,128]{2,1,0:T(8,128)} collective-permute-done((f32[16,96,128]{2,1,0:T(8,128)S(1)}, f32[16,96,128]{2,1,0:T(8,128)}, u32[]{:S(2)}, u32[]{:S(2)}) %collective-permute-start.1) | collective-permute-done | bytes 786464 | tf_op jit(solution)/shard_map/ppermute | solution.py:371
  70.3 3.3 %first_ratio.1 = (f32[16,64,128]{2,1,0:T(8,128)S(1)}, f32[16,128,128]{2,1,0:T(8,128)S(1)}) custom-call(s32[1]{0:T(128)} %bitcast.slab_ref, f32[16,96,128]{2,1,0:T(8,128)S(1)} %get-tuple-element.23.up_ref, f32[16,96,128]{2,1,0:T(8,128)S(1)} %get-tuple-element.24.down_ref, f32[16,96,128]{2,1,0:T(8,128)} %collective-permute-done.below_ref, ...), custom_call_target="tpu_custom_call" | custom-call | flops 99999997952 | bytes 300000000 | tf_op jit(solution)/shard_map/first_ratio/pallas_call | solution.py:42
  73.6 1.0 copy-done.4
  74.6 5.7 %collective-permute-start.2 = (f32[16,64,128]{2,1,0:T(8,128)S(1)}, f32[16,64,128]{2,1,0:T(8,128)S(1)}, u32[]{:S(2)}, u32[]{:S(2)}) collective-permute-start(f32[16,64,128]{2,1,0:T(8,128)S(1)} %get-tuple-element.30.own_ref), channel_id=1, source_target_pairs={{8,1},{2,9},{10,3},{4,11},{12,5},{6,13},{14,7},{16,15},{24,17},{18... | collective-permute-start | bytes 1572872 | tf_op jit(solution)/shard_map/ppermute | solution.py:297
  80.3 1.9 %collective-permute-start.3 = (f32[16,64,128]{2,1,0:T(8,128)S(1)}, f32[16,64,128]{2,1,0:T(8,128)S(1)}, u32[]{:S(2)}, u32[]{:S(2)}) collective-permute-start(f32[16,64,128]{2,1,0:T(8,128)S(1)} %get-tuple-element.30.own_ref), channel_id=1, source_target_pairs={{0,1},{1,0},{2,3},{3,2},{4,5},{5,4},{6,7},{7,6},{8,9},{9,8},{10,11... | collective-permute-start | bytes 1572872 | tf_op jit(solution)/shard_map/ppermute | solution.py:298
  82.2 1.2 x_own.2.part_ref
  83.5 0.9 unpack.1.est_ref
  84.4 2.8 %collective-permute-done.2.side_ref = f32[16,64,128]{2,1,0:T(8,128)S(1)} collective-permute-done((f32[16,64,128]{2,1,0:T(8,128)S(1)}, f32[16,64,128]{2,1,0:T(8,128)S(1)}, u32[]{:S(2)}, u32[]{:S(2)}) %collective-permute-start.2) | collective-permute-done | bytes 524320 | tf_op jit(solution)/shard_map/ppermute | solution.py:297
  87.2 0.9 x_passed.2.part_ref
  88.1 1.5 update.1
  89.6 3.7 %collective-permute-start.4 = (f32[16,64,128]{2,1,0:T(8,128)S(1)}, f32[16,64,128]{2,1,0:T(8,128)S(1)}, u32[]{:S(2)}, u32[]{:S(2)}) collective-permute-start(f32[16,64,128]{2,1,0:T(8,128)S(1)} %get-tuple-element.33.own_ref), channel_id=1, source_target_pairs={{8,1},{2,9},{10,3},{4,11},{12,5},{6,13},{14,7},{16,15},{24,17},{18... | collective-permute-start | bytes 1572872 | tf_op jit(solution)/shard_map/ppermute | solution.py:297
  93.3 1.9 %collective-permute-start.5 = (f32[16,64,128]{2,1,0:T(8,128)S(1)}, f32[16,64,128]{2,1,0:T(8,128)S(1)}, u32[]{:S(2)}, u32[]{:S(2)}) collective-permute-start(f32[16,64,128]{2,1,0:T(8,128)S(1)} %get-tuple-element.33.own_ref), channel_id=1, source_target_pairs={{0,1},{1,0},{2,3},{3,2},{4,5},{5,4},{6,7},{7,6},{8,9},{9,8},{10,11... | collective-permute-start | bytes 1572872 | tf_op jit(solution)/shard_map/ppermute | solution.py:298
  95.2 1.6 %pack_est.1 = f32[1024,128]{1,0:T(8,128)} custom-call(f32[16,64,128]{2,1,0:T(8,128)S(1)} %get-tuple-element.32.in_ref), custom_call_target="tpu_custom_call" | custom-call | flops 1000000000 | bytes 3000000 | tf_op jit(solution)/shard_map/pack_est/pallas_call | solution.py:42
  96.9 1.2 x_own.3.part_ref
  98.1 7.5 %all-to-all-start.3 = ((f32[64,16,128]{2,1,0:T(8,128)}), f32[64,16,128]{2,1,0:T(8,128)S(1)}, u32[]{:S(2)}, u32[]{:S(2)}) async-start(f32[64,16,128]{2,1,0:T(8,128)} %bitcast.10), calls=%async_computation.3 | async-start | bytes 1048576 | tf_op jit(solution)/shard_map/all_to_all | solution.py:223
  105.6 0.9 x_passed.3.part_ref
  106.6 0.9 x_swapped.1.v_ref
  107.5 1.3 collective-permute-start.7
  108.8 4.4 %collective-permute-start.6 = (f32[16,64,128]{2,1,0:T(8,128)S(1)}, f32[16,64,128]{2,1,0:T(8,128)S(1)}, u32[]{:S(2)}, u32[]{:S(2)}) collective-permute-start(f32[16,64,128]{2,1,0:T(8,128)S(1)} %x_swapped.1.v_ref), channel_id=1, source_target_pairs={{0,64},{64,128},{128,192},{192,256},{256,320},{320,384},{384,448},... | collective-permute-start | bytes 1572872 | tf_op jit(solution)/shard_map/ppermute | solution.py:396
  113.2 9.9 %collective-permute-done.7.above_ref = f32[16,64,128]{2,1,0:T(8,128)S(1)} collective-permute-done((f32[16,64,128]{2,1,0:T(8,128)S(1)}, f32[16,64,128]{2,1,0:T(8,128)S(1)}, u32[]{:S(2)}, u32[]{:S(2)}) %collective-permute-start.7) | collective-permute-done | bytes 524320 | tf_op jit(solution)/shard_map/ppermute | solution.py:397
  124.0 1.9 %ratio.1.in_ref = f32[16,64,128]{2,1,0:T(8,128)S(1)} custom-call(s32[1]{0:T(128)} %bitcast.slab_ref, f32[16,64,128]{2,1,0:T(8,128)S(1)} %x_swapped.1.v_ref, f32[16,64,128]{2,1,0:T(8,128)S(1)} %collective-permute-done.6.below_ref, f32[16,64,128]{2,1,0:T(8,128)S(1)} %collective-permute-done.7.above_ref, f32[16,128,128]{2,1,0:T(8,128)S(1)} %copy-done.5, ...), custom_call_target="tpu_custom_call" | custom-call | flops 4000000000 | bytes 12000000 | tf_op jit(solution)/shard_map/ratio/pallas_call | solution.py:42
  126.8 28.7 %all_to_all.20 = f32[64,16,128]{2,1,0:T(8,128)S(1)} all-to-all(f32[64,16,128]{2,1,0:T(8,128)S(1)} %bitcast.18), channel_id=1, replica_groups=mesh['z'=8,'x'=4,'yl'=2,'yh'=4,'c'=2] {'x','yl','yh','c'}, dimensions={0} | all-to-all | bytes 1048576 | tf_op jit(solution)/shard_map/all_to_all | solution.py:223
  155.5 2.0 %last.1 = f32[128,1024]{1,0:T(8,128)} custom-call(f32[31]{0:T(128)S(1)} %copy-done.1, f32[1024,128]{1,0:T(8,128)S(1)} %bitcast.19, f32[1024,128]{1,0:T(8,128)S(1)} %bitcast.16), custom_call_target="tpu_custom_call" | custom-call | flops 4000000000 | bytes 12000000 | tf_op jit(solution)/shard_map/last/pallas_call | solution.py:42
  (19 shorter events, 3.2 us)
Async XLA Ops:
  0.0 0.7 copy-start.1
  4.3 11.7 %copy-start.2 = (f32[31]{0:T(128)S(1)}, f32[31]{0:T(128)}, u32[]{:S(2)}) copy-start(f32[31]{0:T(128)} %psf_y_ref.1) | copy-start | bytes 376
  4.3 11.7 %copy-start.3 = (f32[63]{0:T(128)S(1)}, f32[63]{0:T(128)}, u32[]{:S(2)}) copy-start(f32[63]{0:T(128)} %psf_z_ref.1) | copy-start | bytes 760
  4.3 39.9 %all-to-all-start = ((f32[64,32,128]{2,1,0:T(8,128)}), f32[64,32,128]{2,1,0:T(8,128)S(1)}, u32[]{:S(2)}, u32[]{:S(2)}) async-start(f32[64,32,128]{2,1,0:T(8,128)} %bitcast.4), calls=%async_computation | async-start | bytes 2097152 | tf_op jit(solution)/shard_map/all_to_all | solution.py:223
  44.2 7.8 %copy-start = (f32[8,16,1024]{2,1,0:T(8,128)S(1)}, f32[8,16,1024]{2,1,0:T(8,128)}, u32[]{:S(2)}) copy-start(f32[8,16,1024]{2,1,0:T(8,128)} %param.6) | copy-start | bytes 1572868
  45.8 19.7 %collective-permute-start = (f32[16,96,128]{2,1,0:T(8,128)S(1)}, f32[16,96,128]{2,1,0:T(8,128)}, u32[]{:S(2)}, u32[]{:S(2)}) collective-permute-start(f32[16,96,128]{2,1,0:T(8,128)S(1)} %get-tuple-element.23.up_ref), channel_id=1, source_target_pairs={{0,64},{64,128},{128,192},{192,256},{256,320},{320,384},{384,448},... | collective-permute-start | bytes 2359304 | tf_op jit(solution)/shard_map/ppermute | solution.py:370
  50.6 19.6 %collective-permute-start.1 = (f32[16,96,128]{2,1,0:T(8,128)S(1)}, f32[16,96,128]{2,1,0:T(8,128)}, u32[]{:S(2)}, u32[]{:S(2)}) collective-permute-start(f32[16,96,128]{2,1,0:T(8,128)S(1)} %get-tuple-element.24.down_ref), channel_id=1, source_target_pairs={{64,0},{128,64},{192,128},{256,192},{320,256},{384,320},{448,384},... | collective-permute-start | bytes 2359304 | tf_op jit(solution)/shard_map/ppermute | solution.py:371
  52.9 30.5 %all-to-all-start.1 = ((f32[64,16,128]{2,1,0:T(8,128)}), f32[64,16,128]{2,1,0:T(8,128)S(1)}, u32[]{:S(2)}, u32[]{:S(2)}) async-start(f32[64,16,128]{2,1,0:T(8,128)} %bitcast.6), calls=%async_computation.1 | async-start | bytes 1048576 | tf_op jit(solution)/shard_map/all_to_all | solution.py:223
  73.6 1.0 copy-start.4
  74.6 12.6 %collective-permute-start.2 = (f32[16,64,128]{2,1,0:T(8,128)S(1)}, f32[16,64,128]{2,1,0:T(8,128)S(1)}, u32[]{:S(2)}, u32[]{:S(2)}) collective-permute-start(f32[16,64,128]{2,1,0:T(8,128)S(1)} %get-tuple-element.30.own_ref), channel_id=1, source_target_pairs={{8,1},{2,9},{10,3},{4,11},{12,5},{6,13},{14,7},{16,15},{24,17},{18... | collective-permute-start | bytes 1572872 | tf_op jit(solution)/shard_map/ppermute | solution.py:297
  80.3 7.8 %collective-permute-start.3 = (f32[16,64,128]{2,1,0:T(8,128)S(1)}, f32[16,64,128]{2,1,0:T(8,128)S(1)}, u32[]{:S(2)}, u32[]{:S(2)}) collective-permute-start(f32[16,64,128]{2,1,0:T(8,128)S(1)} %get-tuple-element.30.own_ref), channel_id=1, source_target_pairs={{0,1},{1,0},{2,3},{3,2},{4,5},{5,4},{6,7},{7,6},{8,9},{9,8},{10,11... | collective-permute-start | bytes 1572872 | tf_op jit(solution)/shard_map/ppermute | solution.py:298
  89.6 16.0 %collective-permute-start.4 = (f32[16,64,128]{2,1,0:T(8,128)S(1)}, f32[16,64,128]{2,1,0:T(8,128)S(1)}, u32[]{:S(2)}, u32[]{:S(2)}) collective-permute-start(f32[16,64,128]{2,1,0:T(8,128)S(1)} %get-tuple-element.33.own_ref), channel_id=1, source_target_pairs={{8,1},{2,9},{10,3},{4,11},{12,5},{6,13},{14,7},{16,15},{24,17},{18... | collective-permute-start | bytes 1572872 | tf_op jit(solution)/shard_map/ppermute | solution.py:297
  93.3 13.2 %collective-permute-start.5 = (f32[16,64,128]{2,1,0:T(8,128)S(1)}, f32[16,64,128]{2,1,0:T(8,128)S(1)}, u32[]{:S(2)}, u32[]{:S(2)}) collective-permute-start(f32[16,64,128]{2,1,0:T(8,128)S(1)} %get-tuple-element.33.own_ref), channel_id=1, source_target_pairs={{0,1},{1,0},{2,3},{3,2},{4,5},{5,4},{6,7},{7,6},{8,9},{9,8},{10,11... | collective-permute-start | bytes 1572872 | tf_op jit(solution)/shard_map/ppermute | solution.py:298
  98.1 28.7 %all-to-all-start.3 = ((f32[64,16,128]{2,1,0:T(8,128)}), f32[64,16,128]{2,1,0:T(8,128)S(1)}, u32[]{:S(2)}, u32[]{:S(2)}) async-start(f32[64,16,128]{2,1,0:T(8,128)} %bitcast.10), calls=%async_computation.3 | async-start | bytes 1048576 | tf_op jit(solution)/shard_map/all_to_all | solution.py:223
  106.5 17.5 %copy-start.5 = (f32[16,128,128]{2,1,0:T(8,128)S(1)}, f32[16,128,128]{2,1,0:T(8,128)}, u32[]{:S(2)}) copy-start(f32[16,128,128]{2,1,0:T(8,128)} %copy-done.4) | copy-start | bytes 3145732
  107.5 15.6 %collective-permute-start.7 = (f32[16,64,128]{2,1,0:T(8,128)S(1)}, f32[16,64,128]{2,1,0:T(8,128)S(1)}, u32[]{:S(2)}, u32[]{:S(2)}) collective-permute-start(f32[16,64,128]{2,1,0:T(8,128)S(1)} %x_swapped.1.v_ref), channel_id=1, source_target_pairs={{64,0},{128,64},{192,128},{256,192},{320,256},{384,320},{448,384},... | collective-permute-start | bytes 1572872 | tf_op jit(solution)/shard_map/ppermute | solution.py:397
  108.8 15.2 %collective-permute-start.6 = (f32[16,64,128]{2,1,0:T(8,128)S(1)}, f32[16,64,128]{2,1,0:T(8,128)S(1)}, u32[]{:S(2)}, u32[]{:S(2)}) collective-permute-start(f32[16,64,128]{2,1,0:T(8,128)S(1)} %x_swapped.1.v_ref), channel_id=1, source_target_pairs={{0,64},{64,128},{128,192},{192,256},{256,320},{320,384},{384,448},... | collective-permute-start | bytes 1572872 | tf_op jit(solution)/shard_map/ppermute | solution.py:396

commit v6 on v5

--- a/solution.py
+++ b/solution.py
@@ -33,24 +33,26 @@
     return isinstance(s, tuple)
 
 
-def call(kernel, out, args, us, name, scratch=(), free=(), free_out=False):
-    pinned = [
-        a if a.ndim == 1 or i in free else pltpu.with_memory_space_constraint(a, pltpu.VMEM)
-        for i, a in enumerate(args)
-    ]
-    kind = jax.ShapeDtypeStruct if free_out else pltpu.VMEM
+def call(kernel, out, args, us, name, scratch=(), save=None):
+    args = [a if a.ndim == 1 else pltpu.with_memory_space_constraint(a, pltpu.VMEM) for a in args]
+    shapes = jax.tree.map(lambda s: pltpu.VMEM(s, jnp.float32), out, is_leaf=is_shape)
+    specs = jax.tree.map(lambda s: VMEM, out, is_leaf=is_shape)
+    scratch = [pltpu.VMEM(s, jnp.float32) for s in scratch]
+    if save:
+        shapes, specs = [shapes, pltpu.HBM(save, jnp.float32)], [specs, HBM]
+        scratch.append(pltpu.SemaphoreType.DMA((2,)))
     return pl.pallas_call(
         kernel,
-        out_shape=jax.tree.map(lambda s: kind(s, jnp.float32), out, is_leaf=is_shape),
+        out_shape=shapes,
         in_specs=[SMEM if a.ndim == 1 else VMEM for a in args],
-        out_specs=jax.tree.map(lambda s: VMEM, out, is_leaf=is_shape),
-        scratch_shapes=[pltpu.VMEM(s, jnp.float32) for s in scratch],
+        out_specs=specs,
+        scratch_shapes=scratch,
         cost_estimate=pl.CostEstimate(
             flops=int(us * 1e9), bytes_accessed=int(us * 3e6), transcendentals=0
         ),
         compiler_params=pltpu.CompilerParams(vmem_limit_bytes=LIMIT),
         name=name,
-    )(*pinned)
+    )(*args)
 
 
 def split(m):
@@ -85,9 +87,12 @@
     return m[:, :128], m[:, 128:]
 
 
-def prep_kernel(psf_y_ref, psf_z_ref, yf_ref, ya_ref, zo_ref, zl_ref, zh_ref, za_ref):
+def prep_kernel(
+    psf_y_ref, psf_x_ref, psf_z_ref, yf_ref, ya_ref, xn_ref, xf_ref, zo_ref, zl_ref, zh_ref, za_ref
+):
     yf_ref[...] = band(psf_y_ref, -15, True, 128)[:, :128]
     ya_ref[...] = band(psf_y_ref, -15, False, 128)[:, :128]
+    xn_ref[...], xf_ref[...] = x_band(psf_x_ref, True)
     fwd = band(psf_z_ref, 1, False, 128)
     zl_ref[...] = fwd[:64, :64]
     zo_ref[...] = fwd[:, 64:128]
@@ -95,9 +100,9 @@
     za_ref[...] = band(psf_z_ref, 1, True, 64)[:, :128]
 
 
-def prepare(psf_y, psf_z):
-    out = [(128, 128), (128, 128), (128, 64), (64, 64), (64, 64), (64, 128)]
-    return call(prep_kernel, out, [psf_y, psf_z], 1, "prepare")
+def prepare(psf_y, psf_x, psf_z):
+    out = [(128, 128)] * 4 + [(128, 64), (64, 64), (64, 64), (64, 128)]
+    return call(prep_kernel, out, [psf_y, psf_x, psf_z], 1, "prepare")
 
 
 def blur_lanes(tiles, near, far):
@@ -124,43 +129,63 @@
         out_ref[at : at + 16, :] = turned[16 * i : 16 * i + 16, :]
 
 
-def first_kernel(psf_x_ref, est_hbm, obs_hbm, out_ref, est_ref, obs_ref, sems):
-    copies = [
-        pltpu.make_async_copy(
-            src.at[pl.ds(16 * i, 16), :], dst.at[pl.ds(16 * i, 16), :], sems.at[8 * n + i]
-        )
-        for n, (src, dst) in enumerate(((est_hbm, est_ref), (obs_hbm, obs_ref)))
-        for i in range(8)
-    ]
-    for copy in copies:
-        copy.start()
+def first_kernel(psf_x_hbm, est_hbm, obs_hbm, out_ref, est_ref, obs_ref, psf_x_ref, sems):
+    taps = pltpu.make_async_copy(psf_x_hbm, psf_x_ref, sems.at[16])
+    taps.start()
+    copies = []
+    for n, (src, dst) in enumerate(((est_hbm, est_ref), (obs_hbm, obs_ref))):
+        for t in range(8):
+            spot = pl.ds(128 * t, 128)
+            copies.append(
+                pltpu.make_async_copy(src.at[:, spot], dst.at[:, spot], sems.at[8 * n + t])
+            )
+            copies[-1].start()
+    taps.wait()
     near, far = x_band(psf_x_ref, False)
     for copy in copies[:8]:
         copy.wait()
     blurred = blur_lanes([est_ref[:, 128 * t : 128 * t + 128] for t in range(8)], near, far)
     for t in range(8):
         write_columns(out_ref, t, blurred[t], 32, 0)
-    for copy in copies[8:]:
-        copy.wait()
     for t in range(8):
+        copies[8 + t].wait()
         write_columns(out_ref, t, obs_ref[:, 128 * t : 128 * t + 128], 32, 16)
 
 
-def turn_kernel(in_ref, out_ref):
+def save_observed(low_ref, high_ref, out_hbm, sems):
+    copies = [
+        pltpu.make_async_copy(
+            ref.at[:, pl.ds(64, 32), :], out_hbm.at[:, pl.ds(32 * i, 32), :], sems.at[i]
+        )
+        for i, ref in enumerate((low_ref, high_ref))
+    ]
+    for copy in copies:
+        copy.start()
+    return copies
+
+
+def turn_kernel(in_ref, down_ref, up_ref, out_ref, obs_hbm, sems):
+    copies = save_observed(down_ref, up_ref, obs_hbm, sems)
     for t in range(8):
         write_columns(out_ref, t, in_ref[:, 128 * t : 128 * t + 128])
-
-
-def last_kernel(psf_x_ref, back_ref, est_ref, out_ref):
-    near, far = x_band(psf_x_ref, True)
-
+    for copy in copies:
+        copy.wait()
+
+
+def last_kernel(back_ref, est_ref, near_ref, far_ref, out_hbm, out_ref, sems):
     def tile(ref, t):
         spots = [rows_at(t, i) for i in range(8)]
         return jnp.concatenate([ref[at : at + 16, :] for at in spots], axis=0).T
 
-    blurred = blur_lanes([tile(back_ref, t) for t in range(8)], near, far)
+    blurred = blur_lanes([tile(back_ref, t) for t in range(8)], near_ref[...], far_ref[...])
+    copies = []
     for t in range(8):
-        out_ref[:, 128 * t : 128 * t + 128] = blurred[t] * tile(est_ref, t)
+        spot = pl.ds(128 * t, 128)
+        out_ref[:, spot] = blurred[t] * tile(est_ref, t)
+        copies.append(pltpu.make_async_copy(out_ref.at[:, spot], out_hbm.at[:, spot], sems.at[t]))
+        copies[t].start()
+    for copy in copies:
+        copy.wait()
 
 
 def swap_groups(tiles):
@@ -262,144 +287,147 @@
     over_planes(body)
 
 
-def add_side(w, core_ref, part_ref, side_ref, shift, finish):
+def add_sides(w, core_ref, part_ref, passed_ref, swapped_ref, finish):
     def run(shift):
         def body(z):
             acc = [part_ref[i, z, :] for i in range(16)]
-            finish(z, add_block(w, side_ref, z, acc, shift))
+            acc = add_block(w, swapped_ref, z, acc, shift)
+            finish(z, add_block(w, passed_ref, z, acc, -shift))
 
         over_planes(body)
 
-    pl.when(core_ref[0] == 0)(lambda: run(shift))
-    pl.when(core_ref[0] != 0)(lambda: run(-shift))
-
-
-def side_kernel(flip, shift, psf_ref, core_ref, part_ref, side_ref, out_ref):
+    pl.when(core_ref[0] == 0)(lambda: run(16))
+    pl.when(core_ref[0] != 0)(lambda: run(-16))
+
+
+def sides_kernel(flip, psf_ref, core_ref, swapped_ref, passed_ref, part_ref, out_ref):
     def finish(z, acc):
         for i in range(16):
             out_ref[i, z, :] = acc[i]
 
-    add_side(tap_vectors(psf_ref, flip), core_ref, part_ref, side_ref, shift, finish)
-
-
-def update_kernel(flip, psf_ref, core_ref, part_ref, side_ref, est_ref, y_ref, new_ref, out_ref):
+    add_sides(tap_vectors(psf_ref, flip), core_ref, part_ref, passed_ref, swapped_ref, finish)
+
+
+def update_kernel(flip, psf_ref, core_ref, swapped_ref, passed_ref, part_ref, est_ref, y_ref, new_ref, out_ref):
+    y = split(y_ref[...])
+
     def finish(z, acc):
         for i in range(16):
-            new_ref[i, z, :] = est_ref[i, z, :] * acc[i]
-
-    add_side(tap_vectors(psf_ref, flip), core_ref, part_ref, side_ref, 16, finish)
-    y = split(y_ref[...])
+            acc[i] = est_ref[i, z, :] * acc[i]
+            new_ref[i, z, :] = acc[i]
+
+    add_sides(tap_vectors(psf_ref, flip), core_ref, part_ref, passed_ref, swapped_ref, finish)
     for i in range(16):
         out_ref[i] = dot(split(new_ref[i]), y)
 
 
-def x_halo(v, psf, core, flip, ride=None):
+def x_halo(v, psf, flip, later):
     passed = lax.ppermute(v, SLAB, NEXT)
     swapped = lax.ppermute(v, "c", SWAP)
     part = call(functools.partial(own_x_kernel, flip), BLOCK, [psf, v], 1.3, "x_own")
-    if ride is not None:
-        ride, part = lax.optimization_barrier((ride, part))
-        ride = exchange(ride)
-    kernel = functools.partial(side_kernel, flip, -16)
-    part = call(kernel, BLOCK, [psf, core, part, passed], 1, "x_passed")
-    return part, swapped, ride
-
-
-def ratio_kernel(
-    slab_ref, v_ref, below_ref, above_ref, obs_ref, zo_ref, zl_ref, zh_ref, za_ref, ya_ref,
-    out_ref, ratio_ref
-):
+    later, part = lax.optimization_barrier((later, part))
+    return [swapped, passed, part], later
+
+
+def ratio_planes(slab_ref, v_ref, below_ref, above_ref, obs, mats, out_ref, ratio_ref):
     has_below = jnp.full((32, 128), slab_ref[0], jnp.int32) > 0
     has_above = jnp.full((32, 128), slab_ref[0], jnp.int32) < 7
-    own, low_band, high_band = split(zo_ref[...]), split(zl_ref[...]), split(zh_ref[...])
-    adjoint, y = split(za_ref[...]), split(ya_ref[...])
+    own, low_band, high_band, adjoint, y = [split(m[...]) for m in mats]
     for x in range(16):
         part = dot(own, split(v_ref[x, :64, :]))
         low = part[:64] + dot(low_band, split(below_ref[x, :64, :]))
         high = part[64:] + dot(high_band, split(above_ref[x, :64, :]))
-        ratio_ref[x, :32, :] = jnp.where(has_below, obs_ref[x, :32, :] / low[:32], 0.0)
-        ratio_ref[x, 32:64, :] = obs_ref[x, 32:64, :] / low[32:]
-        ratio_ref[x, 64:96, :] = obs_ref[x, 64:96, :] / high[:32]
-        ratio_ref[x, 96:, :] = jnp.where(has_above, obs_ref[x, 96:, :] / high[32:], 0.0)
+        ratio_ref[x, :32, :] = jnp.where(has_below, obs(0, x) / low[:32], 0.0)
+        ratio_ref[x, 32:64, :] = obs(1, x) / low[32:]
+        ratio_ref[x, 64:96, :] = obs(2, x) / high[:32]
+        ratio_ref[x, 96:, :] = jnp.where(has_above, obs(3, x) / high[32:], 0.0)
     for x in range(16):
         out_ref[x] = dot(split(dot(adjoint, split(ratio_ref[x]))), y)
 
 
-def first_ratio_kernel(
-    slab_ref, up_ref, down_ref, below_ref, above_ref, zo_ref, zl_ref, zh_ref, za_ref, ya_ref,
-    out_ref, obs_ref, ratio_ref
-):
+def ratio_kernel(slab_ref, v_ref, below_ref, above_ref, obs_ref, halo_ref, *refs):
+    *mats, out_ref, ratio_ref, back_ref, rows_ref = refs
+
+    def obs(i, x):
+        ref, at = ((halo_ref, 0), (obs_ref, 0), (obs_ref, 32), (halo_ref, 32))[i]
+        return ref[x, at : at + 32, :]
+
+    ratio_planes(slab_ref, v_ref, below_ref, above_ref, obs, mats, back_ref, ratio_ref)
+    pack_one(back_ref, out_ref, rows_ref, 16, 0)
+
+
+def first_ratio_kernel(slab_ref, up_ref, down_ref, below_ref, above_ref, *refs):
+    *mats, out_ref, halo_hbm, ratio_ref, sems = refs
     parts = (below_ref, down_ref, up_ref, above_ref)
-    for i in range(4):
-        obs_ref[:, 32 * i : 32 * i + 32, :] = parts[i][:, 64:, :]
-    ratio_kernel(
-        slab_ref, up_ref, below_ref, above_ref, obs_ref, zo_ref, zl_ref, zh_ref, za_ref, ya_ref,
-        out_ref, ratio_ref
-    )
+    copies = save_observed(below_ref, above_ref, halo_hbm, sems)
+
+    def obs(i, x):
+        return parts[i][x, 64:, :]
+
+    ratio_planes(slab_ref, up_ref, below_ref, above_ref, obs, mats, out_ref, ratio_ref)
+    for copy in copies:
+        copy.wait()
 
 
 def per_device(observed, estimate, psf_y, psf_x, psf_z):
     core = lax.axis_index("c").reshape(1)
     slab = lax.axis_index("z").reshape(1)
-    est0 = estimate.reshape(128, 1024)
+    est0, obs0 = estimate.reshape(128, 1024), observed.reshape(128, 1024)
 
     first = pl.pallas_call(
         first_kernel,
         out_shape=pltpu.VMEM((2048, 128), jnp.float32),
-        in_specs=[SMEM, HBM, HBM],
+        in_specs=[HBM, HBM, HBM],
         out_specs=VMEM,
         scratch_shapes=[
             pltpu.VMEM((128, 1024), jnp.float32),
             pltpu.VMEM((128, 1024), jnp.float32),
-            pltpu.SemaphoreType.DMA((16,)),
+            pltpu.SMEM((31,), jnp.float32),
+            pltpu.SemaphoreType.DMA((17,)),
         ],
         compiler_params=pltpu.CompilerParams(vmem_limit_bytes=LIMIT),
         name="first",
-    )(
-        psf_x,
-        pltpu.with_memory_space_constraint(est0, pltpu.HBM),
-        pltpu.with_memory_space_constraint(observed.reshape(128, 1024), pltpu.HBM),
-    )
+    )(*[pltpu.with_memory_space_constraint(a, pltpu.HBM) for a in (psf_x, est0, obs0)])
     arrived = exchange(first)
-    yf, ya, zo, zl, zh, za = prepare(psf_y, psf_z)
-    turned = call(turn_kernel, ROWS, [est0], 1, "turn", free=(0,))
-
+    yf, ya, xn, xf, zo, zl, zh, za = prepare(psf_y, psf_x, psf_z)
     mats = [zo, zl, zh, za, ya]
     out = [(16, 96, 128), (16, 96, 128)]
     up, down = call(arrive_kernel, out, [arrived, yf], 2, "arrive", [ROWS, ROWS, BLOCK])
     below = lax.ppermute(up, "z", UP)
     above = lax.ppermute(down, "z", DOWN)
-    turned, up = lax.optimization_barrier((turned, up))
+    turned, obs = call(turn_kernel, ROWS, [est0, down, up], 1, "turn", save=BLOCK)
     rode = exchange(turned)
-    back, obs = call(
-        first_ratio_kernel,
-        [BLOCK, (16, 128, 128)],
-        [slab, up, down, below, above, *mats],
-        100,
-        "first_ratio",
-        [(16, 128, 128)],
-    )
+    args = [slab, up, down, below, above, *mats]
+    scratch = [(16, 128, 128)]
+    back, halo = call(first_ratio_kernel, BLOCK, args, 100, "first_ratio", scratch, BLOCK)
     est = call(unpack_kernel, BLOCK, [rode], 1, "unpack", [ROWS])
-    part, swapped, _ = x_halo(back, psf_x, core, True)
+    sides, _ = x_halo(back, psf_x, True, ())
     est, v = call(
         functools.partial(update_kernel, True),
         [BLOCK, BLOCK],
-        [psf_x, core, part, swapped, est, yf],
+        [psf_x, core, *sides, est, yf],
         2,
         "update",
     )
     est_rows = call(pack_kernel, ROWS, [est], 1, "pack_est", [ROWS])
-    part, swapped, est_rows = x_halo(v, psf_x, core, False, est_rows)
-    kernel = functools.partial(side_kernel, False, 16)
-    v = call(kernel, BLOCK, [psf_x, core, part, swapped], 1, "x_swapped")
+    sides, est_rows = x_halo(v, psf_x, False, est_rows)
+    est_rows = exchange(est_rows)
+    v = call(functools.partial(sides_kernel, False), BLOCK, [psf_x, core, *sides], 1, "x_sides")
 
     below = lax.ppermute(v, "z", UP)
     above = lax.ppermute(v, "z", DOWN)
-    back = call(
-        ratio_kernel, BLOCK, [slab, v, below, above, obs, *mats], 4, "ratio", [(16, 128, 128)]
-    )
-    rows = exchange(call(pack_kernel, ROWS, [back], 1, "pack_back", [ROWS]))
-    out = call(last_kernel, (128, 1024), [psf_x, rows, est_rows], 4, "last", free_out=True)
+    scratch = [(16, 128, 128), BLOCK, ROWS]
+    rows = call(ratio_kernel, ROWS, [slab, v, below, above, obs, halo, *mats], 4, "ratio", scratch)
+    rows = exchange(rows)
+    out = pl.pallas_call(
+        last_kernel,
+        out_shape=pltpu.HBM((128, 1024), jnp.float32),
+        in_specs=[VMEM] * 4,
+        out_specs=HBM,
+        scratch_shapes=[pltpu.VMEM((128, 1024), jnp.float32), pltpu.SemaphoreType.DMA((8,))],
+        compiler_params=pltpu.CompilerParams(vmem_limit_bytes=LIMIT),
+        name="last",
+    )(*[pltpu.with_memory_space_constraint(a, pltpu.VMEM) for a in (rows, est_rows, xn, xf)])
     return out.reshape(8, 16, 1024)
 
 

time: 160 us -> 156 us (0.975)
  Pallas kernels: 24.4 us -> 22.6 us
    pallas_call x15 -> x12, Pallas kernels: 20.7 us -> 18.9 us  [the longest x11 17.6 us: call(): pl.pallas_call(kernel, out_shape=shapes, in_specs=[SMEM if a.ndim == 1 el...]
  transfers between devices with their start and end apart: 11 -> 11, of which waited for: 6 -> 6; matrix products, arithmetic and copies ran while one was open for 0% -> 0% of each run, Pallas kernels for 10% -> 9%
where the time goes in v6:
time: 156 us; the launch traced here: 154 us
  starting transfers between devices  51.4 us (33%)
  waiting for transfers between devices  49.9 us (32%)
  blocking collectives  28.8 us (18%)
  Pallas kernels  22.6 us (14%)
    all_to_all x1, blocking collectives, exchange(): t = lax.all_to_all(rows.reshape(64, per, 128), SLAB, 0, 0, tiled=True)  28.8 us
    all_to_all x3, waiting for transfers between devices, exchange(): t = lax.all_to_all(rows.reshape(64, per, 128), SLAB, 0, 0, tiled=True)  26.7 us
    all_to_all x3, starting transfers between devices, exchange(): t = lax.all_to_all(rows.reshape(64, per, 128), SLAB, 0, 0, tiled=True)  26.1 us
    pallas_call x11, Pallas kernels, call(): pl.pallas_call(kernel, out_shape=shapes, in_specs=[SMEM if a.ndim == 1 el...  17.6 us
    ppermute x1, waiting for transfers between devices, per_device(): above = lax.ppermute(v, 'z', DOWN)  9.72 us
    ppermute x2, starting transfers between devices, x_halo(): passed = lax.ppermute(v, SLAB, NEXT)  9.41 us
    ppermute x1, waiting for transfers between devices, per_device(): below = lax.ppermute(up, 'z', UP)  5.02 us
    ppermute x1, starting transfers between devices, per_device(): below = lax.ppermute(up, 'z', UP)  4.89 us
  transfers between devices with their start and end apart: 11, of which 6 were waited for; matrix products, arithmetic and copies ran while one was open for 0% of the time, Pallas kernels for 9%

profile of v6, /device:TPU:1, one launch (start us, length us, event | category | flops | bytes accessed | tf_op | source)
XLA Modules:
  0.0 153.8 jit_solution(11050273699318767532)
XLA Ops:
  0.0 3.7 %first.1 = f32[2048,128]{1,0:T(8,128)} custom-call(f32[31]{0:T(128)} %psf_ref.7, f32[128,1024]{1,0:T(8,128)} %bitcast.16, f32[128,1024]{1,0:T(8,128)} %bitcast.20), custom_call_target="tpu_custom_call" | custom-call | tf_op jit(solution)/shard_map/first/pallas_call | solution.py:377
  3.7 11.8 %all-to-all-start = ((f32[64,32,128]{2,1,0:T(8,128)}), f32[64,32,128]{2,1,0:T(8,128)S(1)}, u32[]{:S(2)}, u32[]{:S(2)}) async-start(f32[64,32,128]{2,1,0:T(8,128)} %bitcast.4), calls=%async_computation | async-start | bytes 2097152 | tf_op jit(solution)/shard_map/all_to_all | solution.py:248
  15.5 0.9 prepare.1
  16.4 0.6 copy-done.6
  17.0 26.7 %all-to-all-done = f32[64,32,128]{2,1,0:T(8,128)S(1)} async-done(((f32[64,32,128]{2,1,0:T(8,128)}), f32[64,32,128]{2,1,0:T(8,128)S(1)}, u32[]{:S(2)}, u32[]{:S(2)}) %all-to-all-start) | async-done | bytes 1048608 | tf_op jit(solution)/shard_map/all_to_all | solution.py:248
  43.7 1.6 %arrive.1 = (f32[16,96,128]{2,1,0:T(8,128)S(1)}, f32[16,96,128]{2,1,0:T(8,128)S(1)}) custom-call(f32[2048,128]{1,0:T(8,128)S(1)} %bitcast.15, f32[128,128]{1,0:T(8,128)S(1)} %get-tuple-element.23.y_ref), custom_call_target="tpu_custom_call" | custom-call | flops 2000000000 | bytes 6000000 | tf_op jit(solution)/shard_map/arrive/pallas_call | solution.py:44
  45.3 4.9 %collective-permute-start = (f32[16,96,128]{2,1,0:T(8,128)S(1)}, f32[16,96,128]{2,1,0:T(8,128)}, u32[]{:S(2)}, u32[]{:S(2)}) collective-permute-start(f32[16,96,128]{2,1,0:T(8,128)S(1)} %get-tuple-element.24.up_ref), channel_id=1, source_target_pairs={{0,64},{64,128},{128,192},{192,256},{256,320},{320,384},{384,448},... | collective-permute-start | bytes 2359304 | tf_op jit(solution)/shard_map/ppermute | solution.py:396
  50.2 1.3 collective-permute-start.1
  51.5 1.6 %turn.1 = (f32[1024,128]{1,0:T(8,128)}, f32[16,64,128]{2,1,0:T(8,128)}) custom-call(f32[128,1024]{1,0:T(8,128)S(1)} %bitcast.17, f32[16,96,128]{2,1,0:T(8,128)S(1)} %get-tuple-element.25.down_ref, f32[16,96,128]{2,1,0:T(8,128)S(1)} %get-tuple-element.24.up_ref), custom_call_target="tpu_custom_call" | custom-call | flops 1000000000 | bytes 3000000 | tf_op jit(solution)/shard_map/turn/pallas_call | solution.py:44
  53.1 6.8 %all-to-all-start.1 = ((f32[64,16,128]{2,1,0:T(8,128)}), f32[64,16,128]{2,1,0:T(8,128)S(1)}, u32[]{:S(2)}, u32[]{:S(2)}) async-start(f32[64,16,128]{2,1,0:T(8,128)} %bitcast.6), calls=%async_computation.1 | async-start | bytes 1048576 | tf_op jit(solution)/shard_map/all_to_all | solution.py:248
  60.0 5.0 %collective-permute-done.below_ref = f32[16,96,128]{2,1,0:T(8,128)} collective-permute-done((f32[16,96,128]{2,1,0:T(8,128)S(1)}, f32[16,96,128]{2,1,0:T(8,128)}, u32[]{:S(2)}, u32[]{:S(2)}) %collective-permute-start) | collective-permute-done | bytes 786464 | tf_op jit(solution)/shard_map/ppermute | solution.py:396
  65.0 4.8 %collective-permute-done.1.above_ref = f32[16,96,128]{2,1,0:T(8,128)} collective-permute-done((f32[16,96,128]{2,1,0:T(8,128)S(1)}, f32[16,96,128]{2,1,0:T(8,128)}, u32[]{:S(2)}, u32[]{:S(2)}) %collective-permute-start.1) | collective-permute-done | bytes 786464 | tf_op jit(solution)/shard_map/ppermute | solution.py:397
  69.8 3.3 %first_ratio.1 = (f32[16,64,128]{2,1,0:T(8,128)S(1)}, f32[16,64,128]{2,1,0:T(8,128)}) custom-call(s32[1]{0:T(128)} %bitcast.slab_ref, f32[16,96,128]{2,1,0:T(8,128)S(1)} %get-tuple-element.24.up_ref, f32[16,96,128]{2,1,0:T(8,128)S(1)} %get-tuple-element.25.down_ref, f32[16,96,128]{2,1,0:T(8,128)} %collective-permute-done.below_ref, ...), custom_call_target="tpu_custom_call" | custom-call | flops 99999997952 | bytes 300000000 | tf_op jit(solution)/shard_map/first_ratio/pallas_call | solution.py:44
  73.2 5.7 %collective-permute-start.3 = (f32[16,64,128]{2,1,0:T(8,128)S(1)}, f32[16,64,128]{2,1,0:T(8,128)S(1)}, u32[]{:S(2)}, u32[]{:S(2)}) collective-permute-start(f32[16,64,128]{2,1,0:T(8,128)S(1)} %get-tuple-element.31.own_ref), channel_id=1, source_target_pairs={{8,1},{2,9},{10,3},{4,11},{12,5},{6,13},{14,7},{16,15},{24,17},{18... | collective-permute-start | bytes 1572872 | tf_op jit(solution)/shard_map/ppermute | solution.py:325
  78.9 1.9 %collective-permute-start.2 = (f32[16,64,128]{2,1,0:T(8,128)S(1)}, f32[16,64,128]{2,1,0:T(8,128)S(1)}, u32[]{:S(2)}, u32[]{:S(2)}) collective-permute-start(f32[16,64,128]{2,1,0:T(8,128)S(1)} %get-tuple-element.31.own_ref), channel_id=1, source_target_pairs={{0,1},{1,0},{2,3},{3,2},{4,5},{5,4},{6,7},{7,6},{8,9},{9,8},{10,11... | collective-permute-start | bytes 1572872 | tf_op jit(solution)/shard_map/ppermute | solution.py:326
  80.8 1.2 x_own.2.part_ref
  82.1 0.9 unpack.1.est_ref
  82.9 2.8 %collective-permute-done.3.passed_ref = f32[16,64,128]{2,1,0:T(8,128)S(1)} collective-permute-done((f32[16,64,128]{2,1,0:T(8,128)S(1)}, f32[16,64,128]{2,1,0:T(8,128)S(1)}, u32[]{:S(2)}, u32[]{:S(2)}) %collective-permute-start.3) | collective-permute-done | bytes 524320 | tf_op jit(solution)/shard_map/ppermute | solution.py:325
  85.8 1.8 %update.1 = (f32[16,64,128]{2,1,0:T(8,128)S(1)}, f32[16,64,128]{2,1,0:T(8,128)S(1)}) custom-call(f32[31]{0:T(128)S(1)} %copy-done.1, s32[1]{0:T(128)} %bitcast.1.core_ref, f32[16,64,128]{2,1,0:T(8,128)S(1)} %collective-permute-done.2.swapped_ref, f32[16,64,128]{2,1,0:T(8,128)S(1)} %collective-permute-done.3.passed_ref, f32[16,64,128]{2,1,0:T(8,128)S(1)} %x_own.2.part_ref, ...), custom_call_target="tpu_custom_call" | custom-call | flops 2000000000 | bytes 6000000 | tf_op jit(solution)/shard_map/update/pallas_call | solution.py:44
  87.5 3.7 %collective-permute-start.5 = (f32[16,64,128]{2,1,0:T(8,128)S(1)}, f32[16,64,128]{2,1,0:T(8,128)S(1)}, u32[]{:S(2)}, u32[]{:S(2)}) collective-permute-start(f32[16,64,128]{2,1,0:T(8,128)S(1)} %get-tuple-element.33.own_ref), channel_id=1, source_target_pairs={{8,1},{2,9},{10,3},{4,11},{12,5},{6,13},{14,7},{16,15},{24,17},{18... | collective-permute-start | bytes 1572872 | tf_op jit(solution)/shard_map/ppermute | solution.py:325
  91.2 1.9 %collective-permute-start.4 = (f32[16,64,128]{2,1,0:T(8,128)S(1)}, f32[16,64,128]{2,1,0:T(8,128)S(1)}, u32[]{:S(2)}, u32[]{:S(2)}) collective-permute-start(f32[16,64,128]{2,1,0:T(8,128)S(1)} %get-tuple-element.33.own_ref), channel_id=1, source_target_pairs={{0,1},{1,0},{2,3},{3,2},{4,5},{5,4},{6,7},{7,6},{8,9},{9,8},{10,11... | collective-permute-start | bytes 1572872 | tf_op jit(solution)/shard_map/ppermute | solution.py:326
  93.1 1.6 %pack_est.1 = f32[1024,128]{1,0:T(8,128)} custom-call(f32[16,64,128]{2,1,0:T(8,128)S(1)} %get-tuple-element.34.in_ref), custom_call_target="tpu_custom_call" | custom-call | flops 1000000000 | bytes 3000000 | tf_op jit(solution)/shard_map/pack_est/pallas_call | solution.py:44
  94.8 1.2 x_own.3.part_ref
  96.0 7.5 %all-to-all-start.3 = ((f32[64,16,128]{2,1,0:T(8,128)}), f32[64,16,128]{2,1,0:T(8,128)S(1)}, u32[]{:S(2)}, u32[]{:S(2)}) async-start(f32[64,16,128]{2,1,0:T(8,128)} %bitcast.10), calls=%async_computation.3 | async-start | bytes 1048576 | tf_op jit(solution)/shard_map/all_to_all | solution.py:248
  103.5 1.2 x_sides.1.v_ref
  104.8 1.3 collective-permute-start.7
  106.1 4.6 %collective-permute-start.6 = (f32[16,64,128]{2,1,0:T(8,128)S(1)}, f32[16,64,128]{2,1,0:T(8,128)S(1)}, u32[]{:S(2)}, u32[]{:S(2)}) collective-permute-start(f32[16,64,128]{2,1,0:T(8,128)S(1)} %x_sides.1.v_ref), channel_id=1, source_target_pairs={{0,64},{64,128},{128,192},{192,256},{256,320},{320,384},{384,448},... | collective-permute-start | bytes 1572872 | tf_op jit(solution)/shard_map/ppermute | solution.py:417
  110.7 9.7 %collective-permute-done.7.above_ref = f32[16,64,128]{2,1,0:T(8,128)S(1)} collective-permute-done((f32[16,64,128]{2,1,0:T(8,128)S(1)}, f32[16,64,128]{2,1,0:T(8,128)S(1)}, u32[]{:S(2)}, u32[]{:S(2)}) %collective-permute-start.7) | collective-permute-done | bytes 524320 | tf_op jit(solution)/shard_map/ppermute | solution.py:418
  120.4 0.9 collective-permute-done.6.below_ref
  121.3 2.2 %ratio.1 = f32[1024,128]{1,0:T(8,128)S(1)} custom-call(s32[1]{0:T(128)} %bitcast.slab_ref, f32[16,64,128]{2,1,0:T(8,128)S(1)} %x_sides.1.v_ref, f32[16,64,128]{2,1,0:T(8,128)S(1)} %collective-permute-done.6.below_ref, f32[16,64,128]{2,1,0:T(8,128)S(1)} %collective-permute-done.7.above_ref, f32[16,64,128]{2,1,0:T(8,128)S(1)} %copy-done.4, ...), custom_call_target="tpu_custom_call" | custom-call | flops 4000000000 | bytes 12000000 | tf_op jit(solution)/shard_map/ratio/pallas_call | solution.py:44
  123.5 28.8 %all_to_all.20 = f32[64,16,128]{2,1,0:T(8,128)S(1)} all-to-all(f32[64,16,128]{2,1,0:T(8,128)S(1)} %bitcast.19), channel_id=1, replica_groups=mesh['z'=8,'x'=4,'yl'=2,'yh'=4,'c'=2] {'x','yl','yh','c'}, dimensions={0} | all-to-all | bytes 1048576 | tf_op jit(solution)/shard_map/all_to_all | solution.py:248
  152.2 1.4 last.1
  (22 shorter events, 0.1 us)
Async XLA Ops:
  3.7 11.8 %copy-start.1 = (f32[31]{0:T(128)S(1)}, f32[31]{0:T(128)}, u32[]{:S(2)}) copy-start(f32[31]{0:T(128)} %psf_ref.7) | copy-start | bytes 376
  3.7 11.8 %copy-start.2 = (f32[31]{0:T(128)S(1)}, f32[31]{0:T(128)}, u32[]{:S(2)}) copy-start(f32[31]{0:T(128)} %psf_y_ref.1) | copy-start | bytes 376
  3.7 11.8 %copy-start.3 = (f32[63]{0:T(128)S(1)}, f32[63]{0:T(128)}, u32[]{:S(2)}) copy-start(f32[63]{0:T(128)} %psf_z_ref.1) | copy-start | bytes 760
  3.7 40.0 %all-to-all-start = ((f32[64,32,128]{2,1,0:T(8,128)}), f32[64,32,128]{2,1,0:T(8,128)S(1)}, u32[]{:S(2)}, u32[]{:S(2)}) async-start(f32[64,32,128]{2,1,0:T(8,128)} %bitcast.4), calls=%async_computation | async-start | bytes 2097152 | tf_op jit(solution)/shard_map/all_to_all | solution.py:248
  16.4 0.6 copy-start.6
  43.7 7.8 %copy-start = (f32[8,16,1024]{2,1,0:T(8,128)S(1)}, f32[8,16,1024]{2,1,0:T(8,128)}, u32[]{:S(2)}) copy-start(f32[8,16,1024]{2,1,0:T(8,128)} %param.6) | copy-start | bytes 1572868
  45.3 19.7 %collective-permute-start = (f32[16,96,128]{2,1,0:T(8,128)S(1)}, f32[16,96,128]{2,1,0:T(8,128)}, u32[]{:S(2)}, u32[]{:S(2)}) collective-permute-start(f32[16,96,128]{2,1,0:T(8,128)S(1)} %get-tuple-element.24.up_ref), channel_id=1, source_target_pairs={{0,64},{64,128},{128,192},{192,256},{256,320},{320,384},{384,448},... | collective-permute-start | bytes 2359304 | tf_op jit(solution)/shard_map/ppermute | solution.py:396
  50.2 19.6 %collective-permute-start.1 = (f32[16,96,128]{2,1,0:T(8,128)S(1)}, f32[16,96,128]{2,1,0:T(8,128)}, u32[]{:S(2)}, u32[]{:S(2)}) collective-permute-start(f32[16,96,128]{2,1,0:T(8,128)S(1)} %get-tuple-element.25.down_ref), channel_id=1, source_target_pairs={{64,0},{128,64},{192,128},{256,192},{320,256},{384,320},{448,384},... | collective-permute-start | bytes 2359304 | tf_op jit(solution)/shard_map/ppermute | solution.py:397
  53.1 16.7 %copy-start.7 = (f32[64,128]{1,0:T(8,128)S(1)}, f32[64,128]{1,0:T(8,128)}, u32[]{:S(2)}) copy-start(f32[64,128]{1,0:T(8,128)} %copy-done.6) | copy-start | bytes 98308
  53.1 28.9 %all-to-all-start.1 = ((f32[64,16,128]{2,1,0:T(8,128)}), f32[64,16,128]{2,1,0:T(8,128)S(1)}, u32[]{:S(2)}, u32[]{:S(2)}) async-start(f32[64,16,128]{2,1,0:T(8,128)} %bitcast.6), calls=%async_computation.1 | async-start | bytes 1048576 | tf_op jit(solution)/shard_map/all_to_all | solution.py:248
  73.2 12.6 %collective-permute-start.3 = (f32[16,64,128]{2,1,0:T(8,128)S(1)}, f32[16,64,128]{2,1,0:T(8,128)S(1)}, u32[]{:S(2)}, u32[]{:S(2)}) collective-permute-start(f32[16,64,128]{2,1,0:T(8,128)S(1)} %get-tuple-element.31.own_ref), channel_id=1, source_target_pairs={{8,1},{2,9},{10,3},{4,11},{12,5},{6,13},{14,7},{16,15},{24,17},{18... | collective-permute-start | bytes 1572872 | tf_op jit(solution)/shard_map/ppermute | solution.py:325
  78.9 6.9 %collective-permute-start.2 = (f32[16,64,128]{2,1,0:T(8,128)S(1)}, f32[16,64,128]{2,1,0:T(8,128)S(1)}, u32[]{:S(2)}, u32[]{:S(2)}) collective-permute-start(f32[16,64,128]{2,1,0:T(8,128)S(1)} %get-tuple-element.31.own_ref), channel_id=1, source_target_pairs={{0,1},{1,0},{2,3},{3,2},{4,5},{5,4},{6,7},{7,6},{8,9},{9,8},{10,11... | collective-permute-start | bytes 1572872 | tf_op jit(solution)/shard_map/ppermute | solution.py:326
  87.5 16.0 %collective-permute-start.5 = (f32[16,64,128]{2,1,0:T(8,128)S(1)}, f32[16,64,128]{2,1,0:T(8,128)S(1)}, u32[]{:S(2)}, u32[]{:S(2)}) collective-permute-start(f32[16,64,128]{2,1,0:T(8,128)S(1)} %get-tuple-element.33.own_ref), channel_id=1, source_target_pairs={{8,1},{2,9},{10,3},{4,11},{12,5},{6,13},{14,7},{16,15},{24,17},{18... | collective-permute-start | bytes 1572872 | tf_op jit(solution)/shard_map/ppermute | solution.py:325
  91.2 12.3 %collective-permute-start.4 = (f32[16,64,128]{2,1,0:T(8,128)S(1)}, f32[16,64,128]{2,1,0:T(8,128)S(1)}, u32[]{:S(2)}, u32[]{:S(2)}) collective-permute-start(f32[16,64,128]{2,1,0:T(8,128)S(1)} %get-tuple-element.33.own_ref), channel_id=1, source_target_pairs={{0,1},{1,0},{2,3},{3,2},{4,5},{5,4},{6,7},{7,6},{8,9},{9,8},{10,11... | collective-permute-start | bytes 1572872 | tf_op jit(solution)/shard_map/ppermute | solution.py:326
  96.0 27.5 %all-to-all-start.3 = ((f32[64,16,128]{2,1,0:T(8,128)}), f32[64,16,128]{2,1,0:T(8,128)S(1)}, u32[]{:S(2)}, u32[]{:S(2)}) async-start(f32[64,16,128]{2,1,0:T(8,128)} %bitcast.10), calls=%async_computation.3 | async-start | bytes 1048576 | tf_op jit(solution)/shard_map/all_to_all | solution.py:248
  103.5 17.8 %copy-start.4 = (f32[16,64,128]{2,1,0:T(8,128)S(1)}, f32[16,64,128]{2,1,0:T(8,128)}, u32[]{:S(2)}) copy-start(f32[16,64,128]{2,1,0:T(8,128)} %get-tuple-element.36.obs_ref) | copy-start | bytes 1572868
  103.5 17.8 %copy-start.5 = (f32[16,64,128]{2,1,0:T(8,128)S(1)}, f32[16,64,128]{2,1,0:T(8,128)}, u32[]{:S(2)}) copy-start(f32[16,64,128]{2,1,0:T(8,128)} %get-tuple-element.37.halo_ref) | copy-start | bytes 1572868
  103.5 17.8 %copy-start.8 = (f32[64,128]{1,0:T(8,128)S(1)}, f32[64,128]{1,0:T(8,128)}, u32[]{:S(2)}) copy-start(f32[64,128]{1,0:T(8,128)} %copy-done.6) | copy-start | bytes 98308
  104.8 15.6 %collective-permute-start.7 = (f32[16,64,128]{2,1,0:T(8,128)S(1)}, f32[16,64,128]{2,1,0:T(8,128)S(1)}, u32[]{:S(2)}, u32[]{:S(2)}) collective-permute-start(f32[16,64,128]{2,1,0:T(8,128)S(1)} %x_sides.1.v_ref), channel_id=1, source_target_pairs={{64,0},{128,64},{192,128},{256,192},{320,256},{384,320},{448,384},... | collective-permute-start | bytes 1572872 | tf_op jit(solution)/shard_map/ppermute | solution.py:418
  106.1 15.2 %collective-permute-start.6 = (f32[16,64,128]{2,1,0:T(8,128)S(1)}, f32[16,64,128]{2,1,0:T(8,128)S(1)}, u32[]{:S(2)}, u32[]{:S(2)}) collective-permute-start(f32[16,64,128]{2,1,0:T(8,128)S(1)} %x_sides.1.v_ref), channel_id=1, source_target_pairs={{0,64},{64,128},{128,192},{192,256},{256,320},{320,384},{384,448},... | collective-permute-start | bytes 1572872 | tf_op jit(solution)/shard_map/ppermute | solution.py:417

commit v7 on v6

--- a/solution.py
+++ b/solution.py
@@ -39,7 +39,8 @@
     specs = jax.tree.map(lambda s: VMEM, out, is_leaf=is_shape)
     scratch = [pltpu.VMEM(s, jnp.float32) for s in scratch]
     if save:
-        shapes, specs = [shapes, pltpu.HBM(save, jnp.float32)], [specs, HBM]
+        shapes = [*(shapes if isinstance(shapes, list) else [shapes]), pltpu.HBM(save, jnp.float32)]
+        specs = [*(specs if isinstance(specs, list) else [specs]), HBM]
         scratch.append(pltpu.SemaphoreType.DMA((2,)))
     return pl.pallas_call(
         kernel,
@@ -88,7 +89,7 @@
 
 
 def prep_kernel(
-    psf_y_ref, psf_x_ref, psf_z_ref, yf_ref, ya_ref, xn_ref, xf_ref, zo_ref, zl_ref, zh_ref, za_ref
+    psf_y_ref, psf_x_ref, psf_z_ref, yf_ref, ya_ref, xn_ref, xf_ref, zo_ref, zl_ref, zh_ref, al_ref, ah_ref
 ):
     yf_ref[...] = band(psf_y_ref, -15, True, 128)[:, :128]
     ya_ref[...] = band(psf_y_ref, -15, False, 128)[:, :128]
@@ -97,11 +98,12 @@
     zl_ref[...] = fwd[:64, :64]
     zo_ref[...] = fwd[:, 64:128]
     zh_ref[...] = fwd[64:, 128:192]
-    za_ref[...] = band(psf_z_ref, 1, True, 64)[:, :128]
+    adjoint = band(psf_z_ref, 1, True, 64)
+    al_ref[...], ah_ref[...] = adjoint[:, :64], adjoint[:, 64:128]
 
 
 def prepare(psf_y, psf_x, psf_z):
-    out = [(128, 128)] * 4 + [(128, 64), (64, 64), (64, 64), (64, 128)]
+    out = [(128, 128)] * 4 + [(128, 64)] + [(64, 64)] * 4
     return call(prep_kernel, out, [psf_y, psf_x, psf_z], 1, "prepare")
 
 
@@ -152,12 +154,12 @@
         write_columns(out_ref, t, obs_ref[:, 128 * t : 128 * t + 128], 32, 16)
 
 
-def save_observed(low_ref, high_ref, out_hbm, sems):
+def save_observed(refs, out_hbm, sems):
     copies = [
         pltpu.make_async_copy(
             ref.at[:, pl.ds(64, 32), :], out_hbm.at[:, pl.ds(32 * i, 32), :], sems.at[i]
         )
-        for i, ref in enumerate((low_ref, high_ref))
+        for i, ref in enumerate(refs)
     ]
     for copy in copies:
         copy.start()
@@ -165,7 +167,7 @@
 
 
 def turn_kernel(in_ref, down_ref, up_ref, out_ref, obs_hbm, sems):
-    copies = save_observed(down_ref, up_ref, obs_hbm, sems)
+    copies = save_observed([down_ref, up_ref], obs_hbm, sems)
     for t in range(8):
         write_columns(out_ref, t, in_ref[:, 128 * t : 128 * t + 128])
     for copy in copies:
@@ -329,44 +331,76 @@
     return [swapped, passed, part], later
 
 
-def ratio_planes(slab_ref, v_ref, below_ref, above_ref, obs, mats, out_ref, ratio_ref):
+def high_planes(slab_ref, v_ref, above_ref, obs, mats, sum_ref, low_ref):
+    has_above = jnp.full((32, 128), slab_ref[0], jnp.int32) < 7
+    own, band, adjoint = [split(m[...]) for m in mats]
+    for x in range(16):
+        part = dot(own, split(v_ref[x, :64, :]))
+        low_ref[x] = part[:64]
+        sum_ref[x] = part[64:] + dot(band, split(above_ref[x, :64, :]))
+    for x in range(16):
+        sum_ref[x, :32, :] = obs(2, x) / sum_ref[x, :32, :]
+        sum_ref[x, 32:, :] = jnp.where(has_above, obs(3, x) / sum_ref[x, 32:, :], 0.0)
+    for x in range(16):
+        sum_ref[x] = dot(adjoint, split(sum_ref[x]))
+
+
+def low_planes(slab_ref, low_ref, sum_ref, below_ref, obs, mats, out_ref):
     has_below = jnp.full((32, 128), slab_ref[0], jnp.int32) > 0
-    has_above = jnp.full((32, 128), slab_ref[0], jnp.int32) < 7
-    own, low_band, high_band, adjoint, y = [split(m[...]) for m in mats]
-    for x in range(16):
-        part = dot(own, split(v_ref[x, :64, :]))
-        low = part[:64] + dot(low_band, split(below_ref[x, :64, :]))
-        high = part[64:] + dot(high_band, split(above_ref[x, :64, :]))
-        ratio_ref[x, :32, :] = jnp.where(has_below, obs(0, x) / low[:32], 0.0)
-        ratio_ref[x, 32:64, :] = obs(1, x) / low[32:]
-        ratio_ref[x, 64:96, :] = obs(2, x) / high[:32]
-        ratio_ref[x, 96:, :] = jnp.where(has_above, obs(3, x) / high[32:], 0.0)
-    for x in range(16):
-        out_ref[x] = dot(split(dot(adjoint, split(ratio_ref[x]))), y)
-
-
-def ratio_kernel(slab_ref, v_ref, below_ref, above_ref, obs_ref, halo_ref, *refs):
-    *mats, out_ref, ratio_ref, back_ref, rows_ref = refs
+    band, adjoint, y = [split(m[...]) for m in mats]
+    for x in range(16):
+        out_ref[x] = low_ref[x] + dot(band, split(below_ref[x, :64, :]))
+    for x in range(16):
+        out_ref[x, :32, :] = jnp.where(has_below, obs(0, x) / out_ref[x, :32, :], 0.0)
+        out_ref[x, 32:, :] = obs(1, x) / out_ref[x, 32:, :]
+    for x in range(16):
+        out_ref[x] = sum_ref[x] + dot(adjoint, split(out_ref[x]))
+    for x in range(16):
+        out_ref[x] = dot(split(out_ref[x]), y)
+
+
+def first_high_kernel(slab_ref, up_ref, above_ref, zo_ref, zh_ref, ah_ref, *refs):
+    sum_ref, low_ref, halo_hbm, sems = refs
+    copies = save_observed([above_ref], halo_hbm, sems)
 
     def obs(i, x):
-        ref, at = ((halo_ref, 0), (obs_ref, 0), (obs_ref, 32), (halo_ref, 32))[i]
-        return ref[x, at : at + 32, :]
-
-    ratio_planes(slab_ref, v_ref, below_ref, above_ref, obs, mats, back_ref, ratio_ref)
-    pack_one(back_ref, out_ref, rows_ref, 16, 0)
-
-
-def first_ratio_kernel(slab_ref, up_ref, down_ref, below_ref, above_ref, *refs):
-    *mats, out_ref, halo_hbm, ratio_ref, sems = refs
-    parts = (below_ref, down_ref, up_ref, above_ref)
-    copies = save_observed(below_ref, above_ref, halo_hbm, sems)
-
-    def obs(i, x):
-        return parts[i][x, 64:, :]
-
-    ratio_planes(slab_ref, up_ref, below_ref, above_ref, obs, mats, out_ref, ratio_ref)
+        return (up_ref, above_ref)[i - 2][x, 64:, :]
+
+    high_planes(slab_ref, up_ref, above_ref, obs, (zo_ref, zh_ref, ah_ref), sum_ref, low_ref)
     for copy in copies:
         copy.wait()
+
+
+def first_low_kernel(slab_ref, low_ref, sum_ref, down_ref, below_ref, zl_ref, al_ref, ya_ref, *refs):
+    out_ref, halo_hbm, sems = refs
+    copies = save_observed([below_ref], halo_hbm, sems)
+
+    def obs(i, x):
+        return (below_ref, down_ref)[i][x, 64:, :]
+
+    low_planes(slab_ref, low_ref, sum_ref, below_ref, obs, (zl_ref, al_ref, ya_ref), out_ref)
+    for copy in copies:
+        copy.wait()
+
+
+def high_kernel(
+    slab_ref, v_ref, above_ref, halo_ref, obs_ref, zo_ref, zh_ref, ah_ref, sum_ref, low_ref
+):
+    def obs(i, x):
+        return obs_ref[x, 32:, :] if i == 2 else halo_ref[x]
+
+    high_planes(slab_ref, v_ref, above_ref, obs, (zo_ref, zh_ref, ah_ref), sum_ref, low_ref)
+
+
+def low_kernel(
+    slab_ref, low_ref, sum_ref, below_ref, obs_ref, halo_ref, zl_ref, al_ref, ya_ref,
+    out_ref, back_ref, rows_ref
+):
+    def obs(i, x):
+        return obs_ref[x, :32, :] if i else halo_ref[x]
+
+    low_planes(slab_ref, low_ref, sum_ref, below_ref, obs, (zl_ref, al_ref, ya_ref), back_ref)
+    pack_one(back_ref, out_ref, rows_ref, 16, 0)
 
 
 def per_device(observed, estimate, psf_y, psf_x, psf_z):
@@ -389,17 +423,21 @@
         name="first",
     )(*[pltpu.with_memory_space_constraint(a, pltpu.HBM) for a in (psf_x, est0, obs0)])
     arrived = exchange(first)
-    yf, ya, xn, xf, zo, zl, zh, za = prepare(psf_y, psf_x, psf_z)
-    mats = [zo, zl, zh, za, ya]
+    yf, ya, xn, xf, zo, zl, zh, al, ah = prepare(psf_y, psf_x, psf_z)
+    low_mats, high_mats = [zl, al, ya], [zo, zh, ah]
+    halo = (16, 32, 128)
     out = [(16, 96, 128), (16, 96, 128)]
     up, down = call(arrive_kernel, out, [arrived, yf], 2, "arrive", [ROWS, ROWS, BLOCK])
     below = lax.ppermute(up, "z", UP)
     above = lax.ppermute(down, "z", DOWN)
     turned, obs = call(turn_kernel, ROWS, [est0, down, up], 1, "turn", save=BLOCK)
     rode = exchange(turned)
-    args = [slab, up, down, below, above, *mats]
-    scratch = [(16, 128, 128)]
-    back, halo = call(first_ratio_kernel, BLOCK, args, 100, "first_ratio", scratch, BLOCK)
+    args = [slab, up, above, *high_mats]
+    total, low, halo_above = call(
+        first_high_kernel, [BLOCK, BLOCK], args, 1, "first_high", save=halo
+    )
+    args = [slab, low, total, down, below, *low_mats]
+    back, halo_below = call(first_low_kernel, BLOCK, args, 100, "first_low", save=halo)
     est = call(unpack_kernel, BLOCK, [rode], 1, "unpack", [ROWS])
     sides, _ = x_halo(back, psf_x, True, ())
     est, v = call(
@@ -416,8 +454,10 @@
 
     below = lax.ppermute(v, "z", UP)
     above = lax.ppermute(v, "z", DOWN)
-    scratch = [(16, 128, 128), BLOCK, ROWS]
-    rows = call(ratio_kernel, ROWS, [slab, v, below, above, obs, halo, *mats], 4, "ratio", scratch)
+    args = [slab, v, above, halo_above, obs, *high_mats]
+    total, low = call(high_kernel, [BLOCK, BLOCK], args, 1, "ratio_high")
+    args = [slab, low, total, below, obs, halo_below, *low_mats]
+    rows = call(low_kernel, ROWS, args, 4, "ratio_low", [BLOCK, ROWS])
     rows = exchange(rows)
     out = pl.pallas_call(
         last_kernel,

time: 156 us -> 152 us (0.974)
  waiting for transfers between devices: 49.9 us -> 44.3 us
    ppermute x1, waiting for transfers between devices: 5.02 us -> 0.01 us  [per_device(): below = lax.ppermute(up, 'z', UP)]
    pallas_call x11 -> x13, Pallas kernels: 17.6 us -> 18.6 us  [call(): pl.pallas_call(kernel, out_shape=shapes, in_specs=[SMEM if a.ndim == 1 el...]
  transfers between devices with their start and end apart: 11 -> 11, of which waited for: 6 -> 4; matrix products, arithmetic and copies ran while one was open for 0% -> 0% of each run, Pallas kernels for 9% -> 10%
where the time goes in v7:
time: 152 us; the launch traced here: 150 us
  starting transfers between devices  51.5 us (34%)
  waiting for transfers between devices  44.3 us (29%)
  blocking collectives  28.6 us (19%)
  Pallas kernels  23.6 us (16%)
    all_to_all x1, blocking collectives, exchange(): t = lax.all_to_all(rows.reshape(64, per, 128), SLAB, 0, 0, tiled=True)  28.6 us
    all_to_all x3, starting transfers between devices, exchange(): t = lax.all_to_all(rows.reshape(64, per, 128), SLAB, 0, 0, tiled=True)  26.1 us
    all_to_all x3, waiting for transfers between devices, exchange(): t = lax.all_to_all(rows.reshape(64, per, 128), SLAB, 0, 0, tiled=True)  26.1 us
    pallas_call x13, Pallas kernels, call(): pl.pallas_call(kernel, out_shape=shapes, in_specs=[SMEM if a.ndim == 1 el...  18.6 us
    ppermute x1, waiting for transfers between devices, per_device(): above = lax.ppermute(v, 'z', DOWN)  9.9 us
    ppermute x2, starting transfers between devices, x_halo(): passed = lax.ppermute(v, SLAB, NEXT)  8.82 us
    ppermute x1, waiting for transfers between devices, per_device(): above = lax.ppermute(down, 'z', DOWN)  5.54 us
    ppermute x1, starting transfers between devices, per_device(): below = lax.ppermute(up, 'z', UP)  5.54 us
  transfers between devices with their start and end apart: 11, of which 4 were waited for; matrix products, arithmetic and copies ran while one was open for 0% of the time, Pallas kernels for 10%

profile of v7, /device:TPU:1, one launch (start us, length us, event | category | flops | bytes accessed | tf_op | source)
XLA Modules:
  0.0 149.6 jit_solution(15701033785489972606)
XLA Ops:
  0.0 3.7 %first.1 = f32[2048,128]{1,0:T(8,128)} custom-call(f32[31]{0:T(128)} %psf_ref.7, f32[128,1024]{1,0:T(8,128)} %bitcast.16, f32[128,1024]{1,0:T(8,128)} %bitcast.20), custom_call_target="tpu_custom_call" | custom-call | tf_op jit(solution)/shard_map/first/pallas_call | solution.py:411
  3.7 11.8 %all-to-all-start = ((f32[64,32,128]{2,1,0:T(8,128)}), f32[64,32,128]{2,1,0:T(8,128)S(1)}, u32[]{:S(2)}, u32[]{:S(2)}) async-start(f32[64,32,128]{2,1,0:T(8,128)} %bitcast.4), calls=%async_computation | async-start | bytes 2097152 | tf_op jit(solution)/shard_map/all_to_all | solution.py:250
  15.5 0.9 prepare.1
  16.4 0.6 copy-done.6
  17.6 26.1 %all-to-all-done = f32[64,32,128]{2,1,0:T(8,128)S(1)} async-done(((f32[64,32,128]{2,1,0:T(8,128)}), f32[64,32,128]{2,1,0:T(8,128)S(1)}, u32[]{:S(2)}, u32[]{:S(2)}) %all-to-all-start) | async-done | bytes 1048608 | tf_op jit(solution)/shard_map/all_to_all | solution.py:250
  43.7 1.6 %arrive.1 = (f32[16,96,128]{2,1,0:T(8,128)S(1)}, f32[16,96,128]{2,1,0:T(8,128)S(1)}) custom-call(f32[2048,128]{1,0:T(8,128)S(1)} %bitcast.15, f32[128,128]{1,0:T(8,128)S(1)} %get-tuple-element.29.y_ref), custom_call_target="tpu_custom_call" | custom-call | flops 2000000000 | bytes 6000000 | tf_op jit(solution)/shard_map/arrive/pallas_call | solution.py:45
  45.3 1.3 collective-permute-start
  46.6 5.5 %collective-permute-start.1 = (f32[16,96,128]{2,1,0:T(8,128)S(1)}, f32[16,96,128]{2,1,0:T(8,128)}, u32[]{:S(2)}, u32[]{:S(2)}) collective-permute-start(f32[16,96,128]{2,1,0:T(8,128)S(1)} %get-tuple-element.30.up_ref), channel_id=1, source_target_pairs={{0,64},{64,128},{128,192},{192,256},{256,320},{320,384},{384,448},... | collective-permute-start | bytes 2359304 | tf_op jit(solution)/shard_map/ppermute | solution.py:431
  52.1 1.6 %turn.1 = (f32[1024,128]{1,0:T(8,128)}, f32[16,64,128]{2,1,0:T(8,128)}) custom-call(f32[128,1024]{1,0:T(8,128)S(1)} %bitcast.17, f32[16,96,128]{2,1,0:T(8,128)S(1)} %get-tuple-element.31.down_ref, f32[16,96,128]{2,1,0:T(8,128)S(1)} %get-tuple-element.30.up_ref), custom_call_target="tpu_custom_call" | custom-call | flops 1000000000 | bytes 3000000 | tf_op jit(solution)/shard_map/turn/pallas_call | solution.py:45
  53.7 6.8 %all-to-all-start.1 = ((f32[64,16,128]{2,1,0:T(8,128)}), f32[64,16,128]{2,1,0:T(8,128)S(1)}, u32[]{:S(2)}, u32[]{:S(2)}) async-start(f32[64,16,128]{2,1,0:T(8,128)} %bitcast.6), calls=%async_computation.1 | async-start | bytes 1048576 | tf_op jit(solution)/shard_map/all_to_all | solution.py:250
  60.6 5.5 %collective-permute-done.above_ref = f32[16,96,128]{2,1,0:T(8,128)} collective-permute-done((f32[16,96,128]{2,1,0:T(8,128)S(1)}, f32[16,96,128]{2,1,0:T(8,128)}, u32[]{:S(2)}, u32[]{:S(2)}) %collective-permute-start) | collective-permute-done | bytes 786464 | tf_op jit(solution)/shard_map/ppermute | solution.py:432
  66.1 2.1 %first_high.1 = (f32[16,64,128]{2,1,0:T(8,128)S(1)}, f32[16,64,128]{2,1,0:T(8,128)S(1)}, f32[16,32,128]{2,1,0:T(8,128)}) custom-call(s32[1]{0:T(128)} %bitcast.slab_ref, f32[16,96,128]{2,1,0:T(8,128)S(1)} %get-tuple-element.30.up_ref, f32[16,96,128]{2,1,0:T(8,128)} %collective-permute-done.above_ref, f32[128,64]{1,0:T(8,128)S(1)} %get-tuple-element.32.zo_ref, ...), custom_call_target="tpu_custom_call" | custom-call | flops 1000000000 | bytes 3000000 | tf_op jit(solution)/shard_map/first_high/pallas_call | solution.py:45
  68.3 2.3 %first_low.1 = (f32[16,64,128]{2,1,0:T(8,128)S(1)}, f32[16,32,128]{2,1,0:T(8,128)}) custom-call(s32[1]{0:T(128)} %bitcast.slab_ref, f32[16,64,128]{2,1,0:T(8,128)S(1)} %get-tuple-element.35.low_ref, f32[16,64,128]{2,1,0:T(8,128)S(1)} %get-tuple-element.36.sum_ref, f32[16,96,128]{2,1,0:T(8,128)S(1)} %get-tuple-element.31.down_ref, ...), custom_call_target="tpu_custom_call" | custom-call | flops 99999997952 | bytes 300000000 | tf_op jit(solution)/shard_map/first_low/pallas_call | solution.py:45
  70.6 5.2 %collective-permute-start.3 = (f32[16,64,128]{2,1,0:T(8,128)S(1)}, f32[16,64,128]{2,1,0:T(8,128)S(1)}, u32[]{:S(2)}, u32[]{:S(2)}) collective-permute-start(f32[16,64,128]{2,1,0:T(8,128)S(1)} %get-tuple-element.40.own_ref), channel_id=1, source_target_pairs={{8,1},{2,9},{10,3},{4,11},{12,5},{6,13},{14,7},{16,15},{24,17},{18... | collective-permute-start | bytes 1572872 | tf_op jit(solution)/shard_map/ppermute | solution.py:327
  75.8 1.9 %collective-permute-start.2 = (f32[16,64,128]{2,1,0:T(8,128)S(1)}, f32[16,64,128]{2,1,0:T(8,128)S(1)}, u32[]{:S(2)}, u32[]{:S(2)}) collective-permute-start(f32[16,64,128]{2,1,0:T(8,128)S(1)} %get-tuple-element.40.own_ref), channel_id=1, source_target_pairs={{0,1},{1,0},{2,3},{3,2},{4,5},{5,4},{6,7},{7,6},{8,9},{9,8},{10,11... | collective-permute-start | bytes 1572872 | tf_op jit(solution)/shard_map/ppermute | solution.py:328
  77.7 1.2 x_own.2.part_ref
  78.9 0.9 unpack.1.est_ref
  79.8 2.8 %collective-permute-done.3.passed_ref = f32[16,64,128]{2,1,0:T(8,128)S(1)} collective-permute-done((f32[16,64,128]{2,1,0:T(8,128)S(1)}, f32[16,64,128]{2,1,0:T(8,128)S(1)}, u32[]{:S(2)}, u32[]{:S(2)}) %collective-permute-start.3) | collective-permute-done | bytes 524320 | tf_op jit(solution)/shard_map/ppermute | solution.py:327
  82.6 1.8 %update.1 = (f32[16,64,128]{2,1,0:T(8,128)S(1)}, f32[16,64,128]{2,1,0:T(8,128)S(1)}) custom-call(f32[31]{0:T(128)S(1)} %copy-done.1, s32[1]{0:T(128)} %bitcast.1.core_ref, f32[16,64,128]{2,1,0:T(8,128)S(1)} %collective-permute-done.2.swapped_ref, f32[16,64,128]{2,1,0:T(8,128)S(1)} %collective-permute-done.3.passed_ref, f32[16,64,128]{2,1,0:T(8,128)S(1)} %x_own.2.part_ref, ...), custom_call_target="tpu_custom_call" | custom-call | flops 2000000000 | bytes 6000000 | tf_op jit(solution)/shard_map/update/pallas_call | solution.py:45
  84.4 3.7 %collective-permute-start.5 = (f32[16,64,128]{2,1,0:T(8,128)S(1)}, f32[16,64,128]{2,1,0:T(8,128)S(1)}, u32[]{:S(2)}, u32[]{:S(2)}) collective-permute-start(f32[16,64,128]{2,1,0:T(8,128)S(1)} %get-tuple-element.42.own_ref), channel_id=1, source_target_pairs={{8,1},{2,9},{10,3},{4,11},{12,5},{6,13},{14,7},{16,15},{24,17},{18... | collective-permute-start | bytes 1572872 | tf_op jit(solution)/shard_map/ppermute | solution.py:327
  88.0 1.9 %collective-permute-start.4 = (f32[16,64,128]{2,1,0:T(8,128)S(1)}, f32[16,64,128]{2,1,0:T(8,128)S(1)}, u32[]{:S(2)}, u32[]{:S(2)}) collective-permute-start(f32[16,64,128]{2,1,0:T(8,128)S(1)} %get-tuple-element.42.own_ref), channel_id=1, source_target_pairs={{0,1},{1,0},{2,3},{3,2},{4,5},{5,4},{6,7},{7,6},{8,9},{9,8},{10,11... | collective-permute-start | bytes 1572872 | tf_op jit(solution)/shard_map/ppermute | solution.py:328
  90.0 1.6 %pack_est.1 = f32[1024,128]{1,0:T(8,128)} custom-call(f32[16,64,128]{2,1,0:T(8,128)S(1)} %get-tuple-element.43.in_ref), custom_call_target="tpu_custom_call" | custom-call | flops 1000000000 | bytes 3000000 | tf_op jit(solution)/shard_map/pack_est/pallas_call | solution.py:45
  91.6 1.2 x_own.3.part_ref
  92.8 7.5 %all-to-all-start.3 = ((f32[64,16,128]{2,1,0:T(8,128)}), f32[64,16,128]{2,1,0:T(8,128)S(1)}, u32[]{:S(2)}, u32[]{:S(2)}) async-start(f32[64,16,128]{2,1,0:T(8,128)} %bitcast.10), calls=%async_computation.3 | async-start | bytes 1048576 | tf_op jit(solution)/shard_map/all_to_all | solution.py:250
  100.4 1.2 x_sides.1.v_ref
  101.6 1.3 collective-permute-start.6
  102.9 4.6 %collective-permute-start.7 = (f32[16,64,128]{2,1,0:T(8,128)S(1)}, f32[16,64,128]{2,1,0:T(8,128)S(1)}, u32[]{:S(2)}, u32[]{:S(2)}) collective-permute-start(f32[16,64,128]{2,1,0:T(8,128)S(1)} %x_sides.1.v_ref), channel_id=1, source_target_pairs={{0,64},{64,128},{128,192},{192,256},{256,320},{320,384},{384,448},... | collective-permute-start | bytes 1572872 | tf_op jit(solution)/shard_map/ppermute | solution.py:455
  107.5 9.9 %collective-permute-done.6.above_ref = f32[16,64,128]{2,1,0:T(8,128)S(1)} collective-permute-done((f32[16,64,128]{2,1,0:T(8,128)S(1)}, f32[16,64,128]{2,1,0:T(8,128)S(1)}, u32[]{:S(2)}, u32[]{:S(2)}) %collective-permute-start.6) | collective-permute-done | bytes 524320 | tf_op jit(solution)/shard_map/ppermute | solution.py:456
  117.5 1.0 ratio_high.1
  118.5 1.2 ratio_low.1
  119.7 28.6 %all_to_all.20 = f32[64,16,128]{2,1,0:T(8,128)S(1)} all-to-all(f32[64,16,128]{2,1,0:T(8,128)S(1)} %bitcast.19), channel_id=1, replica_groups=mesh['z'=8,'x'=4,'yl'=2,'yh'=4,'c'=2] {'x','yl','yh','c'}, dimensions={0} | all-to-all | bytes 1048576 | tf_op jit(solution)/shard_map/all_to_all | solution.py:250
  148.3 1.4 last.1
  (32 shorter events, 0.7 us)
Async XLA Ops:
  3.7 11.8 %copy-start.1 = (f32[31]{0:T(128)S(1)}, f32[31]{0:T(128)}, u32[]{:S(2)}) copy-start(f32[31]{0:T(128)} %psf_ref.7) | copy-start | bytes 376
  3.7 11.8 %copy-start.2 = (f32[31]{0:T(128)S(1)}, f32[31]{0:T(128)}, u32[]{:S(2)}) copy-start(f32[31]{0:T(128)} %psf_y_ref.1) | copy-start | bytes 376
  3.7 11.8 %copy-start.3 = (f32[63]{0:T(128)S(1)}, f32[63]{0:T(128)}, u32[]{:S(2)}) copy-start(f32[63]{0:T(128)} %psf_z_ref.1) | copy-start | bytes 760
  3.7 40.0 %all-to-all-start = ((f32[64,32,128]{2,1,0:T(8,128)}), f32[64,32,128]{2,1,0:T(8,128)S(1)}, u32[]{:S(2)}, u32[]{:S(2)}) async-start(f32[64,32,128]{2,1,0:T(8,128)} %bitcast.4), calls=%async_computation | async-start | bytes 2097152 | tf_op jit(solution)/shard_map/all_to_all | solution.py:250
  16.4 0.6 copy-start.6
  17.0 0.6 copy-start.9
  43.7 8.4 %copy-start = (f32[8,16,1024]{2,1,0:T(8,128)S(1)}, f32[8,16,1024]{2,1,0:T(8,128)}, u32[]{:S(2)}) copy-start(f32[8,16,1024]{2,1,0:T(8,128)} %param.6) | copy-start | bytes 1572868
  45.3 20.9 %collective-permute-start = (f32[16,96,128]{2,1,0:T(8,128)S(1)}, f32[16,96,128]{2,1,0:T(8,128)}, u32[]{:S(2)}, u32[]{:S(2)}) collective-permute-start(f32[16,96,128]{2,1,0:T(8,128)S(1)} %get-tuple-element.31.down_ref), channel_id=1, source_target_pairs={{64,0},{128,64},{192,128},{256,192},{320,256},{384,320},{448,384},... | collective-permute-start | bytes 2359304 | tf_op jit(solution)/shard_map/ppermute | solution.py:432
  46.6 21.7 %collective-permute-start.1 = (f32[16,96,128]{2,1,0:T(8,128)S(1)}, f32[16,96,128]{2,1,0:T(8,128)}, u32[]{:S(2)}, u32[]{:S(2)}) collective-permute-start(f32[16,96,128]{2,1,0:T(8,128)S(1)} %get-tuple-element.30.up_ref), channel_id=1, source_target_pairs={{0,64},{64,128},{128,192},{192,256},{256,320},{320,384},{384,448},... | collective-permute-start | bytes 2359304 | tf_op jit(solution)/shard_map/ppermute | solution.py:431
  53.7 25.2 %all-to-all-start.1 = ((f32[64,16,128]{2,1,0:T(8,128)}), f32[64,16,128]{2,1,0:T(8,128)S(1)}, u32[]{:S(2)}, u32[]{:S(2)}) async-start(f32[64,16,128]{2,1,0:T(8,128)} %bitcast.6), calls=%async_computation.1 | async-start | bytes 1048576 | tf_op jit(solution)/shard_map/all_to_all | solution.py:250
  66.1 2.2 %copy-start.7 = (f32[64,64]{1,0:T(8,128)S(1)}, f32[64,64]{1,0:T(8,128)}, u32[]{:S(2)}) copy-start(f32[64,64]{1,0:T(8,128)} %copy-done.6) | copy-start | bytes 49156
  66.1 2.2 %copy-start.10 = (f32[64,64]{1,0:T(8,128)S(1)}, f32[64,64]{1,0:T(8,128)}, u32[]{:S(2)}) copy-start(f32[64,64]{1,0:T(8,128)} %copy-done.9) | copy-start | bytes 49156
  70.6 12.0 %collective-permute-start.3 = (f32[16,64,128]{2,1,0:T(8,128)S(1)}, f32[16,64,128]{2,1,0:T(8,128)S(1)}, u32[]{:S(2)}, u32[]{:S(2)}) collective-permute-start(f32[16,64,128]{2,1,0:T(8,128)S(1)} %get-tuple-element.40.own_ref), channel_id=1, source_target_pairs={{8,1},{2,9},{10,3},{4,11},{12,5},{6,13},{14,7},{16,15},{24,17},{18... | collective-permute-start | bytes 1572872 | tf_op jit(solution)/shard_map/ppermute | solution.py:327
  75.8 6.9 %collective-permute-start.2 = (f32[16,64,128]{2,1,0:T(8,128)S(1)}, f32[16,64,128]{2,1,0:T(8,128)S(1)}, u32[]{:S(2)}, u32[]{:S(2)}) collective-permute-start(f32[16,64,128]{2,1,0:T(8,128)S(1)} %get-tuple-element.40.own_ref), channel_id=1, source_target_pairs={{0,1},{1,0},{2,3},{3,2},{4,5},{5,4},{6,7},{7,6},{8,9},{9,8},{10,11... | collective-permute-start | bytes 1572872 | tf_op jit(solution)/shard_map/ppermute | solution.py:328
  84.4 16.0 %collective-permute-start.5 = (f32[16,64,128]{2,1,0:T(8,128)S(1)}, f32[16,64,128]{2,1,0:T(8,128)S(1)}, u32[]{:S(2)}, u32[]{:S(2)}) collective-permute-start(f32[16,64,128]{2,1,0:T(8,128)S(1)} %get-tuple-element.42.own_ref), channel_id=1, source_target_pairs={{8,1},{2,9},{10,3},{4,11},{12,5},{6,13},{14,7},{16,15},{24,17},{18... | collective-permute-start | bytes 1572872 | tf_op jit(solution)/shard_map/ppermute | solution.py:327
  88.0 12.3 %collective-permute-start.4 = (f32[16,64,128]{2,1,0:T(8,128)S(1)}, f32[16,64,128]{2,1,0:T(8,128)S(1)}, u32[]{:S(2)}, u32[]{:S(2)}) collective-permute-start(f32[16,64,128]{2,1,0:T(8,128)S(1)} %get-tuple-element.42.own_ref), channel_id=1, source_target_pairs={{0,1},{1,0},{2,3},{3,2},{4,5},{5,4},{6,7},{7,6},{8,9},{9,8},{10,11... | collective-permute-start | bytes 1572872 | tf_op jit(solution)/shard_map/ppermute | solution.py:328
  92.8 26.9 %all-to-all-start.3 = ((f32[64,16,128]{2,1,0:T(8,128)}), f32[64,16,128]{2,1,0:T(8,128)S(1)}, u32[]{:S(2)}, u32[]{:S(2)}) async-start(f32[64,16,128]{2,1,0:T(8,128)} %bitcast.10), calls=%async_computation.3 | async-start | bytes 1048576 | tf_op jit(solution)/shard_map/all_to_all | solution.py:250
  100.3 17.1 %copy-start.4 = (f32[16,64,128]{2,1,0:T(8,128)S(1)}, f32[16,64,128]{2,1,0:T(8,128)}, u32[]{:S(2)}) copy-start(f32[16,64,128]{2,1,0:T(8,128)} %get-tuple-element.46.obs_ref) | copy-start | bytes 1572868
  100.3 17.1 %copy-start.5 = (f32[16,32,128]{2,1,0:T(8,128)S(1)}, f32[16,32,128]{2,1,0:T(8,128)}, u32[]{:S(2)}) copy-start(f32[16,32,128]{2,1,0:T(8,128)} %get-tuple-element.45.halo_ref) | copy-start | bytes 786436
  101.6 15.8 %collective-permute-start.6 = (f32[16,64,128]{2,1,0:T(8,128)S(1)}, f32[16,64,128]{2,1,0:T(8,128)S(1)}, u32[]{:S(2)}, u32[]{:S(2)}) collective-permute-start(f32[16,64,128]{2,1,0:T(8,128)S(1)} %x_sides.1.v_ref), channel_id=1, source_target_pairs={{64,0},{128,64},{192,128},{256,192},{320,256},{384,320},{448,384},... | collective-permute-start | bytes 1572872 | tf_op jit(solution)/shard_map/ppermute | solution.py:456
  102.9 15.5 %collective-permute-start.7 = (f32[16,64,128]{2,1,0:T(8,128)S(1)}, f32[16,64,128]{2,1,0:T(8,128)S(1)}, u32[]{:S(2)}, u32[]{:S(2)}) collective-permute-start(f32[16,64,128]{2,1,0:T(8,128)S(1)} %x_sides.1.v_ref), channel_id=1, source_target_pairs={{0,64},{64,128},{128,192},{192,256},{256,320},{320,384},{384,448},... | collective-permute-start | bytes 1572872 | tf_op jit(solution)/shard_map/ppermute | solution.py:455
  117.4 1.0 copy-start.8
  117.5 1.0 copy-start.11
  117.5 1.0 copy-start.12

commit v8 on v7

--- a/solution.py
+++ b/solution.py
@@ -212,7 +212,10 @@
             out_ref[x, zc * 8 : zc * 8 + 8, :] = rows_ref[pl.ds(zc * 128 + x, 8, stride=16), :]
 
 
-def unpack_kernel(in_ref, out_ref, rows_ref):
+def unpack_kernel(in_hbm, out_ref, in_ref, rows_ref, sem):
+    copy = pltpu.make_async_copy(in_hbm, in_ref, sem)
+    copy.start()
+    copy.wait()
     unpack_one(in_ref, out_ref, rows_ref, 16, 0)
 
 
@@ -241,10 +244,6 @@
                 out_ref[at + per * i : at + per * i + 8, :] = tiles[i]
 
 
-def pack_kernel(in_ref, out_ref, rows_ref):
-    pack_one(in_ref, out_ref, rows_ref, 16, 0)
-
-
 def exchange(rows):
     per = rows.shape[0] // 64
     t = lax.all_to_all(rows.reshape(64, per, 128), SLAB, 0, 0, tiled=True)
@@ -310,17 +309,19 @@
     add_sides(tap_vectors(psf_ref, flip), core_ref, part_ref, passed_ref, swapped_ref, finish)
 
 
-def update_kernel(flip, psf_ref, core_ref, swapped_ref, passed_ref, part_ref, est_ref, y_ref, new_ref, out_ref):
-    y = split(y_ref[...])
-
+def update_kernel(
+    flip, psf_ref, core_ref, swapped_ref, passed_ref, part_ref, est_ref, y_ref, rows_ref, out_ref,
+    new_ref, turn_ref
+):
     def finish(z, acc):
         for i in range(16):
-            acc[i] = est_ref[i, z, :] * acc[i]
-            new_ref[i, z, :] = acc[i]
+            new_ref[i, z, :] = est_ref[i, z, :] * acc[i]
 
     add_sides(tap_vectors(psf_ref, flip), core_ref, part_ref, passed_ref, swapped_ref, finish)
+    y = split(y_ref[...])
     for i in range(16):
         out_ref[i] = dot(split(new_ref[i]), y)
+    pack_one(new_ref, rows_ref, turn_ref, 16, 0)
 
 
 def x_halo(v, psf, flip, later):
@@ -438,16 +439,29 @@
     )
     args = [slab, low, total, down, below, *low_mats]
     back, halo_below = call(first_low_kernel, BLOCK, args, 100, "first_low", save=halo)
-    est = call(unpack_kernel, BLOCK, [rode], 1, "unpack", [ROWS])
+    est = pl.pallas_call(
+        unpack_kernel,
+        out_shape=pltpu.VMEM(BLOCK, jnp.float32),
+        in_specs=[HBM],
+        out_specs=VMEM,
+        scratch_shapes=[
+            pltpu.VMEM(ROWS, jnp.float32),
+            pltpu.VMEM(ROWS, jnp.float32),
+            pltpu.SemaphoreType.DMA(()),
+        ],
+        cost_estimate=pl.CostEstimate(flops=10**9, bytes_accessed=10**6, transcendentals=0),
+        compiler_params=pltpu.CompilerParams(vmem_limit_bytes=LIMIT),
+        name="unpack",
+    )(pltpu.with_memory_space_constraint(rode, pltpu.HBM))
     sides, _ = x_halo(back, psf_x, True, ())
-    est, v = call(
+    est_rows, v = call(
         functools.partial(update_kernel, True),
-        [BLOCK, BLOCK],
+        [ROWS, BLOCK],
         [psf_x, core, *sides, est, yf],
         2,
         "update",
+        [BLOCK, ROWS],
     )
-    est_rows = call(pack_kernel, ROWS, [est], 1, "pack_est", [ROWS])
     sides, est_rows = x_halo(v, psf_x, False, est_rows)
     est_rows = exchange(est_rows)
     v = call(functools.partial(sides_kernel, False), BLOCK, [psf_x, core, *sides], 1, "x_sides")

time: 152 us -> 150 us (0.987)
    pallas_call x13 -> x11, Pallas kernels: 18.6 us -> 16.2 us  [call(): pl.pallas_call(kernel, out_shape=shapes, in_specs=[SMEM if a.ndim == 1 el...]
    pallas_call x0 -> x1, Pallas kernels: none -> 1.92 us  [per_device(): pl.pallas_call(unpack_kernel, out_shape=pltpu.VMEM(BLOCK, jnp.float32), i...]
  transfers between devices with their start and end apart: 11 -> 11, of which waited for: 4 -> 4; matrix products, arithmetic and copies ran while one was open for 0% -> 0% of each run, Pallas kernels for 10% -> 9%
where the time goes in v8:
time: 150 us; the launch traced here: 148 us
  starting transfers between devices  50.9 us (34%)
  waiting for transfers between devices  43.9 us (29%)
  blocking collectives  28.6 us (19%)
  Pallas kernels  23.2 us (15%)
    all_to_all x1, blocking collectives, exchange(): t = lax.all_to_all(rows.reshape(64, per, 128), SLAB, 0, 0, tiled=True)  28.6 us
    all_to_all x3, starting transfers between devices, exchange(): t = lax.all_to_all(rows.reshape(64, per, 128), SLAB, 0, 0, tiled=True)  26.3 us
    all_to_all x3, waiting for transfers between devices, exchange(): t = lax.all_to_all(rows.reshape(64, per, 128), SLAB, 0, 0, tiled=True)  26.1 us
    pallas_call x11, Pallas kernels, call(): pl.pallas_call(kernel, out_shape=shapes, in_specs=[SMEM if a.ndim == 1 el...  16.2 us
    ppermute x1, waiting for transfers between devices, per_device(): above = lax.ppermute(v, 'z', DOWN)  9.9 us
    ppermute x2, starting transfers between devices, x_halo(): passed = lax.ppermute(v, SLAB, NEXT)  8.81 us
    ppermute x1, waiting for transfers between devices, per_device(): above = lax.ppermute(down, 'z', DOWN)  6.17 us
    ppermute x1, starting transfers between devices, per_device(): below = lax.ppermute(up, 'z', UP)  4.67 us
  transfers between devices with their start and end apart: 11, of which 4 were waited for; matrix products, arithmetic and copies ran while one was open for 0% of the time, Pallas kernels for 9%

profile of v8, /device:TPU:1, one launch (start us, length us, event | category | flops | bytes accessed | tf_op | source)
XLA Modules:
  0.0 148.2 jit_solution(10024596623992228291)
XLA Ops:
  0.0 3.7 %first.1 = f32[2048,128]{1,0:T(8,128)} custom-call(f32[31]{0:T(128)} %psf_ref.7, f32[128,1024]{1,0:T(8,128)} %bitcast.16, f32[128,1024]{1,0:T(8,128)} %bitcast.19), custom_call_target="tpu_custom_call" | custom-call | tf_op jit(solution)/shard_map/first/pallas_call | solution.py:412
  3.7 11.8 %all-to-all-start = ((f32[64,32,128]{2,1,0:T(8,128)}), f32[64,32,128]{2,1,0:T(8,128)S(1)}, u32[]{:S(2)}, u32[]{:S(2)}) async-start(f32[64,32,128]{2,1,0:T(8,128)} %bitcast.4), calls=%async_computation | async-start | bytes 2097152 | tf_op jit(solution)/shard_map/all_to_all | solution.py:249
  15.5 0.9 prepare.1
  16.4 0.6 copy-done.6
  17.0 0.6 copy-done.9
  17.6 26.1 %all-to-all-done = f32[64,32,128]{2,1,0:T(8,128)S(1)} async-done(((f32[64,32,128]{2,1,0:T(8,128)}), f32[64,32,128]{2,1,0:T(8,128)S(1)}, u32[]{:S(2)}, u32[]{:S(2)}) %all-to-all-start) | async-done | bytes 1048608 | tf_op jit(solution)/shard_map/all_to_all | solution.py:249
  43.7 1.6 %arrive.1 = (f32[16,96,128]{2,1,0:T(8,128)S(1)}, f32[16,96,128]{2,1,0:T(8,128)S(1)}) custom-call(f32[2048,128]{1,0:T(8,128)S(1)} %bitcast.15, f32[128,128]{1,0:T(8,128)S(1)} %get-tuple-element.29.y_ref), custom_call_target="tpu_custom_call" | custom-call | flops 2000000000 | bytes 6000000 | tf_op jit(solution)/shard_map/arrive/pallas_call | solution.py:45
  45.3 1.3 collective-permute-start
  46.6 4.7 %collective-permute-start.1 = (f32[16,96,128]{2,1,0:T(8,128)S(1)}, f32[16,96,128]{2,1,0:T(8,128)S(1)}, u32[]{:S(2)}, u32[]{:S(2)}) collective-permute-start(f32[16,96,128]{2,1,0:T(8,128)S(1)} %get-tuple-element.30.up_ref), channel_id=1, source_target_pairs={{0,64},{64,128},{128,192},{192,256},{256,320},{320,384},{384,448},... | collective-permute-start | bytes 2359304 | tf_op jit(solution)/shard_map/ppermute | solution.py:432
  51.3 1.7 %turn.1 = (f32[1024,128]{1,0:T(8,128)}, f32[16,64,128]{2,1,0:T(8,128)}) custom-call(f32[128,1024]{1,0:T(8,128)S(1)} %bitcast.17, f32[16,96,128]{2,1,0:T(8,128)S(1)} %get-tuple-element.31.down_ref, f32[16,96,128]{2,1,0:T(8,128)S(1)} %get-tuple-element.30.up_ref), custom_call_target="tpu_custom_call" | custom-call | flops 1000000000 | bytes 3000000 | tf_op jit(solution)/shard_map/turn/pallas_call | solution.py:45
  52.9 7.0 %all-to-all-start.1 = ((f32[64,16,128]{2,1,0:T(8,128)}), f32[64,16,128]{2,1,0:T(8,128)}, u32[]{:S(2)}, u32[]{:S(2)}) async-start(f32[64,16,128]{2,1,0:T(8,128)} %bitcast.6), calls=%async_computation.1 | async-start | bytes 1048576 | tf_op jit(solution)/shard_map/all_to_all | solution.py:249
  59.9 6.2 %collective-permute-done.above_ref = f32[16,96,128]{2,1,0:T(8,128)} collective-permute-done((f32[16,96,128]{2,1,0:T(8,128)S(1)}, f32[16,96,128]{2,1,0:T(8,128)}, u32[]{:S(2)}, u32[]{:S(2)}) %collective-permute-start) | collective-permute-done | bytes 786464 | tf_op jit(solution)/shard_map/ppermute | solution.py:433
  66.1 2.1 %first_high.1 = (f32[16,64,128]{2,1,0:T(8,128)S(1)}, f32[16,64,128]{2,1,0:T(8,128)S(1)}, f32[16,32,128]{2,1,0:T(8,128)}) custom-call(s32[1]{0:T(128)} %bitcast.slab_ref, f32[16,96,128]{2,1,0:T(8,128)S(1)} %get-tuple-element.30.up_ref, f32[16,96,128]{2,1,0:T(8,128)} %collective-permute-done.above_ref, f32[128,64]{1,0:T(8,128)S(1)} %get-tuple-element.32.zo_ref, ...), custom_call_target="tpu_custom_call" | custom-call | flops 1000000000 | bytes 3000000 | tf_op jit(solution)/shard_map/first_high/pallas_call | solution.py:45
  68.3 1.3 first_low.1
  69.6 5.2 %collective-permute-start.3 = (f32[16,64,128]{2,1,0:T(8,128)S(1)}, f32[16,64,128]{2,1,0:T(8,128)S(1)}, u32[]{:S(2)}, u32[]{:S(2)}) collective-permute-start(f32[16,64,128]{2,1,0:T(8,128)S(1)} %get-tuple-element.40.own_ref), channel_id=1, source_target_pairs={{8,1},{2,9},{10,3},{4,11},{12,5},{6,13},{14,7},{16,15},{24,17},{18... | collective-permute-start | bytes 1572872 | tf_op jit(solution)/shard_map/ppermute | solution.py:328
  74.7 1.9 %collective-permute-start.2 = (f32[16,64,128]{2,1,0:T(8,128)S(1)}, f32[16,64,128]{2,1,0:T(8,128)S(1)}, u32[]{:S(2)}, u32[]{:S(2)}) collective-permute-start(f32[16,64,128]{2,1,0:T(8,128)S(1)} %get-tuple-element.40.own_ref), channel_id=1, source_target_pairs={{0,1},{1,0},{2,3},{3,2},{4,5},{5,4},{6,7},{7,6},{8,9},{9,8},{10,11... | collective-permute-start | bytes 1572872 | tf_op jit(solution)/shard_map/ppermute | solution.py:329
  76.7 1.2 x_own.2.part_ref
  77.9 1.9 %unpack.1.est_ref = f32[16,64,128]{2,1,0:T(8,128)S(1)} custom-call(f32[1024,128]{1,0:T(8,128)} %bitcast.7.in_hbm), custom_call_target="tpu_custom_call" | custom-call | flops 1000000000 | bytes 1000000 | tf_op jit(solution)/shard_map/unpack/pallas_call | solution.py:442
  79.8 1.8 %collective-permute-done.3.passed_ref = f32[16,64,128]{2,1,0:T(8,128)S(1)} collective-permute-done((f32[16,64,128]{2,1,0:T(8,128)S(1)}, f32[16,64,128]{2,1,0:T(8,128)S(1)}, u32[]{:S(2)}, u32[]{:S(2)}) %collective-permute-start.3) | collective-permute-done | bytes 524320 | tf_op jit(solution)/shard_map/ppermute | solution.py:328
  81.6 2.9 %update.1 = (f32[1024,128]{1,0:T(8,128)}, f32[16,64,128]{2,1,0:T(8,128)S(1)}) custom-call(f32[31]{0:T(128)S(1)} %copy-done.1, s32[1]{0:T(128)} %bitcast.1.core_ref, f32[16,64,128]{2,1,0:T(8,128)S(1)} %collective-permute-done.2.swapped_ref, f32[16,64,128]{2,1,0:T(8,128)S(1)} %collective-permute-done.3.passed_ref, f32[16,64,128]{2,1,0:T(8,128)S(1)} %x_own.2.part_ref, ...), custom_call_target="tpu_custom_call" | custom-call | flops 2000000000 | bytes 6000000 | tf_op jit(solution)/shard_map/update/pallas_call | solution.py:45
  84.5 3.7 %collective-permute-start.5 = (f32[16,64,128]{2,1,0:T(8,128)S(1)}, f32[16,64,128]{2,1,0:T(8,128)S(1)}, u32[]{:S(2)}, u32[]{:S(2)}) collective-permute-start(f32[16,64,128]{2,1,0:T(8,128)S(1)} %get-tuple-element.42.own_ref), channel_id=1, source_target_pairs={{8,1},{2,9},{10,3},{4,11},{12,5},{6,13},{14,7},{16,15},{24,17},{18... | collective-permute-start | bytes 1572872 | tf_op jit(solution)/shard_map/ppermute | solution.py:328
  88.1 1.9 %collective-permute-start.4 = (f32[16,64,128]{2,1,0:T(8,128)S(1)}, f32[16,64,128]{2,1,0:T(8,128)S(1)}, u32[]{:S(2)}, u32[]{:S(2)}) collective-permute-start(f32[16,64,128]{2,1,0:T(8,128)S(1)} %get-tuple-element.42.own_ref), channel_id=1, source_target_pairs={{0,1},{1,0},{2,3},{3,2},{4,5},{5,4},{6,7},{7,6},{8,9},{9,8},{10,11... | collective-permute-start | bytes 1572872 | tf_op jit(solution)/shard_map/ppermute | solution.py:329
  90.1 1.2 x_own.3.part_ref
  91.3 7.5 %all-to-all-start.3 = ((f32[64,16,128]{2,1,0:T(8,128)}), f32[64,16,128]{2,1,0:T(8,128)S(1)}, u32[]{:S(2)}, u32[]{:S(2)}) async-start(f32[64,16,128]{2,1,0:T(8,128)} %bitcast.10), calls=%async_computation.3 | async-start | bytes 1048576 | tf_op jit(solution)/shard_map/all_to_all | solution.py:249
  98.9 1.2 x_sides.1.v_ref
  100.1 1.3 collective-permute-start.6
  101.4 4.7 %collective-permute-start.7 = (f32[16,64,128]{2,1,0:T(8,128)S(1)}, f32[16,64,128]{2,1,0:T(8,128)S(1)}, u32[]{:S(2)}, u32[]{:S(2)}) collective-permute-start(f32[16,64,128]{2,1,0:T(8,128)S(1)} %x_sides.1.v_ref), channel_id=1, source_target_pairs={{0,64},{64,128},{128,192},{192,256},{256,320},{320,384},{384,448},... | collective-permute-start | bytes 1572872 | tf_op jit(solution)/shard_map/ppermute | solution.py:469
  106.0 9.9 %collective-permute-done.6.above_ref = f32[16,64,128]{2,1,0:T(8,128)S(1)} collective-permute-done((f32[16,64,128]{2,1,0:T(8,128)S(1)}, f32[16,64,128]{2,1,0:T(8,128)S(1)}, u32[]{:S(2)}, u32[]{:S(2)}) %collective-permute-start.6) | collective-permute-done | bytes 524320 | tf_op jit(solution)/shard_map/ppermute | solution.py:470
  116.0 1.0 ratio_high.1
  117.0 1.2 ratio_low.1
  118.2 28.6 %all_to_all.20 = f32[64,16,128]{2,1,0:T(8,128)S(1)} all-to-all(f32[64,16,128]{2,1,0:T(8,128)S(1)} %bitcast.18), channel_id=1, replica_groups=mesh['z'=8,'x'=4,'yl'=2,'yh'=4,'c'=2] {'x','yl','yh','c'}, dimensions={0} | all-to-all | bytes 1048576 | tf_op jit(solution)/shard_map/all_to_all | solution.py:249
  146.8 1.4 last.1
  (31 shorter events, 0.1 us)
Async XLA Ops:
  3.7 11.8 %copy-start.1 = (f32[31]{0:T(128)S(1)}, f32[31]{0:T(128)}, u32[]{:S(2)}) copy-start(f32[31]{0:T(128)} %psf_ref.7) | copy-start | bytes 376
  3.7 11.8 %copy-start.2 = (f32[31]{0:T(128)S(1)}, f32[31]{0:T(128)}, u32[]{:S(2)}) copy-start(f32[31]{0:T(128)} %psf_y_ref.1) | copy-start | bytes 376
  3.7 11.8 %copy-start.3 = (f32[63]{0:T(128)S(1)}, f32[63]{0:T(128)}, u32[]{:S(2)}) copy-start(f32[63]{0:T(128)} %psf_z_ref.1) | copy-start | bytes 760
  3.7 40.0 %all-to-all-start = ((f32[64,32,128]{2,1,0:T(8,128)}), f32[64,32,128]{2,1,0:T(8,128)S(1)}, u32[]{:S(2)}, u32[]{:S(2)}) async-start(f32[64,32,128]{2,1,0:T(8,128)} %bitcast.4), calls=%async_computation | async-start | bytes 2097152 | tf_op jit(solution)/shard_map/all_to_all | solution.py:249
  16.4 0.6 copy-start.6
  17.0 0.6 copy-start.9
  43.7 7.6 %copy-start = (f32[8,16,1024]{2,1,0:T(8,128)S(1)}, f32[8,16,1024]{2,1,0:T(8,128)}, u32[]{:S(2)}) copy-start(f32[8,16,1024]{2,1,0:T(8,128)} %param.6) | copy-start | bytes 1572868
  45.3 20.9 %collective-permute-start = (f32[16,96,128]{2,1,0:T(8,128)S(1)}, f32[16,96,128]{2,1,0:T(8,128)}, u32[]{:S(2)}, u32[]{:S(2)}) collective-permute-start(f32[16,96,128]{2,1,0:T(8,128)S(1)} %get-tuple-element.31.down_ref), channel_id=1, source_target_pairs={{64,0},{128,64},{192,128},{256,192},{320,256},{384,320},{448,384},... | collective-permute-start | bytes 2359304 | tf_op jit(solution)/shard_map/ppermute | solution.py:433
  46.6 21.7 %collective-permute-start.1 = (f32[16,96,128]{2,1,0:T(8,128)S(1)}, f32[16,96,128]{2,1,0:T(8,128)S(1)}, u32[]{:S(2)}, u32[]{:S(2)}) collective-permute-start(f32[16,96,128]{2,1,0:T(8,128)S(1)} %get-tuple-element.30.up_ref), channel_id=1, source_target_pairs={{0,64},{64,128},{128,192},{192,256},{256,320},{320,384},{384,448},... | collective-permute-start | bytes 2359304 | tf_op jit(solution)/shard_map/ppermute | solution.py:432
  52.9 25.0 %all-to-all-start.1 = ((f32[64,16,128]{2,1,0:T(8,128)}), f32[64,16,128]{2,1,0:T(8,128)}, u32[]{:S(2)}, u32[]{:S(2)}) async-start(f32[64,16,128]{2,1,0:T(8,128)} %bitcast.6), calls=%async_computation.1 | async-start | bytes 1048576 | tf_op jit(solution)/shard_map/all_to_all | solution.py:249
  66.1 2.2 %copy-start.7 = (f32[64,64]{1,0:T(8,128)S(1)}, f32[64,64]{1,0:T(8,128)}, u32[]{:S(2)}) copy-start(f32[64,64]{1,0:T(8,128)} %copy-done.6) | copy-start | bytes 49156
  66.1 2.2 %copy-start.10 = (f32[64,64]{1,0:T(8,128)S(1)}, f32[64,64]{1,0:T(8,128)}, u32[]{:S(2)}) copy-start(f32[64,64]{1,0:T(8,128)} %copy-done.9) | copy-start | bytes 49156
  69.6 12.0 %collective-permute-start.3 = (f32[16,64,128]{2,1,0:T(8,128)S(1)}, f32[16,64,128]{2,1,0:T(8,128)S(1)}, u32[]{:S(2)}, u32[]{:S(2)}) collective-permute-start(f32[16,64,128]{2,1,0:T(8,128)S(1)} %get-tuple-element.40.own_ref), channel_id=1, source_target_pairs={{8,1},{2,9},{10,3},{4,11},{12,5},{6,13},{14,7},{16,15},{24,17},{18... | collective-permute-start | bytes 1572872 | tf_op jit(solution)/shard_map/ppermute | solution.py:328
  74.7 6.9 %collective-permute-start.2 = (f32[16,64,128]{2,1,0:T(8,128)S(1)}, f32[16,64,128]{2,1,0:T(8,128)S(1)}, u32[]{:S(2)}, u32[]{:S(2)}) collective-permute-start(f32[16,64,128]{2,1,0:T(8,128)S(1)} %get-tuple-element.40.own_ref), channel_id=1, source_target_pairs={{0,1},{1,0},{2,3},{3,2},{4,5},{5,4},{6,7},{7,6},{8,9},{9,8},{10,11... | collective-permute-start | bytes 1572872 | tf_op jit(solution)/shard_map/ppermute | solution.py:329
  84.5 14.4 %collective-permute-start.5 = (f32[16,64,128]{2,1,0:T(8,128)S(1)}, f32[16,64,128]{2,1,0:T(8,128)S(1)}, u32[]{:S(2)}, u32[]{:S(2)}) collective-permute-start(f32[16,64,128]{2,1,0:T(8,128)S(1)} %get-tuple-element.42.own_ref), channel_id=1, source_target_pairs={{8,1},{2,9},{10,3},{4,11},{12,5},{6,13},{14,7},{16,15},{24,17},{18... | collective-permute-start | bytes 1572872 | tf_op jit(solution)/shard_map/ppermute | solution.py:328
  88.1 10.7 %collective-permute-start.4 = (f32[16,64,128]{2,1,0:T(8,128)S(1)}, f32[16,64,128]{2,1,0:T(8,128)S(1)}, u32[]{:S(2)}, u32[]{:S(2)}) collective-permute-start(f32[16,64,128]{2,1,0:T(8,128)S(1)} %get-tuple-element.42.own_ref), channel_id=1, source_target_pairs={{0,1},{1,0},{2,3},{3,2},{4,5},{5,4},{6,7},{7,6},{8,9},{9,8},{10,11... | collective-permute-start | bytes 1572872 | tf_op jit(solution)/shard_map/ppermute | solution.py:329
  91.3 26.9 %all-to-all-start.3 = ((f32[64,16,128]{2,1,0:T(8,128)}), f32[64,16,128]{2,1,0:T(8,128)S(1)}, u32[]{:S(2)}, u32[]{:S(2)}) async-start(f32[64,16,128]{2,1,0:T(8,128)} %bitcast.10), calls=%async_computation.3 | async-start | bytes 1048576 | tf_op jit(solution)/shard_map/all_to_all | solution.py:249
  98.8 17.1 %copy-start.4 = (f32[16,64,128]{2,1,0:T(8,128)S(1)}, f32[16,64,128]{2,1,0:T(8,128)}, u32[]{:S(2)}) copy-start(f32[16,64,128]{2,1,0:T(8,128)} %get-tuple-element.46.obs_ref) | copy-start | bytes 1572868
  98.8 17.1 %copy-start.5 = (f32[16,32,128]{2,1,0:T(8,128)S(1)}, f32[16,32,128]{2,1,0:T(8,128)}, u32[]{:S(2)}) copy-start(f32[16,32,128]{2,1,0:T(8,128)} %get-tuple-element.45.halo_ref) | copy-start | bytes 786436
  100.1 15.9 %collective-permute-start.6 = (f32[16,64,128]{2,1,0:T(8,128)S(1)}, f32[16,64,128]{2,1,0:T(8,128)S(1)}, u32[]{:S(2)}, u32[]{:S(2)}) collective-permute-start(f32[16,64,128]{2,1,0:T(8,128)S(1)} %x_sides.1.v_ref), channel_id=1, source_target_pairs={{64,0},{128,64},{192,128},{256,192},{320,256},{384,320},{448,384},... | collective-permute-start | bytes 1572872 | tf_op jit(solution)/shard_map/ppermute | solution.py:470
  101.4 15.6 %collective-permute-start.7 = (f32[16,64,128]{2,1,0:T(8,128)S(1)}, f32[16,64,128]{2,1,0:T(8,128)S(1)}, u32[]{:S(2)}, u32[]{:S(2)}) collective-permute-start(f32[16,64,128]{2,1,0:T(8,128)S(1)} %x_sides.1.v_ref), channel_id=1, source_target_pairs={{0,64},{64,128},{128,192},{192,256},{256,320},{320,384},{384,448},... | collective-permute-start | bytes 1572872 | tf_op jit(solution)/shard_map/ppermute | solution.py:469
  116.0 1.0 copy-start.8
  116.0 1.0 copy-start.11
  116.0 1.0 copy-start.12

commit v9 on v8

--- a/solution.py
+++ b/solution.py
@@ -288,10 +288,10 @@
     over_planes(body)
 
 
-def add_sides(w, core_ref, part_ref, passed_ref, swapped_ref, finish):
+def add_sides(w, core_ref, start, passed_ref, swapped_ref, finish):
     def run(shift):
         def body(z):
-            acc = [part_ref[i, z, :] for i in range(16)]
+            acc = start(z)
             acc = add_block(w, swapped_ref, z, acc, shift)
             finish(z, add_block(w, passed_ref, z, acc, -shift))
 
@@ -301,12 +301,17 @@
     pl.when(core_ref[0] != 0)(lambda: run(-16))
 
 
-def sides_kernel(flip, psf_ref, core_ref, swapped_ref, passed_ref, part_ref, out_ref):
+def x_kernel(flip, psf_ref, core_ref, swapped_ref, passed_ref, own_ref, out_ref):
+    w = tap_vectors(psf_ref, flip)
+
+    def start(z):
+        return add_block(w, own_ref, z, [None] * 16, 0)
+
     def finish(z, acc):
         for i in range(16):
             out_ref[i, z, :] = acc[i]
 
-    add_sides(tap_vectors(psf_ref, flip), core_ref, part_ref, passed_ref, swapped_ref, finish)
+    add_sides(w, core_ref, start, passed_ref, swapped_ref, finish)
 
 
 def update_kernel(
@@ -317,19 +322,21 @@
         for i in range(16):
             new_ref[i, z, :] = est_ref[i, z, :] * acc[i]
 
-    add_sides(tap_vectors(psf_ref, flip), core_ref, part_ref, passed_ref, swapped_ref, finish)
+    def start(z):
+        return [part_ref[i, z, :] for i in range(16)]
+
+    w = tap_vectors(psf_ref, flip)
+    add_sides(w, core_ref, start, passed_ref, swapped_ref, finish)
     y = split(y_ref[...])
     for i in range(16):
         out_ref[i] = dot(split(new_ref[i]), y)
     pack_one(new_ref, rows_ref, turn_ref, 16, 0)
 
 
-def x_halo(v, psf, flip, later):
+def x_halo(v):
+    swapped = lax.ppermute(v, "c", SWAP)
     passed = lax.ppermute(v, SLAB, NEXT)
-    swapped = lax.ppermute(v, "c", SWAP)
-    part = call(functools.partial(own_x_kernel, flip), BLOCK, [psf, v], 1.3, "x_own")
-    later, part = lax.optimization_barrier((later, part))
-    return [swapped, passed, part], later
+    return [swapped, passed]
 
 
 def high_planes(slab_ref, v_ref, above_ref, obs, mats, sum_ref, low_ref):
@@ -453,7 +460,8 @@
         compiler_params=pltpu.CompilerParams(vmem_limit_bytes=LIMIT),
         name="unpack",
     )(pltpu.with_memory_space_constraint(rode, pltpu.HBM))
-    sides, _ = x_halo(back, psf_x, True, ())
+    part = call(functools.partial(own_x_kernel, True), BLOCK, [psf_x, back], 1.3, "x_own")
+    sides = [*x_halo(back), part]
     est_rows, v = call(
         functools.partial(update_kernel, True),
         [ROWS, BLOCK],
@@ -462,9 +470,9 @@
         "update",
         [BLOCK, ROWS],
     )
-    sides, est_rows = x_halo(v, psf_x, False, est_rows)
+    args = [psf_x, core, *x_halo(v), v]
     est_rows = exchange(est_rows)
-    v = call(functools.partial(sides_kernel, False), BLOCK, [psf_x, core, *sides], 1, "x_sides")
+    v = call(functools.partial(x_kernel, False), BLOCK, args, 100, "x_all")
 
     below = lax.ppermute(v, "z", UP)
     above = lax.ppermute(v, "z", DOWN)

time: 150 us -> 150 us (level)
    pallas_call x11 -> x10, Pallas kernels: 16.2 us -> 15.7 us  [call(): pl.pallas_call(kernel, out_shape=shapes, in_specs=[SMEM if a.ndim == 1 el...]
where the time goes in v9:
time: 150 us; the launch traced here: 148 us
  starting transfers between devices  50.9 us (34%)
  waiting for transfers between devices  43.9 us (29%)
  blocking collectives  28.6 us (19%)
  Pallas kernels  22.6 us (15%)
    all_to_all x1, blocking collectives, exchange(): t = lax.all_to_all(rows.reshape(64, per, 128), SLAB, 0, 0, tiled=True)  28.6 us
    all_to_all x3, starting transfers between devices, exchange(): t = lax.all_to_all(rows.reshape(64, per, 128), SLAB, 0, 0, tiled=True)  26.3 us
    all_to_all x3, waiting for transfers between devices, exchange(): t = lax.all_to_all(rows.reshape(64, per, 128), SLAB, 0, 0, tiled=True)  26.1 us
    pallas_call x10, Pallas kernels, call(): pl.pallas_call(kernel, out_shape=shapes, in_specs=[SMEM if a.ndim == 1 el...  15.7 us
    ppermute x1, waiting for transfers between devices, per_device(): above = lax.ppermute(v, 'z', DOWN)  9.91 us
    ppermute x2, starting transfers between devices, x_halo(): passed = lax.ppermute(v, SLAB, NEXT)  8.81 us
    ppermute x1, waiting for transfers between devices, per_device(): above = lax.ppermute(down, 'z', DOWN)  6.17 us
    ppermute x1, starting transfers between devices, per_device(): below = lax.ppermute(up, 'z', UP)  4.67 us
  transfers between devices with their start and end apart: 11, of which 4 were waited for; matrix products, arithmetic and copies ran while one was open for 0% of the time, Pallas kernels for 9%

profile of v9, /device:TPU:1, one launch (start us, length us, event | category | flops | bytes accessed | tf_op | source)
XLA Modules:
  0.0 147.6 jit_solution(3513124370166961380)
XLA Ops:
  0.0 3.7 %first.1 = f32[2048,128]{1,0:T(8,128)} custom-call(f32[31]{0:T(128)} %psf_ref.5, f32[128,1024]{1,0:T(8,128)} %bitcast.16, f32[128,1024]{1,0:T(8,128)} %bitcast.19), custom_call_target="tpu_custom_call" | custom-call | tf_op jit(solution)/shard_map/first/pallas_call | solution.py:419
  3.7 0.0 copy-start.1
  3.7 11.8 %all-to-all-start = ((f32[64,32,128]{2,1,0:T(8,128)}), f32[64,32,128]{2,1,0:T(8,128)S(1)}, u32[]{:S(2)}, u32[]{:S(2)}) async-start(f32[64,32,128]{2,1,0:T(8,128)} %bitcast.4), calls=%async_computation | async-start | bytes 2097152 | tf_op jit(solution)/shard_map/all_to_all | solution.py:249
  15.5 0.9 prepare.1
  16.4 0.6 copy-done.6
  17.0 0.6 copy-done.9
  17.6 26.1 %all-to-all-done = f32[64,32,128]{2,1,0:T(8,128)S(1)} async-done(((f32[64,32,128]{2,1,0:T(8,128)}), f32[64,32,128]{2,1,0:T(8,128)S(1)}, u32[]{:S(2)}, u32[]{:S(2)}) %all-to-all-start) | async-done | bytes 1048608 | tf_op jit(solution)/shard_map/all_to_all | solution.py:249
  43.7 1.6 %arrive.1 = (f32[16,96,128]{2,1,0:T(8,128)S(1)}, f32[16,96,128]{2,1,0:T(8,128)S(1)}) custom-call(f32[2048,128]{1,0:T(8,128)S(1)} %bitcast.15, f32[128,128]{1,0:T(8,128)S(1)} %get-tuple-element.27.y_ref), custom_call_target="tpu_custom_call" | custom-call | flops 2000000000 | bytes 6000000 | tf_op jit(solution)/shard_map/arrive/pallas_call | solution.py:45
  45.3 1.3 collective-permute-start
  46.6 4.7 %collective-permute-start.1 = (f32[16,96,128]{2,1,0:T(8,128)S(1)}, f32[16,96,128]{2,1,0:T(8,128)S(1)}, u32[]{:S(2)}, u32[]{:S(2)}) collective-permute-start(f32[16,96,128]{2,1,0:T(8,128)S(1)} %get-tuple-element.28.up_ref), channel_id=1, source_target_pairs={{0,64},{64,128},{128,192},{192,256},{256,320},{320,384},{384,448},... | collective-permute-start | bytes 2359304 | tf_op jit(solution)/shard_map/ppermute | solution.py:439
  51.3 1.7 %turn.1 = (f32[1024,128]{1,0:T(8,128)}, f32[16,64,128]{2,1,0:T(8,128)}) custom-call(f32[128,1024]{1,0:T(8,128)S(1)} %bitcast.17, f32[16,96,128]{2,1,0:T(8,128)S(1)} %get-tuple-element.29.down_ref, f32[16,96,128]{2,1,0:T(8,128)S(1)} %get-tuple-element.28.up_ref), custom_call_target="tpu_custom_call" | custom-call | flops 1000000000 | bytes 3000000 | tf_op jit(solution)/shard_map/turn/pallas_call | solution.py:45
  52.9 7.0 %all-to-all-start.1 = ((f32[64,16,128]{2,1,0:T(8,128)}), f32[64,16,128]{2,1,0:T(8,128)}, u32[]{:S(2)}, u32[]{:S(2)}) async-start(f32[64,16,128]{2,1,0:T(8,128)} %bitcast.6), calls=%async_computation.1 | async-start | bytes 1048576 | tf_op jit(solution)/shard_map/all_to_all | solution.py:249
  59.9 6.2 %collective-permute-done.above_ref = f32[16,96,128]{2,1,0:T(8,128)} collective-permute-done((f32[16,96,128]{2,1,0:T(8,128)S(1)}, f32[16,96,128]{2,1,0:T(8,128)}, u32[]{:S(2)}, u32[]{:S(2)}) %collective-permute-start) | collective-permute-done | bytes 786464 | tf_op jit(solution)/shard_map/ppermute | solution.py:440
  66.1 2.1 %first_high.1 = (f32[16,64,128]{2,1,0:T(8,128)S(1)}, f32[16,64,128]{2,1,0:T(8,128)S(1)}, f32[16,32,128]{2,1,0:T(8,128)}) custom-call(s32[1]{0:T(128)} %bitcast.slab_ref, f32[16,96,128]{2,1,0:T(8,128)S(1)} %get-tuple-element.28.up_ref, f32[16,96,128]{2,1,0:T(8,128)} %collective-permute-done.above_ref, f32[128,64]{1,0:T(8,128)S(1)} %get-tuple-element.30.zo_ref, ...), custom_call_target="tpu_custom_call" | custom-call | flops 1000000000 | bytes 3000000 | tf_op jit(solution)/shard_map/first_high/pallas_call | solution.py:45
  68.3 1.3 first_low.1
  69.6 5.2 %collective-permute-start.3 = (f32[16,64,128]{2,1,0:T(8,128)S(1)}, f32[16,64,128]{2,1,0:T(8,128)S(1)}, u32[]{:S(2)}, u32[]{:S(2)}) collective-permute-start(f32[16,64,128]{2,1,0:T(8,128)S(1)} %get-tuple-element.38.own_ref), channel_id=1, source_target_pairs={{8,1},{2,9},{10,3},{4,11},{12,5},{6,13},{14,7},{16,15},{24,17},{18... | collective-permute-start | bytes 1572872 | tf_op jit(solution)/shard_map/ppermute | solution.py:338
  74.7 1.9 %collective-permute-start.2 = (f32[16,64,128]{2,1,0:T(8,128)S(1)}, f32[16,64,128]{2,1,0:T(8,128)S(1)}, u32[]{:S(2)}, u32[]{:S(2)}) collective-permute-start(f32[16,64,128]{2,1,0:T(8,128)S(1)} %get-tuple-element.38.own_ref), channel_id=1, source_target_pairs={{0,1},{1,0},{2,3},{3,2},{4,5},{5,4},{6,7},{7,6},{8,9},{9,8},{10,11... | collective-permute-start | bytes 1572872 | tf_op jit(solution)/shard_map/ppermute | solution.py:337
  76.7 1.2 x_own.1.part_ref
  77.9 1.9 %unpack.1.est_ref = f32[16,64,128]{2,1,0:T(8,128)S(1)} custom-call(f32[1024,128]{1,0:T(8,128)} %bitcast.7.in_hbm), custom_call_target="tpu_custom_call" | custom-call | flops 1000000000 | bytes 1000000 | tf_op jit(solution)/shard_map/unpack/pallas_call | solution.py:449
  79.8 1.8 %collective-permute-done.3.passed_ref = f32[16,64,128]{2,1,0:T(8,128)S(1)} collective-permute-done((f32[16,64,128]{2,1,0:T(8,128)S(1)}, f32[16,64,128]{2,1,0:T(8,128)S(1)}, u32[]{:S(2)}, u32[]{:S(2)}) %collective-permute-start.3) | collective-permute-done | bytes 524320 | tf_op jit(solution)/shard_map/ppermute | solution.py:338
  81.6 2.9 %update.1 = (f32[1024,128]{1,0:T(8,128)}, f32[16,64,128]{2,1,0:T(8,128)S(1)}) custom-call(f32[31]{0:T(128)S(1)} %copy-done.1, s32[1]{0:T(128)} %bitcast.1.core_ref, f32[16,64,128]{2,1,0:T(8,128)S(1)} %collective-permute-done.2.swapped_ref, f32[16,64,128]{2,1,0:T(8,128)S(1)} %collective-permute-done.3.passed_ref, f32[16,64,128]{2,1,0:T(8,128)S(1)} %x_own.1.part_ref, ...), custom_call_target="tpu_custom_call" | custom-call | flops 2000000000 | bytes 6000000 | tf_op jit(solution)/shard_map/update/pallas_call | solution.py:45
  84.5 3.7 %collective-permute-start.5 = (f32[16,64,128]{2,1,0:T(8,128)S(1)}, f32[16,64,128]{2,1,0:T(8,128)S(1)}, u32[]{:S(2)}, u32[]{:S(2)}) collective-permute-start(f32[16,64,128]{2,1,0:T(8,128)S(1)} %get-tuple-element.40.own_ref), channel_id=1, source_target_pairs={{8,1},{2,9},{10,3},{4,11},{12,5},{6,13},{14,7},{16,15},{24,17},{18... | collective-permute-start | bytes 1572872 | tf_op jit(solution)/shard_map/ppermute | solution.py:338
  88.1 1.9 %collective-permute-start.4 = (f32[16,64,128]{2,1,0:T(8,128)S(1)}, f32[16,64,128]{2,1,0:T(8,128)S(1)}, u32[]{:S(2)}, u32[]{:S(2)}) collective-permute-start(f32[16,64,128]{2,1,0:T(8,128)S(1)} %get-tuple-element.40.own_ref), channel_id=1, source_target_pairs={{0,1},{1,0},{2,3},{3,2},{4,5},{5,4},{6,7},{7,6},{8,9},{9,8},{10,11... | collective-permute-start | bytes 1572872 | tf_op jit(solution)/shard_map/ppermute | solution.py:337
  90.1 7.5 %all-to-all-start.3 = ((f32[64,16,128]{2,1,0:T(8,128)}), f32[64,16,128]{2,1,0:T(8,128)S(1)}, u32[]{:S(2)}, u32[]{:S(2)}) async-start(f32[64,16,128]{2,1,0:T(8,128)} %bitcast.10), calls=%async_computation.3 | async-start | bytes 1048576 | tf_op jit(solution)/shard_map/all_to_all | solution.py:249
  97.6 1.9 %x_all.1.v_ref = f32[16,64,128]{2,1,0:T(8,128)S(1)} custom-call(f32[31]{0:T(128)S(1)} %copy-done.1, s32[1]{0:T(128)} %bitcast.1.core_ref, f32[16,64,128]{2,1,0:T(8,128)S(1)} %collective-permute-done.4.swapped_ref, f32[16,64,128]{2,1,0:T(8,128)S(1)} %collective-permute-done.5.passed_ref, f32[16,64,128]{2,1,0:T(8,128)S(1)} %get-tuple-element.40.own_ref), custom_call_target="tpu_custom_call" | custom-call | flops 99999997952 | bytes 300000000 | tf_op jit(solution)/shard_map/x_all/pallas_call | solution.py:45
  99.5 1.3 collective-permute-start.6
  100.8 4.7 %collective-permute-start.7 = (f32[16,64,128]{2,1,0:T(8,128)S(1)}, f32[16,64,128]{2,1,0:T(8,128)S(1)}, u32[]{:S(2)}, u32[]{:S(2)}) collective-permute-start(f32[16,64,128]{2,1,0:T(8,128)S(1)} %x_all.1.v_ref), channel_id=1, source_target_pairs={{0,64},{64,128},{128,192},{192,256},{256,320},{320,384},{384,448},... | collective-permute-start | bytes 1572872 | tf_op jit(solution)/shard_map/ppermute | solution.py:477
  105.5 9.9 %collective-permute-done.6.above_ref = f32[16,64,128]{2,1,0:T(8,128)S(1)} collective-permute-done((f32[16,64,128]{2,1,0:T(8,128)S(1)}, f32[16,64,128]{2,1,0:T(8,128)S(1)}, u32[]{:S(2)}, u32[]{:S(2)}) %collective-permute-start.6) | collective-permute-done | bytes 524320 | tf_op jit(solution)/shard_map/ppermute | solution.py:478
  115.4 1.0 ratio_high.1
  116.4 1.2 ratio_low.1
  117.6 28.6 %all_to_all.20 = f32[64,16,128]{2,1,0:T(8,128)S(1)} all-to-all(f32[64,16,128]{2,1,0:T(8,128)S(1)} %bitcast.18), channel_id=1, replica_groups=mesh['z'=8,'x'=4,'yl'=2,'yh'=4,'c'=2] {'x','yl','yh','c'}, dimensions={0} | all-to-all | bytes 1048576 | tf_op jit(solution)/shard_map/all_to_all | solution.py:249
  146.2 1.4 last.1
  (30 shorter events, 0.1 us)
Async XLA Ops:
  3.7 11.8 %copy-start.1 = (f32[31]{0:T(128)S(1)}, f32[31]{0:T(128)}, u32[]{:S(2)}) copy-start(f32[31]{0:T(128)} %psf_ref.5) | copy-start | bytes 376
  3.7 11.8 %copy-start.2 = (f32[31]{0:T(128)S(1)}, f32[31]{0:T(128)}, u32[]{:S(2)}) copy-start(f32[31]{0:T(128)} %psf_y_ref.1) | copy-start | bytes 376
  3.7 11.8 %copy-start.3 = (f32[63]{0:T(128)S(1)}, f32[63]{0:T(128)}, u32[]{:S(2)}) copy-start(f32[63]{0:T(128)} %psf_z_ref.1) | copy-start | bytes 760
  3.7 40.0 %all-to-all-start = ((f32[64,32,128]{2,1,0:T(8,128)}), f32[64,32,128]{2,1,0:T(8,128)S(1)}, u32[]{:S(2)}, u32[]{:S(2)}) async-start(f32[64,32,128]{2,1,0:T(8,128)} %bitcast.4), calls=%async_computation | async-start | bytes 2097152 | tf_op jit(solution)/shard_map/all_to_all | solution.py:249
  16.4 0.6 copy-start.6
  17.0 0.6 copy-start.9
  43.7 7.6 %copy-start = (f32[8,16,1024]{2,1,0:T(8,128)S(1)}, f32[8,16,1024]{2,1,0:T(8,128)}, u32[]{:S(2)}) copy-start(f32[8,16,1024]{2,1,0:T(8,128)} %param.6) | copy-start | bytes 1572868
  45.3 20.9 %collective-permute-start = (f32[16,96,128]{2,1,0:T(8,128)S(1)}, f32[16,96,128]{2,1,0:T(8,128)}, u32[]{:S(2)}, u32[]{:S(2)}) collective-permute-start(f32[16,96,128]{2,1,0:T(8,128)S(1)} %get-tuple-element.29.down_ref), channel_id=1, source_target_pairs={{64,0},{128,64},{192,128},{256,192},{320,256},{384,320},{448,384},... | collective-permute-start | bytes 2359304 | tf_op jit(solution)/shard_map/ppermute | solution.py:440
  46.6 21.7 %collective-permute-start.1 = (f32[16,96,128]{2,1,0:T(8,128)S(1)}, f32[16,96,128]{2,1,0:T(8,128)S(1)}, u32[]{:S(2)}, u32[]{:S(2)}) collective-permute-start(f32[16,96,128]{2,1,0:T(8,128)S(1)} %get-tuple-element.28.up_ref), channel_id=1, source_target_pairs={{0,64},{64,128},{128,192},{192,256},{256,320},{320,384},{384,448},... | collective-permute-start | bytes 2359304 | tf_op jit(solution)/shard_map/ppermute | solution.py:439
  52.9 25.0 %all-to-all-start.1 = ((f32[64,16,128]{2,1,0:T(8,128)}), f32[64,16,128]{2,1,0:T(8,128)}, u32[]{:S(2)}, u32[]{:S(2)}) async-start(f32[64,16,128]{2,1,0:T(8,128)} %bitcast.6), calls=%async_computation.1 | async-start | bytes 1048576 | tf_op jit(solution)/shard_map/all_to_all | solution.py:249
  66.1 2.2 %copy-start.7 = (f32[64,64]{1,0:T(8,128)S(1)}, f32[64,64]{1,0:T(8,128)}, u32[]{:S(2)}) copy-start(f32[64,64]{1,0:T(8,128)} %copy-done.6) | copy-start | bytes 49156
  66.1 2.2 %copy-start.10 = (f32[64,64]{1,0:T(8,128)S(1)}, f32[64,64]{1,0:T(8,128)}, u32[]{:S(2)}) copy-start(f32[64,64]{1,0:T(8,128)} %copy-done.9) | copy-start | bytes 49156
  69.6 12.0 %collective-permute-start.3 = (f32[16,64,128]{2,1,0:T(8,128)S(1)}, f32[16,64,128]{2,1,0:T(8,128)S(1)}, u32[]{:S(2)}, u32[]{:S(2)}) collective-permute-start(f32[16,64,128]{2,1,0:T(8,128)S(1)} %get-tuple-element.38.own_ref), channel_id=1, source_target_pairs={{8,1},{2,9},{10,3},{4,11},{12,5},{6,13},{14,7},{16,15},{24,17},{18... | collective-permute-start | bytes 1572872 | tf_op jit(solution)/shard_map/ppermute | solution.py:338
  74.7 6.9 %collective-permute-start.2 = (f32[16,64,128]{2,1,0:T(8,128)S(1)}, f32[16,64,128]{2,1,0:T(8,128)S(1)}, u32[]{:S(2)}, u32[]{:S(2)}) collective-permute-start(f32[16,64,128]{2,1,0:T(8,128)S(1)} %get-tuple-element.38.own_ref), channel_id=1, source_target_pairs={{0,1},{1,0},{2,3},{3,2},{4,5},{5,4},{6,7},{7,6},{8,9},{9,8},{10,11... | collective-permute-start | bytes 1572872 | tf_op jit(solution)/shard_map/ppermute | solution.py:337
  84.5 13.2 %collective-permute-start.5 = (f32[16,64,128]{2,1,0:T(8,128)S(1)}, f32[16,64,128]{2,1,0:T(8,128)S(1)}, u32[]{:S(2)}, u32[]{:S(2)}) collective-permute-start(f32[16,64,128]{2,1,0:T(8,128)S(1)} %get-tuple-element.40.own_ref), channel_id=1, source_target_pairs={{8,1},{2,9},{10,3},{4,11},{12,5},{6,13},{14,7},{16,15},{24,17},{18... | collective-permute-start | bytes 1572872 | tf_op jit(solution)/shard_map/ppermute | solution.py:338
  88.1 9.5 %collective-permute-start.4 = (f32[16,64,128]{2,1,0:T(8,128)S(1)}, f32[16,64,128]{2,1,0:T(8,128)S(1)}, u32[]{:S(2)}, u32[]{:S(2)}) collective-permute-start(f32[16,64,128]{2,1,0:T(8,128)S(1)} %get-tuple-element.40.own_ref), channel_id=1, source_target_pairs={{0,1},{1,0},{2,3},{3,2},{4,5},{5,4},{6,7},{7,6},{8,9},{9,8},{10,11... | collective-permute-start | bytes 1572872 | tf_op jit(solution)/shard_map/ppermute | solution.py:337
  90.1 27.5 %all-to-all-start.3 = ((f32[64,16,128]{2,1,0:T(8,128)}), f32[64,16,128]{2,1,0:T(8,128)S(1)}, u32[]{:S(2)}, u32[]{:S(2)}) async-start(f32[64,16,128]{2,1,0:T(8,128)} %bitcast.10), calls=%async_computation.3 | async-start | bytes 1048576 | tf_op jit(solution)/shard_map/all_to_all | solution.py:249
  97.6 17.8 %copy-start.4 = (f32[16,64,128]{2,1,0:T(8,128)S(1)}, f32[16,64,128]{2,1,0:T(8,128)}, u32[]{:S(2)}) copy-start(f32[16,64,128]{2,1,0:T(8,128)} %get-tuple-element.42.obs_ref) | copy-start | bytes 1572868
  97.6 17.8 %copy-start.5 = (f32[16,32,128]{2,1,0:T(8,128)S(1)}, f32[16,32,128]{2,1,0:T(8,128)}, u32[]{:S(2)}) copy-start(f32[16,32,128]{2,1,0:T(8,128)} %get-tuple-element.41.halo_ref) | copy-start | bytes 786436
  99.5 15.9 %collective-permute-start.6 = (f32[16,64,128]{2,1,0:T(8,128)S(1)}, f32[16,64,128]{2,1,0:T(8,128)S(1)}, u32[]{:S(2)}, u32[]{:S(2)}) collective-permute-start(f32[16,64,128]{2,1,0:T(8,128)S(1)} %x_all.1.v_ref), channel_id=1, source_target_pairs={{64,0},{128,64},{192,128},{256,192},{320,256},{384,320},{448,384},... | collective-permute-start | bytes 1572872 | tf_op jit(solution)/shard_map/ppermute | solution.py:478
  100.8 15.6 %collective-permute-start.7 = (f32[16,64,128]{2,1,0:T(8,128)S(1)}, f32[16,64,128]{2,1,0:T(8,128)S(1)}, u32[]{:S(2)}, u32[]{:S(2)}) collective-permute-start(f32[16,64,128]{2,1,0:T(8,128)S(1)} %x_all.1.v_ref), channel_id=1, source_target_pairs={{0,64},{64,128},{128,192},{192,256},{256,320},{320,384},{384,448},... | collective-permute-start | bytes 1572872 | tf_op jit(solution)/shard_map/ppermute | solution.py:477
  115.4 1.0 copy-start.8
  115.4 1.0 copy-start.11
  115.4 1.0 copy-start.12

commit v10 on v9

--- a/solution.py
+++ b/solution.py
@@ -134,23 +134,25 @@
 def first_kernel(psf_x_hbm, est_hbm, obs_hbm, out_ref, est_ref, obs_ref, psf_x_ref, sems):
     taps = pltpu.make_async_copy(psf_x_hbm, psf_x_ref, sems.at[16])
     taps.start()
-    copies = []
-    for n, (src, dst) in enumerate(((est_hbm, est_ref), (obs_hbm, obs_ref))):
-        for t in range(8):
-            spot = pl.ds(128 * t, 128)
-            copies.append(
-                pltpu.make_async_copy(src.at[:, spot], dst.at[:, spot], sems.at[8 * n + t])
-            )
-            copies[-1].start()
+    copies = [
+        pltpu.make_async_copy(
+            src.at[pl.ds(64 * i, 64), :], dst.at[pl.ds(64 * i, 64), :], sems.at[2 * n + i]
+        )
+        for n, (src, dst) in enumerate(((est_hbm, est_ref), (obs_hbm, obs_ref)))
+        for i in range(2)
+    ]
+    for copy in copies:
+        copy.start()
     taps.wait()
     near, far = x_band(psf_x_ref, False)
-    for copy in copies[:8]:
-        copy.wait()
+    copies[0].wait()
+    copies[1].wait()
     blurred = blur_lanes([est_ref[:, 128 * t : 128 * t + 128] for t in range(8)], near, far)
     for t in range(8):
         write_columns(out_ref, t, blurred[t], 32, 0)
+    copies[2].wait()
+    copies[3].wait()
     for t in range(8):
-        copies[8 + t].wait()
         write_columns(out_ref, t, obs_ref[:, 128 * t : 128 * t + 128], 32, 16)
 
 

time: 150 us -> 149 us (level)
  no operation moved by 1% of the time
where the time goes in v10:
time: 149 us; the launch traced here: 147 us
  starting transfers between devices  50.9 us (34%)
  waiting for transfers between devices  43.9 us (29%)
  blocking collectives  28.6 us (19%)
  Pallas kernels  22 us (15%)
    all_to_all x1, blocking collectives, exchange(): t = lax.all_to_all(rows.reshape(64, per, 128), SLAB, 0, 0, tiled=True)  28.6 us
    all_to_all x3, starting transfers between devices, exchange(): t = lax.all_to_all(rows.reshape(64, per, 128), SLAB, 0, 0, tiled=True)  26.3 us
    all_to_all x3, waiting for transfers between devices, exchange(): t = lax.all_to_all(rows.reshape(64, per, 128), SLAB, 0, 0, tiled=True)  26.1 us
    pallas_call x10, Pallas kernels, call(): pl.pallas_call(kernel, out_shape=shapes, in_specs=[SMEM if a.ndim == 1 el...  15.7 us
    ppermute x1, waiting for transfers between devices, per_device(): above = lax.ppermute(v, 'z', DOWN)  9.91 us
    ppermute x2, starting transfers between devices, x_halo(): passed = lax.ppermute(v, SLAB, NEXT)  8.81 us
    ppermute x1, waiting for transfers between devices, per_device(): above = lax.ppermute(down, 'z', DOWN)  6.17 us
    ppermute x1, starting transfers between devices, per_device(): below = lax.ppermute(up, 'z', UP)  4.67 us
  transfers between devices with their start and end apart: 11, of which 4 were waited for; matrix products, arithmetic and copies ran while one was open for 0% of the time, Pallas kernels for 9%

profile of v10, /device:TPU:1, one launch (start us, length us, event | category | flops | bytes accessed | tf_op | source)
XLA Modules:
  0.0 146.9 jit_solution(17221865092532453182)
XLA Ops:
  0.0 3.0 %first.1 = f32[2048,128]{1,0:T(8,128)} custom-call(f32[31]{0:T(128)} %psf_ref.5, f32[128,1024]{1,0:T(8,128)} %bitcast.16, f32[128,1024]{1,0:T(8,128)} %bitcast.19), custom_call_target="tpu_custom_call" | custom-call | tf_op jit(solution)/shard_map/first/pallas_call | solution.py:421
  3.0 0.0 copy-start.2
  3.1 11.8 %all-to-all-start = ((f32[64,32,128]{2,1,0:T(8,128)}), f32[64,32,128]{2,1,0:T(8,128)S(1)}, u32[]{:S(2)}, u32[]{:S(2)}) async-start(f32[64,32,128]{2,1,0:T(8,128)} %bitcast.4), calls=%async_computation | async-start | bytes 2097152 | tf_op jit(solution)/shard_map/all_to_all | solution.py:251
  14.9 0.9 prepare.1
  15.8 0.6 copy-done.6
  16.4 0.6 copy-done.9
  17.0 26.1 %all-to-all-done = f32[64,32,128]{2,1,0:T(8,128)S(1)} async-done(((f32[64,32,128]{2,1,0:T(8,128)}), f32[64,32,128]{2,1,0:T(8,128)S(1)}, u32[]{:S(2)}, u32[]{:S(2)}) %all-to-all-start) | async-done | bytes 1048608 | tf_op jit(solution)/shard_map/all_to_all | solution.py:251
  43.0 1.6 %arrive.1 = (f32[16,96,128]{2,1,0:T(8,128)S(1)}, f32[16,96,128]{2,1,0:T(8,128)S(1)}) custom-call(f32[2048,128]{1,0:T(8,128)S(1)} %bitcast.15, f32[128,128]{1,0:T(8,128)S(1)} %get-tuple-element.27.y_ref), custom_call_target="tpu_custom_call" | custom-call | flops 2000000000 | bytes 6000000 | tf_op jit(solution)/shard_map/arrive/pallas_call | solution.py:45
  44.6 1.3 collective-permute-start
  45.9 4.7 %collective-permute-start.1 = (f32[16,96,128]{2,1,0:T(8,128)S(1)}, f32[16,96,128]{2,1,0:T(8,128)S(1)}, u32[]{:S(2)}, u32[]{:S(2)}) collective-permute-start(f32[16,96,128]{2,1,0:T(8,128)S(1)} %get-tuple-element.28.up_ref), channel_id=1, source_target_pairs={{0,64},{64,128},{128,192},{192,256},{256,320},{320,384},{384,448},... | collective-permute-start | bytes 2359304 | tf_op jit(solution)/shard_map/ppermute | solution.py:441
  50.6 1.7 %turn.1 = (f32[1024,128]{1,0:T(8,128)}, f32[16,64,128]{2,1,0:T(8,128)}) custom-call(f32[128,1024]{1,0:T(8,128)S(1)} %bitcast.17, f32[16,96,128]{2,1,0:T(8,128)S(1)} %get-tuple-element.29.down_ref, f32[16,96,128]{2,1,0:T(8,128)S(1)} %get-tuple-element.28.up_ref), custom_call_target="tpu_custom_call" | custom-call | flops 1000000000 | bytes 3000000 | tf_op jit(solution)/shard_map/turn/pallas_call | solution.py:45
  52.3 7.0 %all-to-all-start.1 = ((f32[64,16,128]{2,1,0:T(8,128)}), f32[64,16,128]{2,1,0:T(8,128)}, u32[]{:S(2)}, u32[]{:S(2)}) async-start(f32[64,16,128]{2,1,0:T(8,128)} %bitcast.6), calls=%async_computation.1 | async-start | bytes 1048576 | tf_op jit(solution)/shard_map/all_to_all | solution.py:251
  59.3 6.2 %collective-permute-done.above_ref = f32[16,96,128]{2,1,0:T(8,128)} collective-permute-done((f32[16,96,128]{2,1,0:T(8,128)S(1)}, f32[16,96,128]{2,1,0:T(8,128)}, u32[]{:S(2)}, u32[]{:S(2)}) %collective-permute-start) | collective-permute-done | bytes 786464 | tf_op jit(solution)/shard_map/ppermute | solution.py:442
  65.5 2.1 %first_high.1 = (f32[16,64,128]{2,1,0:T(8,128)S(1)}, f32[16,64,128]{2,1,0:T(8,128)S(1)}, f32[16,32,128]{2,1,0:T(8,128)}) custom-call(s32[1]{0:T(128)} %bitcast.slab_ref, f32[16,96,128]{2,1,0:T(8,128)S(1)} %get-tuple-element.28.up_ref, f32[16,96,128]{2,1,0:T(8,128)} %collective-permute-done.above_ref, f32[128,64]{1,0:T(8,128)S(1)} %get-tuple-element.30.zo_ref, ...), custom_call_target="tpu_custom_call" | custom-call | flops 1000000000 | bytes 3000000 | tf_op jit(solution)/shard_map/first_high/pallas_call | solution.py:45
  67.7 1.3 first_low.1
  68.9 5.2 %collective-permute-start.3 = (f32[16,64,128]{2,1,0:T(8,128)S(1)}, f32[16,64,128]{2,1,0:T(8,128)S(1)}, u32[]{:S(2)}, u32[]{:S(2)}) collective-permute-start(f32[16,64,128]{2,1,0:T(8,128)S(1)} %get-tuple-element.38.own_ref), channel_id=1, source_target_pairs={{8,1},{2,9},{10,3},{4,11},{12,5},{6,13},{14,7},{16,15},{24,17},{18... | collective-permute-start | bytes 1572872 | tf_op jit(solution)/shard_map/ppermute | solution.py:340
  74.1 1.9 %collective-permute-start.2 = (f32[16,64,128]{2,1,0:T(8,128)S(1)}, f32[16,64,128]{2,1,0:T(8,128)S(1)}, u32[]{:S(2)}, u32[]{:S(2)}) collective-permute-start(f32[16,64,128]{2,1,0:T(8,128)S(1)} %get-tuple-element.38.own_ref), channel_id=1, source_target_pairs={{0,1},{1,0},{2,3},{3,2},{4,5},{5,4},{6,7},{7,6},{8,9},{9,8},{10,11... | collective-permute-start | bytes 1572872 | tf_op jit(solution)/shard_map/ppermute | solution.py:339
  76.0 1.2 x_own.1.part_ref
  77.3 1.9 %unpack.1.est_ref = f32[16,64,128]{2,1,0:T(8,128)S(1)} custom-call(f32[1024,128]{1,0:T(8,128)} %bitcast.7.in_hbm), custom_call_target="tpu_custom_call" | custom-call | flops 1000000000 | bytes 1000000 | tf_op jit(solution)/shard_map/unpack/pallas_call | solution.py:451
  79.2 1.8 %collective-permute-done.3.passed_ref = f32[16,64,128]{2,1,0:T(8,128)S(1)} collective-permute-done((f32[16,64,128]{2,1,0:T(8,128)S(1)}, f32[16,64,128]{2,1,0:T(8,128)S(1)}, u32[]{:S(2)}, u32[]{:S(2)}) %collective-permute-start.3) | collective-permute-done | bytes 524320 | tf_op jit(solution)/shard_map/ppermute | solution.py:340
  81.0 2.9 %update.1 = (f32[1024,128]{1,0:T(8,128)}, f32[16,64,128]{2,1,0:T(8,128)S(1)}) custom-call(f32[31]{0:T(128)S(1)} %copy-done.1, s32[1]{0:T(128)} %bitcast.1.core_ref, f32[16,64,128]{2,1,0:T(8,128)S(1)} %collective-permute-done.2.swapped_ref, f32[16,64,128]{2,1,0:T(8,128)S(1)} %collective-permute-done.3.passed_ref, f32[16,64,128]{2,1,0:T(8,128)S(1)} %x_own.1.part_ref, ...), custom_call_target="tpu_custom_call" | custom-call | flops 2000000000 | bytes 6000000 | tf_op jit(solution)/shard_map/update/pallas_call | solution.py:45
  83.8 3.7 %collective-permute-start.5 = (f32[16,64,128]{2,1,0:T(8,128)S(1)}, f32[16,64,128]{2,1,0:T(8,128)S(1)}, u32[]{:S(2)}, u32[]{:S(2)}) collective-permute-start(f32[16,64,128]{2,1,0:T(8,128)S(1)} %get-tuple-element.40.own_ref), channel_id=1, source_target_pairs={{8,1},{2,9},{10,3},{4,11},{12,5},{6,13},{14,7},{16,15},{24,17},{18... | collective-permute-start | bytes 1572872 | tf_op jit(solution)/shard_map/ppermute | solution.py:340
  87.5 1.9 %collective-permute-start.4 = (f32[16,64,128]{2,1,0:T(8,128)S(1)}, f32[16,64,128]{2,1,0:T(8,128)S(1)}, u32[]{:S(2)}, u32[]{:S(2)}) collective-permute-start(f32[16,64,128]{2,1,0:T(8,128)S(1)} %get-tuple-element.40.own_ref), channel_id=1, source_target_pairs={{0,1},{1,0},{2,3},{3,2},{4,5},{5,4},{6,7},{7,6},{8,9},{9,8},{10,11... | collective-permute-start | bytes 1572872 | tf_op jit(solution)/shard_map/ppermute | solution.py:339
  89.4 7.5 %all-to-all-start.3 = ((f32[64,16,128]{2,1,0:T(8,128)}), f32[64,16,128]{2,1,0:T(8,128)S(1)}, u32[]{:S(2)}, u32[]{:S(2)}) async-start(f32[64,16,128]{2,1,0:T(8,128)} %bitcast.10), calls=%async_computation.3 | async-start | bytes 1048576 | tf_op jit(solution)/shard_map/all_to_all | solution.py:251
  97.0 1.9 %x_all.1.v_ref = f32[16,64,128]{2,1,0:T(8,128)S(1)} custom-call(f32[31]{0:T(128)S(1)} %copy-done.1, s32[1]{0:T(128)} %bitcast.1.core_ref, f32[16,64,128]{2,1,0:T(8,128)S(1)} %collective-permute-done.4.swapped_ref, f32[16,64,128]{2,1,0:T(8,128)S(1)} %collective-permute-done.5.passed_ref, f32[16,64,128]{2,1,0:T(8,128)S(1)} %get-tuple-element.40.own_ref), custom_call_target="tpu_custom_call" | custom-call | flops 99999997952 | bytes 300000000 | tf_op jit(solution)/shard_map/x_all/pallas_call | solution.py:45
  98.9 1.3 collective-permute-start.6
  100.2 4.7 %collective-permute-start.7 = (f32[16,64,128]{2,1,0:T(8,128)S(1)}, f32[16,64,128]{2,1,0:T(8,128)S(1)}, u32[]{:S(2)}, u32[]{:S(2)}) collective-permute-start(f32[16,64,128]{2,1,0:T(8,128)S(1)} %x_all.1.v_ref), channel_id=1, source_target_pairs={{0,64},{64,128},{128,192},{192,256},{256,320},{320,384},{384,448},... | collective-permute-start | bytes 1572872 | tf_op jit(solution)/shard_map/ppermute | solution.py:479
  104.8 9.9 %collective-permute-done.6.above_ref = f32[16,64,128]{2,1,0:T(8,128)S(1)} collective-permute-done((f32[16,64,128]{2,1,0:T(8,128)S(1)}, f32[16,64,128]{2,1,0:T(8,128)S(1)}, u32[]{:S(2)}, u32[]{:S(2)}) %collective-permute-start.6) | collective-permute-done | bytes 524320 | tf_op jit(solution)/shard_map/ppermute | solution.py:480
  114.8 1.0 ratio_high.1
  115.8 1.2 ratio_low.1
  117.0 28.6 %all_to_all.20 = f32[64,16,128]{2,1,0:T(8,128)S(1)} all-to-all(f32[64,16,128]{2,1,0:T(8,128)S(1)} %bitcast.18), channel_id=1, replica_groups=mesh['z'=8,'x'=4,'yl'=2,'yh'=4,'c'=2] {'x','yl','yh','c'}, dimensions={0} | all-to-all | bytes 1048576 | tf_op jit(solution)/shard_map/all_to_all | solution.py:251
  145.6 1.4 last.1
  (30 shorter events, 0.1 us)
Async XLA Ops:
  3.0 11.8 %copy-start.1 = (f32[31]{0:T(128)S(1)}, f32[31]{0:T(128)}, u32[]{:S(2)}) copy-start(f32[31]{0:T(128)} %psf_ref.5) | copy-start | bytes 376
  3.0 11.8 %copy-start.2 = (f32[31]{0:T(128)S(1)}, f32[31]{0:T(128)}, u32[]{:S(2)}) copy-start(f32[31]{0:T(128)} %psf_y_ref.1) | copy-start | bytes 376
  3.0 11.8 %copy-start.3 = (f32[63]{0:T(128)S(1)}, f32[63]{0:T(128)}, u32[]{:S(2)}) copy-start(f32[63]{0:T(128)} %psf_z_ref.1) | copy-start | bytes 760
  3.1 40.0 %all-to-all-start = ((f32[64,32,128]{2,1,0:T(8,128)}), f32[64,32,128]{2,1,0:T(8,128)S(1)}, u32[]{:S(2)}, u32[]{:S(2)}) async-start(f32[64,32,128]{2,1,0:T(8,128)} %bitcast.4), calls=%async_computation | async-start | bytes 2097152 | tf_op jit(solution)/shard_map/all_to_all | solution.py:251
  15.8 0.6 copy-start.6
  16.4 0.6 copy-start.9
  43.0 7.6 %copy-start = (f32[8,16,1024]{2,1,0:T(8,128)S(1)}, f32[8,16,1024]{2,1,0:T(8,128)}, u32[]{:S(2)}) copy-start(f32[8,16,1024]{2,1,0:T(8,128)} %param.6) | copy-start | bytes 1572868
  44.6 20.9 %collective-permute-start = (f32[16,96,128]{2,1,0:T(8,128)S(1)}, f32[16,96,128]{2,1,0:T(8,128)}, u32[]{:S(2)}, u32[]{:S(2)}) collective-permute-start(f32[16,96,128]{2,1,0:T(8,128)S(1)} %get-tuple-element.29.down_ref), channel_id=1, source_target_pairs={{64,0},{128,64},{192,128},{256,192},{320,256},{384,320},{448,384},... | collective-permute-start | bytes 2359304 | tf_op jit(solution)/shard_map/ppermute | solution.py:442
  45.9 21.7 %collective-permute-start.1 = (f32[16,96,128]{2,1,0:T(8,128)S(1)}, f32[16,96,128]{2,1,0:T(8,128)S(1)}, u32[]{:S(2)}, u32[]{:S(2)}) collective-permute-start(f32[16,96,128]{2,1,0:T(8,128)S(1)} %get-tuple-element.28.up_ref), channel_id=1, source_target_pairs={{0,64},{64,128},{128,192},{192,256},{256,320},{320,384},{384,448},... | collective-permute-start | bytes 2359304 | tf_op jit(solution)/shard_map/ppermute | solution.py:441
  52.3 25.0 %all-to-all-start.1 = ((f32[64,16,128]{2,1,0:T(8,128)}), f32[64,16,128]{2,1,0:T(8,128)}, u32[]{:S(2)}, u32[]{:S(2)}) async-start(f32[64,16,128]{2,1,0:T(8,128)} %bitcast.6), calls=%async_computation.1 | async-start | bytes 1048576 | tf_op jit(solution)/shard_map/all_to_all | solution.py:251
  65.5 2.2 %copy-start.7 = (f32[64,64]{1,0:T(8,128)S(1)}, f32[64,64]{1,0:T(8,128)}, u32[]{:S(2)}) copy-start(f32[64,64]{1,0:T(8,128)} %copy-done.6) | copy-start | bytes 49156
  65.5 2.2 %copy-start.10 = (f32[64,64]{1,0:T(8,128)S(1)}, f32[64,64]{1,0:T(8,128)}, u32[]{:S(2)}) copy-start(f32[64,64]{1,0:T(8,128)} %copy-done.9) | copy-start | bytes 49156
  68.9 12.0 %collective-permute-start.3 = (f32[16,64,128]{2,1,0:T(8,128)S(1)}, f32[16,64,128]{2,1,0:T(8,128)S(1)}, u32[]{:S(2)}, u32[]{:S(2)}) collective-permute-start(f32[16,64,128]{2,1,0:T(8,128)S(1)} %get-tuple-element.38.own_ref), channel_id=1, source_target_pairs={{8,1},{2,9},{10,3},{4,11},{12,5},{6,13},{14,7},{16,15},{24,17},{18... | collective-permute-start | bytes 1572872 | tf_op jit(solution)/shard_map/ppermute | solution.py:340
  74.1 6.9 %collective-permute-start.2 = (f32[16,64,128]{2,1,0:T(8,128)S(1)}, f32[16,64,128]{2,1,0:T(8,128)S(1)}, u32[]{:S(2)}, u32[]{:S(2)}) collective-permute-start(f32[16,64,128]{2,1,0:T(8,128)S(1)} %get-tuple-element.38.own_ref), channel_id=1, source_target_pairs={{0,1},{1,0},{2,3},{3,2},{4,5},{5,4},{6,7},{7,6},{8,9},{9,8},{10,11... | collective-permute-start | bytes 1572872 | tf_op jit(solution)/shard_map/ppermute | solution.py:339
  83.8 13.2 %collective-permute-start.5 = (f32[16,64,128]{2,1,0:T(8,128)S(1)}, f32[16,64,128]{2,1,0:T(8,128)S(1)}, u32[]{:S(2)}, u32[]{:S(2)}) collective-permute-start(f32[16,64,128]{2,1,0:T(8,128)S(1)} %get-tuple-element.40.own_ref), channel_id=1, source_target_pairs={{8,1},{2,9},{10,3},{4,11},{12,5},{6,13},{14,7},{16,15},{24,17},{18... | collective-permute-start | bytes 1572872 | tf_op jit(solution)/shard_map/ppermute | solution.py:340
  87.5 9.5 %collective-permute-start.4 = (f32[16,64,128]{2,1,0:T(8,128)S(1)}, f32[16,64,128]{2,1,0:T(8,128)S(1)}, u32[]{:S(2)}, u32[]{:S(2)}) collective-permute-start(f32[16,64,128]{2,1,0:T(8,128)S(1)} %get-tuple-element.40.own_ref), channel_id=1, source_target_pairs={{0,1},{1,0},{2,3},{3,2},{4,5},{5,4},{6,7},{7,6},{8,9},{9,8},{10,11... | collective-permute-start | bytes 1572872 | tf_op jit(solution)/shard_map/ppermute | solution.py:339
  89.4 27.6 %all-to-all-start.3 = ((f32[64,16,128]{2,1,0:T(8,128)}), f32[64,16,128]{2,1,0:T(8,128)S(1)}, u32[]{:S(2)}, u32[]{:S(2)}) async-start(f32[64,16,128]{2,1,0:T(8,128)} %bitcast.10), calls=%async_computation.3 | async-start | bytes 1048576 | tf_op jit(solution)/shard_map/all_to_all | solution.py:251
  97.0 17.8 %copy-start.4 = (f32[16,64,128]{2,1,0:T(8,128)S(1)}, f32[16,64,128]{2,1,0:T(8,128)}, u32[]{:S(2)}) copy-start(f32[16,64,128]{2,1,0:T(8,128)} %get-tuple-element.42.obs_ref) | copy-start | bytes 1572868
  97.0 17.8 %copy-start.5 = (f32[16,32,128]{2,1,0:T(8,128)S(1)}, f32[16,32,128]{2,1,0:T(8,128)}, u32[]{:S(2)}) copy-start(f32[16,32,128]{2,1,0:T(8,128)} %get-tuple-element.41.halo_ref) | copy-start | bytes 786436
  98.9 15.9 %collective-permute-start.6 = (f32[16,64,128]{2,1,0:T(8,128)S(1)}, f32[16,64,128]{2,1,0:T(8,128)S(1)}, u32[]{:S(2)}, u32[]{:S(2)}) collective-permute-start(f32[16,64,128]{2,1,0:T(8,128)S(1)} %x_all.1.v_ref), channel_id=1, source_target_pairs={{64,0},{128,64},{192,128},{256,192},{320,256},{384,320},{448,384},... | collective-permute-start | bytes 1572872 | tf_op jit(solution)/shard_map/ppermute | solution.py:480
  100.2 15.6 %collective-permute-start.7 = (f32[16,64,128]{2,1,0:T(8,128)S(1)}, f32[16,64,128]{2,1,0:T(8,128)S(1)}, u32[]{:S(2)}, u32[]{:S(2)}) collective-permute-start(f32[16,64,128]{2,1,0:T(8,128)S(1)} %x_all.1.v_ref), channel_id=1, source_target_pairs={{0,64},{64,128},{128,192},{192,256},{256,320},{320,384},{384,448},... | collective-permute-start | bytes 1572872 | tf_op jit(solution)/shard_map/ppermute | solution.py:479
  114.7 1.0 copy-start.8
  114.7 1.0 copy-start.11
  114.7 1.0 copy-start.12

commit v11 on v10

--- a/solution.py
+++ b/solution.py
@@ -201,7 +201,7 @@
     return [tiles[0]] + [pltpu.roll(tiles[8 - i], 128 - 16 * i, 1) for i in range(1, 8)]
 
 
-def unpack_one(in_ref, out_ref, rows_ref, per, offset):
+def unpack_one(in_ref, place, rows_ref, per, offset):
     for zc in range(8):
         for half in range(2):
             at = zc * 8 * per + half * 8 + offset
@@ -211,26 +211,25 @@
                 rows_ref[at + 16 * i : at + 16 * i + 8, :] = tiles[i]
     for zc in range(8):
         for x in range(16):
-            out_ref[x, zc * 8 : zc * 8 + 8, :] = rows_ref[pl.ds(zc * 128 + x, 8, stride=16), :]
+            out_ref, at = place(zc * 8)
+            out_ref[x, at : at + 8, :] = rows_ref[pl.ds(zc * 128 + x, 8, stride=16), :]
 
 
 def unpack_kernel(in_hbm, out_ref, in_ref, rows_ref, sem):
     copy = pltpu.make_async_copy(in_hbm, in_ref, sem)
     copy.start()
     copy.wait()
-    unpack_one(in_ref, out_ref, rows_ref, 16, 0)
-
-
-def arrive_kernel(in_ref, y_ref, up_ref, down_ref, rows_ref, more_ref, obs_ref):
-    unpack_one(in_ref, up_ref, rows_ref, 32, 0)
-    unpack_one(in_ref, obs_ref, more_ref, 32, 16)
+    unpack_one(in_ref, lambda z: (out_ref, z), rows_ref, 16, 0)
+
+
+def arrive_kernel(in_ref, y_ref, up_ref, down_ref, rows_ref, more_ref, v_ref):
+    unpack_one(in_ref, lambda z: (v_ref, z), rows_ref, 32, 0)
+    unpack_one(in_ref, lambda z: (up_ref, z + 32) if z >= 32 else (down_ref, z + 64), more_ref, 32, 16)
     y = split(y_ref[...])
     for x in range(16):
-        v = dot(split(up_ref[x, :64, :]), y)
+        v = dot(split(v_ref[x]), y)
         up_ref[x, :64, :] = v
         down_ref[x, :64, :] = v
-        up_ref[x, 64:, :] = obs_ref[x, 32:, :]
-        down_ref[x, 64:, :] = obs_ref[x, :32, :]
 
 
 def pack_one(in_ref, out_ref, rows_ref, per, offset):

time: 149 us -> 149 us (level)
  no operation moved by 1% of the time
where the time goes in v11:
time: 149 us; the launch traced here: 147 us
  starting transfers between devices  50.9 us (34%)
  waiting for transfers between devices  43.9 us (29%)
  blocking collectives  28.6 us (19%)
  Pallas kernels  21.9 us (15%)
    all_to_all x1, blocking collectives, exchange(): t = lax.all_to_all(rows.reshape(64, per, 128), SLAB, 0, 0, tiled=True)  28.6 us
    all_to_all x3, starting transfers between devices, exchange(): t = lax.all_to_all(rows.reshape(64, per, 128), SLAB, 0, 0, tiled=True)  26.3 us
    all_to_all x3, waiting for transfers between devices, exchange(): t = lax.all_to_all(rows.reshape(64, per, 128), SLAB, 0, 0, tiled=True)  26.1 us
    pallas_call x10, Pallas kernels, call(): pl.pallas_call(kernel, out_shape=shapes, in_specs=[SMEM if a.ndim == 1 el...  15.6 us
    ppermute x1, waiting for transfers between devices, per_device(): above = lax.ppermute(v, 'z', DOWN)  9.91 us
    ppermute x2, starting transfers between devices, x_halo(): passed = lax.ppermute(v, SLAB, NEXT)  8.82 us
    ppermute x1, waiting for transfers between devices, per_device(): above = lax.ppermute(down, 'z', DOWN)  6.16 us
    ppermute x1, starting transfers between devices, per_device(): below = lax.ppermute(up, 'z', UP)  4.67 us
  transfers between devices with their start and end apart: 11, of which 4 were waited for; matrix products, arithmetic and copies ran while one was open for 0% of the time, Pallas kernels for 9%

profile of v11, /device:TPU:1, one launch (start us, length us, event | category | flops | bytes accessed | tf_op | source)
XLA Modules:
  0.0 146.9 jit_solution(4039134943706954288)
XLA Ops:
  0.0 3.0 %first.1 = f32[2048,128]{1,0:T(8,128)} custom-call(f32[31]{0:T(128)} %psf_ref.5, f32[128,1024]{1,0:T(8,128)} %bitcast.16, f32[128,1024]{1,0:T(8,128)} %bitcast.19), custom_call_target="tpu_custom_call" | custom-call | tf_op jit(solution)/shard_map/first/pallas_call | solution.py:420
  3.0 0.0 copy-start.2
  3.1 11.8 %all-to-all-start = ((f32[64,32,128]{2,1,0:T(8,128)}), f32[64,32,128]{2,1,0:T(8,128)S(1)}, u32[]{:S(2)}, u32[]{:S(2)}) async-start(f32[64,32,128]{2,1,0:T(8,128)} %bitcast.4), calls=%async_computation | async-start | bytes 2097152 | tf_op jit(solution)/shard_map/all_to_all | solution.py:250
  14.9 0.9 prepare.1
  15.8 0.6 copy-done.6
  16.4 0.6 copy-done.9
  17.0 26.1 %all-to-all-done = f32[64,32,128]{2,1,0:T(8,128)S(1)} async-done(((f32[64,32,128]{2,1,0:T(8,128)}), f32[64,32,128]{2,1,0:T(8,128)S(1)}, u32[]{:S(2)}, u32[]{:S(2)}) %all-to-all-start) | async-done | bytes 1048608 | tf_op jit(solution)/shard_map/all_to_all | solution.py:250
  43.0 1.5 %arrive.1 = (f32[16,96,128]{2,1,0:T(8,128)S(1)}, f32[16,96,128]{2,1,0:T(8,128)S(1)}) custom-call(f32[2048,128]{1,0:T(8,128)S(1)} %bitcast.15, f32[128,128]{1,0:T(8,128)S(1)} %get-tuple-element.27.y_ref), custom_call_target="tpu_custom_call" | custom-call | flops 2000000000 | bytes 6000000 | tf_op jit(solution)/shard_map/arrive/pallas_call | solution.py:45
  44.6 1.3 collective-permute-start
  45.9 4.7 %collective-permute-start.1 = (f32[16,96,128]{2,1,0:T(8,128)S(1)}, f32[16,96,128]{2,1,0:T(8,128)S(1)}, u32[]{:S(2)}, u32[]{:S(2)}) collective-permute-start(f32[16,96,128]{2,1,0:T(8,128)S(1)} %get-tuple-element.28.up_ref), channel_id=1, source_target_pairs={{0,64},{64,128},{128,192},{192,256},{256,320},{320,384},{384,448},... | collective-permute-start | bytes 2359304 | tf_op jit(solution)/shard_map/ppermute | solution.py:440
  50.6 1.7 %turn.1 = (f32[1024,128]{1,0:T(8,128)}, f32[16,64,128]{2,1,0:T(8,128)}) custom-call(f32[128,1024]{1,0:T(8,128)S(1)} %bitcast.17, f32[16,96,128]{2,1,0:T(8,128)S(1)} %get-tuple-element.29.down_ref, f32[16,96,128]{2,1,0:T(8,128)S(1)} %get-tuple-element.28.up_ref), custom_call_target="tpu_custom_call" | custom-call | flops 1000000000 | bytes 3000000 | tf_op jit(solution)/shard_map/turn/pallas_call | solution.py:45
  52.2 7.0 %all-to-all-start.1 = ((f32[64,16,128]{2,1,0:T(8,128)}), f32[64,16,128]{2,1,0:T(8,128)}, u32[]{:S(2)}, u32[]{:S(2)}) async-start(f32[64,16,128]{2,1,0:T(8,128)} %bitcast.6), calls=%async_computation.1 | async-start | bytes 1048576 | tf_op jit(solution)/shard_map/all_to_all | solution.py:250
  59.3 6.2 %collective-permute-done.above_ref = f32[16,96,128]{2,1,0:T(8,128)} collective-permute-done((f32[16,96,128]{2,1,0:T(8,128)S(1)}, f32[16,96,128]{2,1,0:T(8,128)}, u32[]{:S(2)}, u32[]{:S(2)}) %collective-permute-start) | collective-permute-done | bytes 786464 | tf_op jit(solution)/shard_map/ppermute | solution.py:441
  65.4 2.1 %first_high.1 = (f32[16,64,128]{2,1,0:T(8,128)S(1)}, f32[16,64,128]{2,1,0:T(8,128)S(1)}, f32[16,32,128]{2,1,0:T(8,128)}) custom-call(s32[1]{0:T(128)} %bitcast.slab_ref, f32[16,96,128]{2,1,0:T(8,128)S(1)} %get-tuple-element.28.up_ref, f32[16,96,128]{2,1,0:T(8,128)} %collective-permute-done.above_ref, f32[128,64]{1,0:T(8,128)S(1)} %get-tuple-element.30.zo_ref, ...), custom_call_target="tpu_custom_call" | custom-call | flops 1000000000 | bytes 3000000 | tf_op jit(solution)/shard_map/first_high/pallas_call | solution.py:45
  67.6 1.3 first_low.1
  68.9 5.2 %collective-permute-start.3 = (f32[16,64,128]{2,1,0:T(8,128)S(1)}, f32[16,64,128]{2,1,0:T(8,128)S(1)}, u32[]{:S(2)}, u32[]{:S(2)}) collective-permute-start(f32[16,64,128]{2,1,0:T(8,128)S(1)} %get-tuple-element.38.own_ref), channel_id=1, source_target_pairs={{8,1},{2,9},{10,3},{4,11},{12,5},{6,13},{14,7},{16,15},{24,17},{18... | collective-permute-start | bytes 1572872 | tf_op jit(solution)/shard_map/ppermute | solution.py:339
  74.1 1.9 %collective-permute-start.2 = (f32[16,64,128]{2,1,0:T(8,128)S(1)}, f32[16,64,128]{2,1,0:T(8,128)S(1)}, u32[]{:S(2)}, u32[]{:S(2)}) collective-permute-start(f32[16,64,128]{2,1,0:T(8,128)S(1)} %get-tuple-element.38.own_ref), channel_id=1, source_target_pairs={{0,1},{1,0},{2,3},{3,2},{4,5},{5,4},{6,7},{7,6},{8,9},{9,8},{10,11... | collective-permute-start | bytes 1572872 | tf_op jit(solution)/shard_map/ppermute | solution.py:338
  76.0 1.2 x_own.1.part_ref
  77.2 1.9 %unpack.1.est_ref = f32[16,64,128]{2,1,0:T(8,128)S(1)} custom-call(f32[1024,128]{1,0:T(8,128)} %bitcast.7.in_hbm), custom_call_target="tpu_custom_call" | custom-call | flops 1000000000 | bytes 1000000 | tf_op jit(solution)/shard_map/unpack/pallas_call | solution.py:450
  79.1 1.8 %collective-permute-done.3.passed_ref = f32[16,64,128]{2,1,0:T(8,128)S(1)} collective-permute-done((f32[16,64,128]{2,1,0:T(8,128)S(1)}, f32[16,64,128]{2,1,0:T(8,128)S(1)}, u32[]{:S(2)}, u32[]{:S(2)}) %collective-permute-start.3) | collective-permute-done | bytes 524320 | tf_op jit(solution)/shard_map/ppermute | solution.py:339
  80.9 2.9 %update.1 = (f32[1024,128]{1,0:T(8,128)}, f32[16,64,128]{2,1,0:T(8,128)S(1)}) custom-call(f32[31]{0:T(128)S(1)} %copy-done.1, s32[1]{0:T(128)} %bitcast.1.core_ref, f32[16,64,128]{2,1,0:T(8,128)S(1)} %collective-permute-done.2.swapped_ref, f32[16,64,128]{2,1,0:T(8,128)S(1)} %collective-permute-done.3.passed_ref, f32[16,64,128]{2,1,0:T(8,128)S(1)} %x_own.1.part_ref, ...), custom_call_target="tpu_custom_call" | custom-call | flops 2000000000 | bytes 6000000 | tf_op jit(solution)/shard_map/update/pallas_call | solution.py:45
  83.8 3.7 %collective-permute-start.5 = (f32[16,64,128]{2,1,0:T(8,128)S(1)}, f32[16,64,128]{2,1,0:T(8,128)S(1)}, u32[]{:S(2)}, u32[]{:S(2)}) collective-permute-start(f32[16,64,128]{2,1,0:T(8,128)S(1)} %get-tuple-element.40.own_ref), channel_id=1, source_target_pairs={{8,1},{2,9},{10,3},{4,11},{12,5},{6,13},{14,7},{16,15},{24,17},{18... | collective-permute-start | bytes 1572872 | tf_op jit(solution)/shard_map/ppermute | solution.py:339
  87.4 1.9 %collective-permute-start.4 = (f32[16,64,128]{2,1,0:T(8,128)S(1)}, f32[16,64,128]{2,1,0:T(8,128)S(1)}, u32[]{:S(2)}, u32[]{:S(2)}) collective-permute-start(f32[16,64,128]{2,1,0:T(8,128)S(1)} %get-tuple-element.40.own_ref), channel_id=1, source_target_pairs={{0,1},{1,0},{2,3},{3,2},{4,5},{5,4},{6,7},{7,6},{8,9},{9,8},{10,11... | collective-permute-start | bytes 1572872 | tf_op jit(solution)/shard_map/ppermute | solution.py:338
  89.4 7.5 %all-to-all-start.3 = ((f32[64,16,128]{2,1,0:T(8,128)}), f32[64,16,128]{2,1,0:T(8,128)S(1)}, u32[]{:S(2)}, u32[]{:S(2)}) async-start(f32[64,16,128]{2,1,0:T(8,128)} %bitcast.10), calls=%async_computation.3 | async-start | bytes 1048576 | tf_op jit(solution)/shard_map/all_to_all | solution.py:250
  97.0 1.9 %x_all.1.v_ref = f32[16,64,128]{2,1,0:T(8,128)S(1)} custom-call(f32[31]{0:T(128)S(1)} %copy-done.1, s32[1]{0:T(128)} %bitcast.1.core_ref, f32[16,64,128]{2,1,0:T(8,128)S(1)} %collective-permute-done.4.swapped_ref, f32[16,64,128]{2,1,0:T(8,128)S(1)} %collective-permute-done.5.passed_ref, f32[16,64,128]{2,1,0:T(8,128)S(1)} %get-tuple-element.40.own_ref), custom_call_target="tpu_custom_call" | custom-call | flops 99999997952 | bytes 300000000 | tf_op jit(solution)/shard_map/x_all/pallas_call | solution.py:45
  98.8 1.3 collective-permute-start.6
  100.1 4.6 %collective-permute-start.7 = (f32[16,64,128]{2,1,0:T(8,128)S(1)}, f32[16,64,128]{2,1,0:T(8,128)S(1)}, u32[]{:S(2)}, u32[]{:S(2)}) collective-permute-start(f32[16,64,128]{2,1,0:T(8,128)S(1)} %x_all.1.v_ref), channel_id=1, source_target_pairs={{0,64},{64,128},{128,192},{192,256},{256,320},{320,384},{384,448},... | collective-permute-start | bytes 1572872 | tf_op jit(solution)/shard_map/ppermute | solution.py:478
  104.8 9.9 %collective-permute-done.6.above_ref = f32[16,64,128]{2,1,0:T(8,128)S(1)} collective-permute-done((f32[16,64,128]{2,1,0:T(8,128)S(1)}, f32[16,64,128]{2,1,0:T(8,128)S(1)}, u32[]{:S(2)}, u32[]{:S(2)}) %collective-permute-start.6) | collective-permute-done | bytes 524320 | tf_op jit(solution)/shard_map/ppermute | solution.py:479
  114.7 1.0 ratio_high.1
  115.7 1.2 ratio_low.1
  116.9 28.6 %all_to_all.20 = f32[64,16,128]{2,1,0:T(8,128)S(1)} all-to-all(f32[64,16,128]{2,1,0:T(8,128)S(1)} %bitcast.18), channel_id=1, replica_groups=mesh['z'=8,'x'=4,'yl'=2,'yh'=4,'c'=2] {'x','yl','yh','c'}, dimensions={0} | all-to-all | bytes 1048576 | tf_op jit(solution)/shard_map/all_to_all | solution.py:250
  145.5 1.4 last.1
  (30 shorter events, 0.1 us)
Async XLA Ops:
  3.0 11.8 %copy-start.1 = (f32[31]{0:T(128)S(1)}, f32[31]{0:T(128)}, u32[]{:S(2)}) copy-start(f32[31]{0:T(128)} %psf_ref.5) | copy-start | bytes 376
  3.0 11.8 %copy-start.2 = (f32[31]{0:T(128)S(1)}, f32[31]{0:T(128)}, u32[]{:S(2)}) copy-start(f32[31]{0:T(128)} %psf_y_ref.1) | copy-start | bytes 376
  3.0 11.8 %copy-start.3 = (f32[63]{0:T(128)S(1)}, f32[63]{0:T(128)}, u32[]{:S(2)}) copy-start(f32[63]{0:T(128)} %psf_z_ref.1) | copy-start | bytes 760
  3.1 40.0 %all-to-all-start = ((f32[64,32,128]{2,1,0:T(8,128)}), f32[64,32,128]{2,1,0:T(8,128)S(1)}, u32[]{:S(2)}, u32[]{:S(2)}) async-start(f32[64,32,128]{2,1,0:T(8,128)} %bitcast.4), calls=%async_computation | async-start | bytes 2097152 | tf_op jit(solution)/shard_map/all_to_all | solution.py:250
  15.8 0.6 copy-start.6
  16.4 0.6 copy-start.9
  43.0 7.5 %copy-start = (f32[8,16,1024]{2,1,0:T(8,128)S(1)}, f32[8,16,1024]{2,1,0:T(8,128)}, u32[]{:S(2)}) copy-start(f32[8,16,1024]{2,1,0:T(8,128)} %param.6) | copy-start | bytes 1572868
  44.6 20.9 %collective-permute-start = (f32[16,96,128]{2,1,0:T(8,128)S(1)}, f32[16,96,128]{2,1,0:T(8,128)}, u32[]{:S(2)}, u32[]{:S(2)}) collective-permute-start(f32[16,96,128]{2,1,0:T(8,128)S(1)} %get-tuple-element.29.down_ref), channel_id=1, source_target_pairs={{64,0},{128,64},{192,128},{256,192},{320,256},{384,320},{448,384},... | collective-permute-start | bytes 2359304 | tf_op jit(solution)/shard_map/ppermute | solution.py:441
  45.9 21.7 %collective-permute-start.1 = (f32[16,96,128]{2,1,0:T(8,128)S(1)}, f32[16,96,128]{2,1,0:T(8,128)S(1)}, u32[]{:S(2)}, u32[]{:S(2)}) collective-permute-start(f32[16,96,128]{2,1,0:T(8,128)S(1)} %get-tuple-element.28.up_ref), channel_id=1, source_target_pairs={{0,64},{64,128},{128,192},{192,256},{256,320},{320,384},{384,448},... | collective-permute-start | bytes 2359304 | tf_op jit(solution)/shard_map/ppermute | solution.py:440
  52.2 25.0 %all-to-all-start.1 = ((f32[64,16,128]{2,1,0:T(8,128)}), f32[64,16,128]{2,1,0:T(8,128)}, u32[]{:S(2)}, u32[]{:S(2)}) async-start(f32[64,16,128]{2,1,0:T(8,128)} %bitcast.6), calls=%async_computation.1 | async-start | bytes 1048576 | tf_op jit(solution)/shard_map/all_to_all | solution.py:250
  65.4 2.2 %copy-start.7 = (f32[64,64]{1,0:T(8,128)S(1)}, f32[64,64]{1,0:T(8,128)}, u32[]{:S(2)}) copy-start(f32[64,64]{1,0:T(8,128)} %copy-done.6) | copy-start | bytes 49156
  65.4 2.2 %copy-start.10 = (f32[64,64]{1,0:T(8,128)S(1)}, f32[64,64]{1,0:T(8,128)}, u32[]{:S(2)}) copy-start(f32[64,64]{1,0:T(8,128)} %copy-done.9) | copy-start | bytes 49156
  68.9 12.0 %collective-permute-start.3 = (f32[16,64,128]{2,1,0:T(8,128)S(1)}, f32[16,64,128]{2,1,0:T(8,128)S(1)}, u32[]{:S(2)}, u32[]{:S(2)}) collective-permute-start(f32[16,64,128]{2,1,0:T(8,128)S(1)} %get-tuple-element.38.own_ref), channel_id=1, source_target_pairs={{8,1},{2,9},{10,3},{4,11},{12,5},{6,13},{14,7},{16,15},{24,17},{18... | collective-permute-start | bytes 1572872 | tf_op jit(solution)/shard_map/ppermute | solution.py:339
  74.1 6.9 %collective-permute-start.2 = (f32[16,64,128]{2,1,0:T(8,128)S(1)}, f32[16,64,128]{2,1,0:T(8,128)S(1)}, u32[]{:S(2)}, u32[]{:S(2)}) collective-permute-start(f32[16,64,128]{2,1,0:T(8,128)S(1)} %get-tuple-element.38.own_ref), channel_id=1, source_target_pairs={{0,1},{1,0},{2,3},{3,2},{4,5},{5,4},{6,7},{7,6},{8,9},{9,8},{10,11... | collective-permute-start | bytes 1572872 | tf_op jit(solution)/shard_map/ppermute | solution.py:338
  83.8 13.2 %collective-permute-start.5 = (f32[16,64,128]{2,1,0:T(8,128)S(1)}, f32[16,64,128]{2,1,0:T(8,128)S(1)}, u32[]{:S(2)}, u32[]{:S(2)}) collective-permute-start(f32[16,64,128]{2,1,0:T(8,128)S(1)} %get-tuple-element.40.own_ref), channel_id=1, source_target_pairs={{8,1},{2,9},{10,3},{4,11},{12,5},{6,13},{14,7},{16,15},{24,17},{18... | collective-permute-start | bytes 1572872 | tf_op jit(solution)/shard_map/ppermute | solution.py:339
  87.4 9.5 %collective-permute-start.4 = (f32[16,64,128]{2,1,0:T(8,128)S(1)}, f32[16,64,128]{2,1,0:T(8,128)S(1)}, u32[]{:S(2)}, u32[]{:S(2)}) collective-permute-start(f32[16,64,128]{2,1,0:T(8,128)S(1)} %get-tuple-element.40.own_ref), channel_id=1, source_target_pairs={{0,1},{1,0},{2,3},{3,2},{4,5},{5,4},{6,7},{7,6},{8,9},{9,8},{10,11... | collective-permute-start | bytes 1572872 | tf_op jit(solution)/shard_map/ppermute | solution.py:338
  89.4 27.5 %all-to-all-start.3 = ((f32[64,16,128]{2,1,0:T(8,128)}), f32[64,16,128]{2,1,0:T(8,128)S(1)}, u32[]{:S(2)}, u32[]{:S(2)}) async-start(f32[64,16,128]{2,1,0:T(8,128)} %bitcast.10), calls=%async_computation.3 | async-start | bytes 1048576 | tf_op jit(solution)/shard_map/all_to_all | solution.py:250
  96.9 17.8 %copy-start.4 = (f32[16,64,128]{2,1,0:T(8,128)S(1)}, f32[16,64,128]{2,1,0:T(8,128)}, u32[]{:S(2)}) copy-start(f32[16,64,128]{2,1,0:T(8,128)} %get-tuple-element.42.obs_ref) | copy-start | bytes 1572868
  96.9 17.8 %copy-start.5 = (f32[16,32,128]{2,1,0:T(8,128)S(1)}, f32[16,32,128]{2,1,0:T(8,128)}, u32[]{:S(2)}) copy-start(f32[16,32,128]{2,1,0:T(8,128)} %get-tuple-element.41.halo_ref) | copy-start | bytes 786436
  98.8 15.9 %collective-permute-start.6 = (f32[16,64,128]{2,1,0:T(8,128)S(1)}, f32[16,64,128]{2,1,0:T(8,128)S(1)}, u32[]{:S(2)}, u32[]{:S(2)}) collective-permute-start(f32[16,64,128]{2,1,0:T(8,128)S(1)} %x_all.1.v_ref), channel_id=1, source_target_pairs={{64,0},{128,64},{192,128},{256,192},{320,256},{384,320},{448,384},... | collective-permute-start | bytes 1572872 | tf_op jit(solution)/shard_map/ppermute | solution.py:479
  100.1 15.6 %collective-permute-start.7 = (f32[16,64,128]{2,1,0:T(8,128)S(1)}, f32[16,64,128]{2,1,0:T(8,128)S(1)}, u32[]{:S(2)}, u32[]{:S(2)}) collective-permute-start(f32[16,64,128]{2,1,0:T(8,128)S(1)} %x_all.1.v_ref), channel_id=1, source_target_pairs={{0,64},{64,128},{128,192},{192,256},{256,320},{320,384},{384,448},... | collective-permute-start | bytes 1572872 | tf_op jit(solution)/shard_map/ppermute | solution.py:478
  114.7 1.0 copy-start.8
  114.7 1.0 copy-start.11
  114.7 1.0 copy-start.12
